TPU v7x, 32 devices: a whole 2x2x4 slice. The times are simulated.
32 devices in a mesh: section: 2 (over core), dp: 2 (over y), context: 2 (over x), tensor: 4 (over z).
Axes of the slice: x: 2, y: 2, z: 4, core: 2. Of those that a mesh axis runs over, the one named last changes fastest.
Arguments:
- inputs: bfloat16 [4, 2, 2048, 768], P(None, 'dp', ('context', 'tensor')), may hold values from -6 to 6
- cotangent: bfloat16 [4, 2, 2048, 768], P(None, 'dp', ('context', 'tensor')), may hold values from -6 to 6
- w_qkv: bfloat16 [2, 3, 768, 768], P('section', None, ('dp', 'context'), 'tensor'), may hold values from -0.21875 to 0.21875
- w_out: bfloat16 [2, 768, 768], P('section', 'tensor', ('dp', 'context')), may hold values from -2.5 to 2.5
- w_up: bfloat16 [2, 768, 3072], P('section', ('dp', 'context'), 'tensor'), may hold values from -0.21875 to 0.21875
- w_down: bfloat16 [2, 3072, 768], P('section', 'tensor', ('dp', 'context')), may hold values from -0.109375 to 0.109375
- norm_gains: bfloat16 [2, 2, 768], P('section', None, ('dp', 'context')), may hold values from 0.5 to 1.5
- norm_shifts: bfloat16 [2, 2, 768], P('section', None, ('dp', 'context')), may hold values from -1.796875 to 1.796875
Outputs:
- layer_outputs: bfloat16 [2, 4, 2, 2048, 768], P('section', None, 'dp', ('context', 'tensor'))
- boundary_grads: bfloat16 [2, 4, 2, 2048, 768], P('section', None, 'dp', ('context', 'tensor'))
- grad_w_qkv: float32 [2, 3, 768, 768], P('section', None, ('dp', 'context'), 'tensor')
- grad_w_out: float32 [2, 768, 768], P('section', 'tensor', ('dp', 'context'))
- grad_w_up: float32 [2, 768, 3072], P('section', ('dp', 'context'), 'tensor')
- grad_w_down: float32 [2, 3072, 768], P('section', 'tensor', ('dp', 'context'))
- grad_norm_gains: float32 [2, 2, 768], P('section', None, ('dp', 'context'))
- grad_norm_shifts: float32 [2, 2, 768], P('section', None, ('dp', 'context'))
All inputs are finite; a program needn't handle non-finite values.
Results may differ from a plain program's by a relative error of at most 0.02.
Values may be sent and summed in bfloat16 or wider, within the bound.
No kernel may reach another device: no remote copies, remote signals or barrier semaphores. Data moves between devices by JAX's collectives and lax.ppermute only.
A program may use at most 320 MiB of HBM per device.

v0:
```python
import jax
import jax.numpy as jnp
from jax import lax
from jax.sharding import PartitionSpec as P

HEAD_DIM = 64


EPS = 1e-05
NEG = -1e30


def shifted(value, axis, steps):
    count = lax.axis_size(axis)
    initial, last = (max(0, -steps), min(count, count - steps))
    return lax.ppermute(value, axis, [(source, source + steps) for source in range(initial, last)])


def normed(values, gain_row, shift_row):
    center = values - jnp.mean(values, -1, keepdims=True)
    spread = jnp.mean(center * center, -1, keepdims=True)
    return center * lax.rsqrt(spread + EPS) * gain_row + shift_row


def fetch_weights(w_qkv, w_out, w_up, w_down, norm_gains, norm_shifts):
    gathered = (
        lax.all_gather(w_qkv, ("dp", "context"), axis=2, tiled=True),
        lax.all_gather(w_out, ("dp", "context"), axis=2, tiled=True),
        lax.all_gather(w_up, ("dp", "context"), axis=1, tiled=True),
        lax.all_gather(w_down, ("dp", "context"), axis=2, tiled=True),
        lax.all_gather(norm_gains, ("dp", "context"), axis=2, tiled=True),
        lax.all_gather(norm_shifts, ("dp", "context"), axis=2, tiled=True),
    )
    return (
        gathered[0][0],
        gathered[1][0],
        gathered[2][0],
        gathered[3][0],
        gathered[4][0].astype(jnp.float32),
        gathered[5][0].astype(jnp.float32),
    )


def reduce_grads(grad_set):
    return (
        lax.psum_scatter(
            grad_set[0].astype(jnp.bfloat16), ("dp", "context"), scatter_dimension=2, tiled=True
        ).astype(jnp.float32),
        lax.psum_scatter(
            grad_set[1].astype(jnp.bfloat16), ("dp", "context"), scatter_dimension=2, tiled=True
        ).astype(jnp.float32),
        lax.psum_scatter(
            grad_set[2].astype(jnp.bfloat16), ("dp", "context"), scatter_dimension=1, tiled=True
        ).astype(jnp.float32),
        lax.psum_scatter(
            grad_set[3].astype(jnp.bfloat16), ("dp", "context"), scatter_dimension=2, tiled=True
        ).astype(jnp.float32),
        lax.psum_scatter(
            grad_set[4].astype(jnp.bfloat16), ("dp", "context"), scatter_dimension=2, tiled=True
        ).astype(jnp.float32),
        lax.psum_scatter(
            grad_set[5].astype(jnp.bfloat16), ("dp", "context"), scatter_dimension=2, tiled=True
        ).astype(jnp.float32),
    )


def collect_rows(local_rows):
    return lax.all_gather(local_rows, "tensor", axis=1, tiled=True)


def collect_grads(local_rows):
    return lax.all_gather(local_rows, "tensor", axis=1, tiled=True)


def reduce_branch(partial_sum):
    return lax.psum_scatter(
        partial_sum.astype(jnp.bfloat16), "tensor", scatter_dimension=1, tiled=True
    ).astype(jnp.float32)


def reduce_inputs(partial_sum):
    return lax.psum_scatter(
        partial_sum.astype(jnp.bfloat16), "tensor", scatter_dimension=1, tiled=True
    ).astype(jnp.float32)


def masked_scores(queries, key_rows, ctx_index):
    row_count = queries.shape[0]
    length = key_rows.shape[0]
    head_count = queries.shape[1] // HEAD_DIM
    query_heads = queries.reshape(row_count, head_count, HEAD_DIM)
    key_heads = key_rows.reshape(length, head_count, HEAD_DIM)
    scores = jnp.einsum(
        "qhe,khe->hqk", query_heads, key_heads, preferred_element_type=jnp.float32
    ) * HEAD_DIM ** (-0.5)
    places = ctx_index * row_count + jnp.arange(row_count)
    allowed = jnp.arange(length)[None, :] <= places[:, None]
    return (jnp.where(allowed[None], scores, NEG), query_heads, key_heads)


def forward(layer_in, weights, ctx_index):
    weight_qkv, weight_out, weight_up, weight_down, gain_rows, shift_rows = weights
    residual = layer_in.astype(jnp.float32)
    normed_a = collect_rows(normed(residual, gain_rows[0], shift_rows[0]).astype(jnp.bfloat16))
    projected = jnp.einsum(
        "bnd,kde->bkne", normed_a, weight_qkv, preferred_element_type=jnp.float32
    ).astype(jnp.bfloat16)
    keys_values = lax.all_gather(projected[:, 1:], "context", axis=2, tiled=True)

    def attend_one(pieces):
        queries, key_value = pieces
        scores, query_heads, key_heads = masked_scores(queries, key_value[0], ctx_index)
        row_max = jnp.max(scores, -1, keepdims=True)
        expanded = jnp.exp(scores - row_max)
        denominator = jnp.sum(expanded, -1, keepdims=True)
        attention = (expanded / denominator).astype(jnp.bfloat16)
        value_heads = key_value[1].reshape(key_heads.shape)
        mixture = jnp.einsum(
            "hqk,khe->qhe", attention, value_heads, preferred_element_type=jnp.float32
        )
        return (
            (row_max + jnp.log(denominator))[..., 0],
            mixture.reshape(queries.shape).astype(jnp.bfloat16),
        )

    log_total, mixture = lax.map(attend_one, (projected[:, 0], keys_values))
    attended = reduce_branch(jnp.dot(mixture, weight_out, preferred_element_type=jnp.float32))
    hidden = residual + attended
    normed_b = collect_rows(normed(hidden, gain_rows[1], shift_rows[1]).astype(jnp.bfloat16))
    pre_act = jnp.dot(normed_b, weight_up, preferred_element_type=jnp.float32)
    activated = jax.nn.gelu(pre_act).astype(jnp.bfloat16)
    branch = reduce_branch(jnp.dot(activated, weight_down, preferred_element_type=jnp.float32))
    saved = (
        layer_in,
        normed_a,
        projected[:, 0],
        keys_values,
        log_total,
        mixture,
        hidden,
        normed_b,
        pre_act,
    )
    return (hidden + branch, saved)


def backward(grad_in, saved, weights, ctx_index):
    weight_qkv, weight_out, weight_up, weight_down, gain_rows, shift_rows = weights
    layer_in, normed_a, queries_all, keys_values, log_total, mixture, hidden, normed_b, pre_act = (
        saved
    )
    grad_branch = collect_grads(grad_in.astype(jnp.bfloat16))
    grad_act = jnp.einsum(
        "bnd,fd->bnf", grad_branch, weight_down, preferred_element_type=jnp.float32
    )
    activated, gelu_back = jax.vjp(jax.nn.gelu, pre_act)
    grad_pre = gelu_back(grad_act)[0].astype(jnp.bfloat16)
    grad_down = jnp.einsum(
        "bnf,bnd->fd",
        activated.astype(jnp.bfloat16),
        grad_branch,
        preferred_element_type=jnp.float32,
    )
    grad_up = jnp.einsum("bnd,bnf->df", normed_b, grad_pre, preferred_element_type=jnp.float32)
    grad_second_norm = reduce_inputs(
        jnp.einsum("bnf,df->bnd", grad_pre, weight_up, preferred_element_type=jnp.float32)
    )
    unused_second, second_back = jax.vjp(normed, hidden, gain_rows[1], shift_rows[1])
    grad_hidden_norm, gain_later, shift_later = second_back(grad_second_norm)
    grad_hidden = grad_in + grad_hidden_norm
    grad_attended = collect_grads(grad_hidden.astype(jnp.bfloat16))
    grad_out = jnp.einsum("bnh,bnd->hd", mixture, grad_attended, preferred_element_type=jnp.float32)
    grad_mixture = jnp.einsum(
        "bnd,hd->bnh", grad_attended, weight_out, preferred_element_type=jnp.float32
    ).astype(jnp.bfloat16)

    def attend_back(pieces):
        queries, key_value, grad_mix, log_row = pieces
        scores, query_heads, key_heads = masked_scores(queries, key_value[0], ctx_index)
        attention = jnp.exp(scores - log_row[..., None])
        value_heads = key_value[1].reshape(key_heads.shape)
        grad_heads = grad_mix.reshape(query_heads.shape)
        grad_attention = jnp.einsum(
            "qhe,khe->hqk", grad_heads, value_heads, preferred_element_type=jnp.float32
        )
        row_inner = jnp.sum(attention * grad_attention, -1, keepdims=True)
        grad_scores = (attention * (grad_attention - row_inner)).astype(jnp.bfloat16)
        grad_query = jnp.einsum(
            "hqk,khe->qhe", grad_scores, key_heads, preferred_element_type=jnp.float32
        ) * HEAD_DIM ** (-0.5)
        grad_key = jnp.einsum(
            "hqk,qhe->khe", grad_scores, query_heads, preferred_element_type=jnp.float32
        ) * HEAD_DIM ** (-0.5)
        grad_value = jnp.einsum(
            "hqk,qhe->khe",
            attention.astype(jnp.bfloat16),
            grad_heads,
            preferred_element_type=jnp.float32,
        )
        length = key_value.shape[1]
        return (
            grad_query.reshape(queries.shape).astype(jnp.bfloat16),
            jnp.stack([grad_key.reshape(length, -1), grad_value.reshape(length, -1)]),
        )

    grad_queries, grad_pair_parts = lax.map(
        attend_back, (queries_all, keys_values, grad_mixture, log_total)
    )
    grad_pairs = lax.psum_scatter(
        grad_pair_parts.astype(jnp.bfloat16), "context", scatter_dimension=2, tiled=True
    )
    grad_proj = jnp.concatenate([grad_queries[:, None], grad_pairs], 1)
    grad_qkv = jnp.einsum("bnd,bkne->kde", normed_a, grad_proj, preferred_element_type=jnp.float32)
    grad_first_norm = reduce_inputs(
        jnp.einsum("bkne,kde->bnd", grad_proj, weight_qkv, preferred_element_type=jnp.float32)
    )
    unused_first, first_back = jax.vjp(
        normed, layer_in.astype(jnp.float32), gain_rows[0], shift_rows[0]
    )
    grad_input_norm, gain_early, shift_early = first_back(grad_first_norm)
    grad_input = grad_hidden + grad_input_norm
    grad_set = (
        grad_qkv[None],
        grad_out[None],
        grad_up[None],
        grad_down[None],
        jnp.stack([gain_early, gain_later])[None],
        jnp.stack([shift_early, shift_later])[None],
    )
    return (grad_input, grad_set)


def per_device(inputs, cotangent, w_qkv, w_out, w_up, w_down, norm_gains, norm_shifts):
    section_index = lax.axis_index("section")
    ctx_index = lax.axis_index("context")
    micro_count = inputs.shape[0]
    arriving = jnp.zeros(inputs.shape[1:], jnp.bfloat16)
    results = []
    saved_list = []
    for step_index in range(micro_count + 1):
        current = fetch_weights(w_qkv, w_out, w_up, w_down, norm_gains, norm_shifts)
        layer_in = jnp.where(section_index == 0, inputs[min(step_index, micro_count - 1)], arriving)
        layer_out, saved = forward(layer_in, current, ctx_index)
        rounded = layer_out.astype(jnp.bfloat16)
        results.append(rounded)
        saved_list.append(saved)
        if step_index < micro_count:
            arriving = shifted(rounded, "section", 1)
    layer_outputs = jnp.stack(
        [
            jnp.where(section_index == 0, results[number], results[number + 1])
            for number in range(micro_count)
        ]
    )[None]
    saved_all = jax.tree.map(lambda *pieces: jnp.stack(pieces), *saved_list)
    returning = jnp.zeros(inputs.shape[1:], jnp.bfloat16)
    sent_list = []
    summed = None
    for step_index in range(micro_count + 1):
        current = fetch_weights(w_qkv, w_out, w_up, w_down, norm_gains, norm_shifts)
        from_top = (
            cotangent[step_index]
            if step_index < micro_count
            else jnp.zeros(cotangent.shape[1:], jnp.bfloat16)
        )
        grad_in = jnp.where(section_index == 1, from_top, returning).astype(jnp.float32)
        position = jnp.clip(step_index - 1 + 2 * section_index, 0, micro_count)
        saved = jax.tree.map(
            lambda stacked: lax.dynamic_index_in_dim(stacked, position, 0, keepdims=False),
            saved_all,
        )
        grad_input, grad_set = backward(grad_in, saved, current, ctx_index)
        sent_back = grad_input.astype(jnp.bfloat16)
        sent_list.append(sent_back)
        if step_index < micro_count:
            returning = shifted(sent_back, "section", -1)
        part_sum = reduce_grads(grad_set)
        summed = part_sum if summed is None else jax.tree.map(jnp.add, summed, part_sum)
    gain_grad, shift_grad = lax.psum((summed[4], summed[5]), "tensor")
    boundary_grads = jnp.stack(
        [
            jnp.where(section_index == 0, sent_list[number + 1], sent_list[number])
            for number in range(micro_count)
        ]
    )[None]
    return (
        layer_outputs,
        boundary_grads,
        summed[0],
        summed[1],
        summed[2],
        summed[3],
        gain_grad,
        shift_grad,
    )


def solution(mesh):
    in_specs = (
        P(None, "dp", ("context", "tensor"), None),
        P(None, "dp", ("context", "tensor"), None),
        P("section", None, ("dp", "context"), "tensor"),
        P("section", "tensor", ("dp", "context")),
        P("section", ("dp", "context"), "tensor"),
        P("section", "tensor", ("dp", "context")),
        P("section", None, ("dp", "context")),
        P("section", None, ("dp", "context")),
    )
    out_specs = (
        P("section", None, "dp", ("context", "tensor"), None),
        P("section", None, "dp", ("context", "tensor"), None),
        P("section", None, ("dp", "context"), "tensor"),
        P("section", "tensor", ("dp", "context")),
        P("section", ("dp", "context"), "tensor"),
        P("section", "tensor", ("dp", "context")),
        P("section", None, ("dp", "context")),
        P("section", None, ("dp", "context")),
    )
    return jax.shard_map(
        per_device, mesh=mesh, in_specs=in_specs, out_specs=out_specs, check_vma=False
    )
```

profile of v0, /device:TPU:0, one launch (start us, length us, event | category | flops | bytes accessed | tf_op | source)
XLA Modules:
  0.0 3380.1 jit_solution(11139519057323290235)
XLA Ops:
  151.7 33.4 reduce-scatter.106.cloned.1.call-done
  190.6 35.3 %all-gather.33.cloned.1.call-done = bf16[1,1024,768]{2,1,0:T(8,128)(2,1)} async-done(((bf16[1,256,768]{2,1,0:T(8,128)(2,1)}), bf16[1,1024,768]{2,1,0:T(8,128)(2,1)}) %all-gather.33.cloned.1.call-update) | async-done | bytes 1572880 | tf_op jit(solution)/shard_map/all_gather | solution.py:68
  259.6 35.4 %reduce-scatter.108.cloned.1.call-done = bf16[1,256,768]{2,1,0:T(8,128)(2,1)} async-done(((bf16[1,1024,768]{2,1,0:T(8,128)(2,1)}), bf16[1,256,768]{2,1,0:T(8,128)(2,1)}) %reduce-scatter.108.cloned.1.call-update) | async-done | bytes 393232 | tf_op jit(solution)/shard_map/reduce_scatter | solution.py:76
  302.8 36.4 %all-gather.39.cloned.1.call-done = bf16[1,1024,768]{2,1,0:T(8,128)(2,1)} async-done(((bf16[1,256,768]{2,1,0:T(8,128)(2,1)}), bf16[1,1024,768]{2,1,0:T(8,128)(2,1)}) %all-gather.39.cloned.1.call-update) | async-done | bytes 1572880 | tf_op jit(solution)/shard_map/all_gather | solution.py:68
  408.8 35.4 %reduce-scatter.110.cloned.1.call-done = bf16[1,256,768]{2,1,0:T(8,128)(2,1)} async-done(((bf16[1,1024,768]{2,1,0:T(8,128)(2,1)}), bf16[1,256,768]{2,1,0:T(8,128)(2,1)}) %reduce-scatter.110.cloned.1.call-update) | async-done | bytes 393232 | tf_op jit(solution)/shard_map/reduce_scatter | solution.py:76
  448.6 36.1 %all-gather.43.cloned.1.call-done = bf16[1,1024,768]{2,1,0:T(8,128)(2,1)} async-done(((bf16[1,256,768]{2,1,0:T(8,128)(2,1)}), bf16[1,1024,768]{2,1,0:T(8,128)(2,1)}) %all-gather.43.cloned.1.call-update) | async-done | bytes 1572880 | tf_op jit(solution)/shard_map/all_gather | solution.py:68
  493.2 33.8 %reduce-scatter.112.cloned.1.call-done = bf16[1,256,768]{2,1,0:T(8,128)(2,1)} async-done(((bf16[1,1024,768]{2,1,0:T(8,128)(2,1)}), bf16[1,256,768]{2,1,0:T(8,128)(2,1)}) %reduce-scatter.112.cloned.1.call-update) | async-done | bytes 393232 | tf_op jit(solution)/shard_map/reduce_scatter | solution.py:76
  535.0 36.4 %all-gather.45.cloned.1.call-done = bf16[1,1024,768]{2,1,0:T(8,128)(2,1)} async-done(((bf16[1,256,768]{2,1,0:T(8,128)(2,1)}), bf16[1,1024,768]{2,1,0:T(8,128)(2,1)}) %all-gather.45.cloned.1.call-update) | async-done | bytes 1572880 | tf_op jit(solution)/shard_map/all_gather | solution.py:68
  578.2 24.3 all-gather.47.cloned.1.call-done
  640.9 35.4 %reduce-scatter.114.cloned.1.call-done = bf16[1,256,768]{2,1,0:T(8,128)(2,1)} async-done(((bf16[1,1024,768]{2,1,0:T(8,128)(2,1)}), bf16[1,256,768]{2,1,0:T(8,128)(2,1)}) %reduce-scatter.114.cloned.1.call-update) | async-done | bytes 393232 | tf_op jit(solution)/shard_map/reduce_scatter | solution.py:76
  680.8 36.1 %all-gather.49.cloned.1.call-done = bf16[1,1024,768]{2,1,0:T(8,128)(2,1)} async-done(((bf16[1,256,768]{2,1,0:T(8,128)(2,1)}), bf16[1,1024,768]{2,1,0:T(8,128)(2,1)}) %all-gather.49.cloned.1.call-update) | async-done | bytes 1572880 | tf_op jit(solution)/shard_map/all_gather | solution.py:68
  725.0 34.2 %reduce-scatter.116.cloned.1.call-done = bf16[1,256,768]{2,1,0:T(8,128)(2,1)} async-done(((bf16[1,1024,768]{2,1,0:T(8,128)(2,1)}), bf16[1,256,768]{2,1,0:T(8,128)(2,1)}) %reduce-scatter.116.cloned.1.call-update) | async-done | bytes 393232 | tf_op jit(solution)/shard_map/reduce_scatter | solution.py:76
  767.2 36.4 %all-gather.51.cloned.1.call-done = bf16[1,1024,768]{2,1,0:T(8,128)(2,1)} async-done(((bf16[1,256,768]{2,1,0:T(8,128)(2,1)}), bf16[1,1024,768]{2,1,0:T(8,128)(2,1)}) %all-gather.51.cloned.1.call-update) | async-done | bytes 1572880 | tf_op jit(solution)/shard_map/all_gather | solution.py:68
  810.6 24.1 all-gather.53.cloned.1.call-done
  873.1 35.4 %reduce-scatter.118.cloned.1.call-done = bf16[1,256,768]{2,1,0:T(8,128)(2,1)} async-done(((bf16[1,1024,768]{2,1,0:T(8,128)(2,1)}), bf16[1,256,768]{2,1,0:T(8,128)(2,1)}) %reduce-scatter.118.cloned.1.call-update) | async-done | bytes 393232 | tf_op jit(solution)/shard_map/reduce_scatter | solution.py:76
  912.9 36.1 %all-gather.55.cloned.1.call-done = bf16[1,1024,768]{2,1,0:T(8,128)(2,1)} async-done(((bf16[1,256,768]{2,1,0:T(8,128)(2,1)}), bf16[1,1024,768]{2,1,0:T(8,128)(2,1)}) %all-gather.55.cloned.1.call-update) | async-done | bytes 1572880 | tf_op jit(solution)/shard_map/all_gather | solution.py:68
  957.4 34.0 %reduce-scatter.120.cloned.1.call-done = bf16[1,256,768]{2,1,0:T(8,128)(2,1)} async-done(((bf16[1,1024,768]{2,1,0:T(8,128)(2,1)}), bf16[1,256,768]{2,1,0:T(8,128)(2,1)}) %reduce-scatter.120.cloned.1.call-update) | async-done | bytes 393232 | tf_op jit(solution)/shard_map/reduce_scatter | solution.py:76
  999.4 36.4 %all-gather.57.cloned.1.call-done = bf16[1,1024,768]{2,1,0:T(8,128)(2,1)} async-done(((bf16[1,256,768]{2,1,0:T(8,128)(2,1)}), bf16[1,1024,768]{2,1,0:T(8,128)(2,1)}) %all-gather.57.cloned.1.call-update) | async-done | bytes 1572880 | tf_op jit(solution)/shard_map/all_gather | solution.py:68
  1042.7 24.2 all-gather.59.cloned.1.call-done
  1106.1 35.4 %reduce-scatter.122.cloned.1.call-done = bf16[1,256,768]{2,1,0:T(8,128)(2,1)} async-done(((bf16[1,1024,768]{2,1,0:T(8,128)(2,1)}), bf16[1,256,768]{2,1,0:T(8,128)(2,1)}) %reduce-scatter.122.cloned.1.call-update) | async-done | bytes 393232 | tf_op jit(solution)/shard_map/reduce_scatter | solution.py:76
  1155.6 26.4 all-gather.61.cloned.1.call-done
  1187.8 32.3 all-gather.81.cloned.1.call-done
  1240.4 23.2 reduce-scatter.126.cloned.1.call-done
  1396.4 32.9 reduce-scatter.130.cloned.1.call-done
  1440.2 36.0 %all-gather.65.cloned.1.call-done = bf16[1,1024,768]{2,1,0:T(8,128)(2,1)} async-done(((bf16[1,256,768]{2,1,0:T(8,128)(2,1)}), bf16[1,1024,768]{2,1,0:T(8,128)(2,1)}) %all-gather.65.cloned.1.call-update) | async-done | bytes 1572880 | tf_op jit(solution)/shard_map/all_gather | solution.py:72
  1485.5 34.2 %reduce-scatter.132.cloned.1.call-done = bf16[1,256,768]{2,1,0:T(8,128)(2,1)} async-done(((bf16[1,1024,768]{2,1,0:T(8,128)(2,1)}), bf16[1,256,768]{2,1,0:T(8,128)(2,1)}) %reduce-scatter.132.cloned.1.call-update) | async-done | bytes 393232 | tf_op jit(solution)/shard_map/reduce_scatter | solution.py:82
  1538.9 22.7 all-gather.67.cloned.1.call-done
  1646.5 35.3 %reduce-scatter.136.cloned.1.call-done = bf16[1,256,768]{2,1,0:T(8,128)(2,1)} async-done(((bf16[1,1024,768]{2,1,0:T(8,128)(2,1)}), bf16[1,256,768]{2,1,0:T(8,128)(2,1)}) %reduce-scatter.136.cloned.1.call-update) | async-done | bytes 393232 | tf_op jit(solution)/shard_map/reduce_scatter | solution.py:82
  1695.3 36.1 %all-gather.69.cloned.1.call-done = bf16[1,1024,768]{2,1,0:T(8,128)(2,1)} async-done(((bf16[1,256,768]{2,1,0:T(8,128)(2,1)}), bf16[1,1024,768]{2,1,0:T(8,128)(2,1)}) %all-gather.69.cloned.1.call-update) | async-done | bytes 1572880 | tf_op jit(solution)/shard_map/all_gather | solution.py:72
  1740.8 34.2 %reduce-scatter.138.cloned.1.call-done = bf16[1,256,768]{2,1,0:T(8,128)(2,1)} async-done(((bf16[1,1024,768]{2,1,0:T(8,128)(2,1)}), bf16[1,256,768]{2,1,0:T(8,128)(2,1)}) %reduce-scatter.138.cloned.1.call-update) | async-done | bytes 393232 | tf_op jit(solution)/shard_map/reduce_scatter | solution.py:82
  1794.1 22.7 all-gather.71.cloned.1.call-done
  1902.1 35.3 %reduce-scatter.142.cloned.1.call-done = bf16[1,256,768]{2,1,0:T(8,128)(2,1)} async-done(((bf16[1,1024,768]{2,1,0:T(8,128)(2,1)}), bf16[1,256,768]{2,1,0:T(8,128)(2,1)}) %reduce-scatter.142.cloned.1.call-update) | async-done | bytes 393232 | tf_op jit(solution)/shard_map/reduce_scatter | solution.py:82
  1950.8 35.9 %all-gather.73.cloned.1.call-done = bf16[1,1024,768]{2,1,0:T(8,128)(2,1)} async-done(((bf16[1,256,768]{2,1,0:T(8,128)(2,1)}), bf16[1,1024,768]{2,1,0:T(8,128)(2,1)}) %all-gather.73.cloned.1.call-update) | async-done | bytes 1572880 | tf_op jit(solution)/shard_map/all_gather | solution.py:72
  1996.0 34.2 %reduce-scatter.144.cloned.1.call-done = bf16[1,256,768]{2,1,0:T(8,128)(2,1)} async-done(((bf16[1,1024,768]{2,1,0:T(8,128)(2,1)}), bf16[1,256,768]{2,1,0:T(8,128)(2,1)}) %reduce-scatter.144.cloned.1.call-update) | async-done | bytes 393232 | tf_op jit(solution)/shard_map/reduce_scatter | solution.py:82
  2157.1 35.3 %reduce-scatter.148.cloned.1.call-done = bf16[1,256,768]{2,1,0:T(8,128)(2,1)} async-done(((bf16[1,1024,768]{2,1,0:T(8,128)(2,1)}), bf16[1,256,768]{2,1,0:T(8,128)(2,1)}) %reduce-scatter.148.cloned.1.call-update) | async-done | bytes 393232 | tf_op jit(solution)/shard_map/reduce_scatter | solution.py:82
  2203.6 36.1 %all-gather.77.cloned.1.call-done = bf16[1,1024,768]{2,1,0:T(8,128)(2,1)} async-done(((bf16[1,256,768]{2,1,0:T(8,128)(2,1)}), bf16[1,1024,768]{2,1,0:T(8,128)(2,1)}) %all-gather.77.cloned.1.call-update) | async-done | bytes 1572880 | tf_op jit(solution)/shard_map/all_gather | solution.py:72
  2249.0 34.2 %reduce-scatter.150.cloned.1.call-done = bf16[1,256,768]{2,1,0:T(8,128)(2,1)} async-done(((bf16[1,1024,768]{2,1,0:T(8,128)(2,1)}), bf16[1,256,768]{2,1,0:T(8,128)(2,1)}) %reduce-scatter.150.cloned.1.call-update) | async-done | bytes 393232 | tf_op jit(solution)/shard_map/reduce_scatter | solution.py:82
  2300.7 24.2 all-gather.79.cloned.1.call-done
  2562.1 26.0 reduce-scatter.206.cloned.1.call-done
  2589.1 30.8 reduce-scatter.188.cloned.1.call-done
  2621.6 25.5 reduce-scatter.178.cloned.1.call-done
  2648.9 28.6 reduce-scatter.168.cloned.1.call-done
  2679.6 24.9 reduce-scatter.198.cloned.1.call-done
  2706.0 25.3 reduce-scatter.208.cloned.1.call-done
  2732.8 30.3 reduce-scatter.190.cloned.1.call-done
  2764.9 25.6 reduce-scatter.180.cloned.1.call-done
  2792.3 28.7 reduce-scatter.170.cloned.1.call-done
  2823.1 24.7 reduce-scatter.200.cloned.1.call-done
  2849.4 25.5 reduce-scatter.210.cloned.1.call-done
  2876.4 30.1 reduce-scatter.192.cloned.1.call-done
  2908.2 25.5 reduce-scatter.182.cloned.1.call-done
  2935.5 28.6 reduce-scatter.172.cloned.1.call-done
  2966.2 25.3 reduce-scatter.202.cloned.1.call-done
  2993.0 25.3 reduce-scatter.212.cloned.1.call-done
  3019.9 30.2 reduce-scatter.194.cloned.1.call-done
  3053.2 28.4 reduce-scatter.156.cloned.1.call-done
  3081.7 31.7 reduce-scatter.158.cloned.1.call-done
  3113.4 31.6 reduce-scatter.160.cloned.1.call-done
  3145.0 31.8 reduce-scatter.162.cloned.1.call-done
  3176.7 31.7 reduce-scatter.164.cloned.1.call-done
  3210.9 25.0 reduce-scatter.184.cloned.1.call-done
  3237.8 28.6 reduce-scatter.174.cloned.1.call-done
  3271.0 33.6 reduce-scatter.154.cloned.1.call-done
  3333.1 26.1 reduce-scatter.214.cloned.1.call-done
  (1031 shorter events, 1385.2 us)
Async XLA Ops:
  84.1 101.0 %reduce-scatter.106.cloned.1.call-start = ((), (), s32[]{:S(2)}) async-start(), calls=%async_computation.57 | async-start | bytes 1966080 | tf_op jit(solution)/shard_map/reduce_scatter | solution.py:76
  190.6 104.4 %reduce-scatter.108.cloned.1.call-start = ((), (), s32[]{:S(2)}) async-start(), calls=%async_computation.61 | async-start | bytes 1966080 | tf_op jit(solution)/shard_map/reduce_scatter | solution.py:76
  259.6 79.7 %all-gather.39.cloned.1.call-start = ((), (), s32[]{:S(2)}) async-start(), calls=%async_computation.62 | async-start | bytes 1966080 | tf_op jit(solution)/shard_map/all_gather | solution.py:68
  344.2 100.0 %reduce-scatter.110.cloned.1.call-start = ((), (), s32[]{:S(2)}) async-start(), calls=%async_computation.64 | async-start | bytes 1966080 | tf_op jit(solution)/shard_map/reduce_scatter | solution.py:76
  448.6 78.4 %reduce-scatter.112.cloned.1.call-start = ((), (), s32[]{:S(2)}) async-start(), calls=%async_computation.66 | async-start | bytes 1966080 | tf_op jit(solution)/shard_map/reduce_scatter | solution.py:76
  492.7 78.7 %all-gather.45.cloned.1.call-start = ((), (), s32[]{:S(2)}) async-start(), calls=%async_computation.67 | async-start | bytes 1966080 | tf_op jit(solution)/shard_map/all_gather | solution.py:68
  576.3 100.0 %reduce-scatter.114.cloned.1.call-start = ((), (), s32[]{:S(2)}) async-start(), calls=%async_computation.69 | async-start | bytes 1966080 | tf_op jit(solution)/shard_map/reduce_scatter | solution.py:76
  640.9 76.0 %all-gather.49.cloned.1.call-start = ((), (), s32[]{:S(2)}) async-start(), calls=%async_computation.70 | async-start | bytes 1966080 | tf_op jit(solution)/shard_map/all_gather | solution.py:68
  680.7 78.5 %reduce-scatter.116.cloned.1.call-start = ((), (), s32[]{:S(2)}) async-start(), calls=%async_computation.71 | async-start | bytes 1966080 | tf_op jit(solution)/shard_map/reduce_scatter | solution.py:76
  724.9 78.7 %all-gather.51.cloned.1.call-start = ((), (), s32[]{:S(2)}) async-start(), calls=%async_computation.72 | async-start | bytes 1966080 | tf_op jit(solution)/shard_map/all_gather | solution.py:68
  808.5 99.9 %reduce-scatter.118.cloned.1.call-start = ((), (), s32[]{:S(2)}) async-start(), calls=%async_computation.74 | async-start | bytes 1966080 | tf_op jit(solution)/shard_map/reduce_scatter | solution.py:76
  912.9 78.5 %reduce-scatter.120.cloned.1.call-start = ((), (), s32[]{:S(2)}) async-start(), calls=%async_computation.76 | async-start | bytes 1966080 | tf_op jit(solution)/shard_map/reduce_scatter | solution.py:76
  957.1 78.7 %all-gather.57.cloned.1.call-start = ((), (), s32[]{:S(2)}) async-start(), calls=%async_computation.77 | async-start | bytes 1966080 | tf_op jit(solution)/shard_map/all_gather | solution.py:68
  1040.7 100.8 %reduce-scatter.122.cloned.1.call-start = ((), (), s32[]{:S(2)}) async-start(), calls=%async_computation.79 | async-start | bytes 1966080 | tf_op jit(solution)/shard_map/reduce_scatter | solution.py:76
  1147.7 115.9 %reduce-scatter.126.cloned.1.call-start = ((), (), s32[]{:S(2)}) async-start(), calls=%async_computation.82 | async-start | bytes 1966080 | tf_op jit(solution)/shard_map/reduce_scatter | solution.py:82
  1229.3 78.1 %all-gather.63.cloned.1.call-start = ((), (), s32[]{:S(2)}) async-start(), calls=%async_computation.83 | async-start | bytes 1966080 | tf_op jit(solution)/shard_map/all_gather | solution.py:72
  1271.6 118.3 %reduce-scatter.128.cloned.1.call-start = ((), (), s32[]{:S(2)}) async-start(), calls=%async_computation.84 | async-start | bytes 2359296 | tf_op jit(solution)/shard_map/reduce_scatter | solution.py:209
  1393.9 82.4 %all-gather.65.cloned.1.call-start = ((), (), s32[]{:S(2)}) async-start(), calls=%async_computation.86 | async-start | bytes 1966080 | tf_op jit(solution)/shard_map/all_gather | solution.py:72
  1440.2 79.6 %reduce-scatter.132.cloned.1.call-start = ((), (), s32[]{:S(2)}) async-start(), calls=%async_computation.87 | async-start | bytes 1966080 | tf_op jit(solution)/shard_map/reduce_scatter | solution.py:82
  1485.5 76.1 %all-gather.67.cloned.1.call-start = ((), (), s32[]{:S(2)}) async-start(), calls=%async_computation.88 | async-start | bytes 1966080 | tf_op jit(solution)/shard_map/all_gather | solution.py:72
  1525.4 117.0 %reduce-scatter.134.cloned.1.call-start = ((), (), s32[]{:S(2)}) async-start(), calls=%async_computation.89 | async-start | bytes 2359296 | tf_op jit(solution)/shard_map/reduce_scatter | solution.py:209
  1646.5 84.9 %all-gather.69.cloned.1.call-start = ((), (), s32[]{:S(2)}) async-start(), calls=%async_computation.91 | async-start | bytes 1966080 | tf_op jit(solution)/shard_map/all_gather | solution.py:72
  1695.2 79.7 %reduce-scatter.138.cloned.1.call-start = ((), (), s32[]{:S(2)}) async-start(), calls=%async_computation.92 | async-start | bytes 1966080 | tf_op jit(solution)/shard_map/reduce_scatter | solution.py:82
  1740.7 76.1 %all-gather.71.cloned.1.call-start = ((), (), s32[]{:S(2)}) async-start(), calls=%async_computation.93 | async-start | bytes 1966080 | tf_op jit(solution)/shard_map/all_gather | solution.py:72
  1780.6 117.3 %reduce-scatter.140.cloned.1.call-start = ((), (), s32[]{:S(2)}) async-start(), calls=%async_computation.94 | async-start | bytes 2359296 | tf_op jit(solution)/shard_map/reduce_scatter | solution.py:209
  1902.0 84.7 %all-gather.73.cloned.1.call-start = ((), (), s32[]{:S(2)}) async-start(), calls=%async_computation.96 | async-start | bytes 1966080 | tf_op jit(solution)/shard_map/all_gather | solution.py:72
  1950.8 79.5 %reduce-scatter.144.cloned.1.call-start = ((), (), s32[]{:S(2)}) async-start(), calls=%async_computation.97 | async-start | bytes 1966080 | tf_op jit(solution)/shard_map/reduce_scatter | solution.py:82
  1996.0 76.1 %all-gather.75.cloned.1.call-start = ((), (), s32[]{:S(2)}) async-start(), calls=%async_computation.98 | async-start | bytes 1966080 | tf_op jit(solution)/shard_map/all_gather | solution.py:72
  2036.0 116.9 %reduce-scatter.146.cloned.1.call-start = ((), (), s32[]{:S(2)}) async-start(), calls=%async_computation.99 | async-start | bytes 2359296 | tf_op jit(solution)/shard_map/reduce_scatter | solution.py:209
  2157.0 82.7 %all-gather.77.cloned.1.call-start = ((), (), s32[]{:S(2)}) async-start(), calls=%async_computation.101 | async-start | bytes 1966080 | tf_op jit(solution)/shard_map/all_gather | solution.py:72
  2203.6 79.7 %reduce-scatter.150.cloned.1.call-start = ((), (), s32[]{:S(2)}) async-start(), calls=%async_computation.102 | async-start | bytes 1966080 | tf_op jit(solution)/shard_map/reduce_scatter | solution.py:82
  2249.0 76.0 %all-gather.79.cloned.1.call-start = ((), (), s32[]{:S(2)}) async-start(), calls=%async_computation.103 | async-start | bytes 1966080 | tf_op jit(solution)/shard_map/all_gather | solution.py:72
  2288.9 242.5 %reduce-scatter.152.cloned.1.call-start = ((), (), s32[]{:S(2)}) async-start(), calls=%async_computation.104 | async-start | bytes 2359296 | tf_op jit(solution)/shard_map/reduce_scatter | solution.py:209
  2382.3 156.0 %reduce-scatter.186.cloned.1.call-start = ((), (), s32[]{:S(2)}) async-start(), calls=%async_computation.122 | async-start | bytes 1474560
  2394.3 145.8 %reduce-scatter.124.cloned.1.call-start = ((), (), s32[]{:S(2)}) async-start(), calls=%async_computation.81 | async-start | bytes 1966080 | tf_op jit(solution)/shard_map/reduce_scatter | solution.py:76
  2398.9 148.4 %reduce-scatter.176.cloned.1.call-start = ((), (), s32[]{:S(2)}) async-start(), calls=%async_computation.117 | async-start | bytes 491520
  2408.7 139.7 %reduce-scatter.166.cloned.1.call-start = ((), (), s32[]{:S(2)}) async-start(), calls=%async_computation.112 | async-start | bytes 1228800
  2417.9 143.2 %reduce-scatter.196.cloned.1.call-start = ((), (), s32[]{:S(2)}) async-start(), calls=%async_computation.127 | async-start | bytes 245760
  2419.4 168.7 %reduce-scatter.206.cloned.1.call-start = ((), (), s32[]{:S(2)}) async-start(), calls=%async_computation.132 | async-start | bytes 245760
  2420.6 199.2 %reduce-scatter.188.cloned.1.call-start = ((), (), s32[]{:S(2)}) async-start(), calls=%async_computation.123 | async-start | bytes 1474560
  2428.7 218.5 %reduce-scatter.178.cloned.1.call-start = ((), (), s32[]{:S(2)}) async-start(), calls=%async_computation.118 | async-start | bytes 491520
  2432.2 245.2 %reduce-scatter.168.cloned.1.call-start = ((), (), s32[]{:S(2)}) async-start(), calls=%async_computation.113 | async-start | bytes 1228800
  2438.8 265.7 %reduce-scatter.198.cloned.1.call-start = ((), (), s32[]{:S(2)}) async-start(), calls=%async_computation.128 | async-start | bytes 245760
  2440.2 291.1 %reduce-scatter.208.cloned.1.call-start = ((), (), s32[]{:S(2)}) async-start(), calls=%async_computation.133 | async-start | bytes 245760
  2441.5 321.6 %reduce-scatter.190.cloned.1.call-start = ((), (), s32[]{:S(2)}) async-start(), calls=%async_computation.124 | async-start | bytes 1474560
  2449.4 341.2 %reduce-scatter.180.cloned.1.call-start = ((), (), s32[]{:S(2)}) async-start(), calls=%async_computation.119 | async-start | bytes 491520
  2453.0 368.1 %reduce-scatter.170.cloned.1.call-start = ((), (), s32[]{:S(2)}) async-start(), calls=%async_computation.114 | async-start | bytes 1228800
  2459.1 388.7 %reduce-scatter.200.cloned.1.call-start = ((), (), s32[]{:S(2)}) async-start(), calls=%async_computation.129 | async-start | bytes 245760
  2460.5 414.3 %reduce-scatter.210.cloned.1.call-start = ((), (), s32[]{:S(2)}) async-start(), calls=%async_computation.134 | async-start | bytes 245760
  2461.7 444.7 %reduce-scatter.192.cloned.1.call-start = ((), (), s32[]{:S(2)}) async-start(), calls=%async_computation.125 | async-start | bytes 1474560
  2469.7 464.1 %reduce-scatter.182.cloned.1.call-start = ((), (), s32[]{:S(2)}) async-start(), calls=%async_computation.120 | async-start | bytes 491520
  2473.3 490.8 %reduce-scatter.172.cloned.1.call-start = ((), (), s32[]{:S(2)}) async-start(), calls=%async_computation.115 | async-start | bytes 1228800
  2479.4 512.1 %reduce-scatter.202.cloned.1.call-start = ((), (), s32[]{:S(2)}) async-start(), calls=%async_computation.130 | async-start | bytes 245760
  2480.8 537.5 %reduce-scatter.212.cloned.1.call-start = ((), (), s32[]{:S(2)}) async-start(), calls=%async_computation.135 | async-start | bytes 245760
  2482.2 567.9 %reduce-scatter.194.cloned.1.call-start = ((), (), s32[]{:S(2)}) async-start(), calls=%async_computation.126 | async-start | bytes 1474560
  2494.1 587.6 %reduce-scatter.156.cloned.1.call-start = ((), (), s32[]{:S(2)}) async-start(), calls=%async_computation.106 | async-start | bytes 1474560 | tf_op jit(solution)/shard_map/reduce_scatter | solution.py:52
  2502.8 610.6 %reduce-scatter.158.cloned.1.call-start = ((), (), s32[]{:S(2)}) async-start(), calls=%async_computation.107 | async-start | bytes 1474560 | tf_op jit(solution)/shard_map/reduce_scatter | solution.py:52
  2506.9 638.1 %reduce-scatter.160.cloned.1.call-start = ((), (), s32[]{:S(2)}) async-start(), calls=%async_computation.108 | async-start | bytes 1474560 | tf_op jit(solution)/shard_map/reduce_scatter | solution.py:52
  2511.0 665.8 %reduce-scatter.162.cloned.1.call-start = ((), (), s32[]{:S(2)}) async-start(), calls=%async_computation.109 | async-start | bytes 1474560 | tf_op jit(solution)/shard_map/reduce_scatter | solution.py:52
  2515.0 693.5 %reduce-scatter.164.cloned.1.call-start = ((), (), s32[]{:S(2)}) async-start(), calls=%async_computation.110 | async-start | bytes 1474560 | tf_op jit(solution)/shard_map/reduce_scatter | solution.py:52
  2519.5 716.4 %reduce-scatter.184.cloned.1.call-start = ((), (), s32[]{:S(2)}) async-start(), calls=%async_computation.121 | async-start | bytes 491520
  2522.6 743.8 %reduce-scatter.174.cloned.1.call-start = ((), (), s32[]{:S(2)}) async-start(), calls=%async_computation.116 | async-start | bytes 1228800
  2538.2 766.3 %reduce-scatter.154.cloned.1.call-start = ((), (), s32[]{:S(2)}) async-start(), calls=%async_computation.105 | async-start | bytes 1966080 | tf_op jit(solution)/shard_map/reduce_scatter | solution.py:82
  2545.6 786.6 %reduce-scatter.204.cloned.1.call-start = ((), (), s32[]{:S(2)}) async-start(), calls=%async_computation.131 | async-start | bytes 245760
  (214 other events, 7426.7 us)
Sparse Core Ops, SparseCore 0:
  42.0 37.3 all-gather.28
  84.2 28.4 all-gather.30
  151.2 33.8 reduce-scatter.105
  302.9 36.2 all-gather.38
  344.3 26.0 all-gather.40
  448.7 35.9 all-gather.42
  535.1 36.2 all-gather.44
  576.5 26.0 all-gather.46
  680.8 35.9 all-gather.48
  767.3 36.2 all-gather.50
  808.6 26.0 all-gather.52
  913.0 35.9 all-gather.54
  999.5 36.2 all-gather.56
  1040.8 26.0 all-gather.58
  1146.0 35.9 all-gather.60
  1184.0 35.9 all-gather.80
  1364.9 24.8 reduce-scatter.127
  1440.3 35.9 all-gather.64
  1525.5 35.9 all-gather.66
  1617.4 24.9 reduce-scatter.133
  1695.3 35.9 all-gather.68
  1780.8 35.9 all-gather.70
  1872.9 24.9 reduce-scatter.139
  1996.1 34.1 reduce-scatter.143
  2127.9 24.9 reduce-scatter.145
  2203.7 35.9 all-gather.76
  2289.0 35.9 all-gather.78
  2382.4 24.9 reduce-scatter.151
  2410.6 28.5 reduce-scatter.185
  2442.0 35.2 reduce-scatter.123
  2480.3 23.3 reduce-scatter.175
  2507.0 27.2 reduce-scatter.165
  2537.1 23.9 reduce-scatter.195
  2564.1 23.9 reduce-scatter.205
  2591.3 28.5 reduce-scatter.187
  2622.7 24.3 reduce-scatter.177
  2650.2 27.2 reduce-scatter.167
  2680.5 23.9 reduce-scatter.197
  2707.3 23.9 reduce-scatter.207
  2734.5 28.5 reduce-scatter.189
  2766.1 24.3 reduce-scatter.179
  2793.8 27.2 reduce-scatter.169
  2823.8 23.9 reduce-scatter.199
  2850.8 23.9 reduce-scatter.209
  2877.9 28.5 reduce-scatter.191
  2909.3 24.3 reduce-scatter.181
  2936.8 27.2 reduce-scatter.171
  2967.5 23.9 reduce-scatter.201
  2994.3 23.9 reduce-scatter.211
  3021.5 28.5 reduce-scatter.193
  3053.1 28.5 reduce-scatter.155
  3084.8 28.5 reduce-scatter.157
  3116.4 28.5 reduce-scatter.159
  3148.2 28.5 reduce-scatter.161
  3179.9 28.5 reduce-scatter.163
  3211.5 24.3 reduce-scatter.183
  3239.2 27.2 reduce-scatter.173
  3269.3 35.2 reduce-scatter.153
Sparse Core Ops, SparseCore 1:
  153.4 26.1 all-gather.34
  190.1 35.9 all-gather.32
  227.7 26.4 all-gather.36
  259.7 35.3 reduce-scatter.107
  408.8 35.3 reduce-scatter.109
  492.8 34.1 reduce-scatter.111
  641.0 35.3 reduce-scatter.113
  725.0 34.1 reduce-scatter.115
  873.1 35.3 reduce-scatter.117
  957.2 34.1 reduce-scatter.119
  1106.1 35.3 reduce-scatter.121
  1229.4 34.1 reduce-scatter.125
  1271.6 35.8 all-gather.62
  1394.0 35.3 reduce-scatter.129
  1485.6 34.1 reduce-scatter.131
  1646.6 35.3 reduce-scatter.135
  1740.8 34.1 reduce-scatter.137
  1902.1 35.3 reduce-scatter.141
  1950.8 35.8 all-gather.72
  2036.1 35.9 all-gather.74
  2157.1 35.3 reduce-scatter.147
  2249.1 34.1 reduce-scatter.149
  3309.1 23.0 reduce-scatter.203
  3335.1 24.0 reduce-scatter.213
where the time goes:
time: 3390 us; the launch traced here: 3380 us
  waiting for transfers between devices  2180 us (64%)
  matrix products  593 us (17%)
  other arithmetic  287 us (8%)
  local copies, waits for them, and re-layouts  205 us (6%)
  blocking collectives  64.2 us (2%)
    unnamed x107, waiting for transfers between devices  573 us
    all_gather x10, waiting for transfers between devices, collect_rows(): return lax.all_gather(local_rows, 'tensor', axis=1, tiled=True)  336 us
    reduce_scatter x10, waiting for transfers between devices, reduce_inputs(): lax.psum_scatter(partial_sum.astype(jnp.bfloat16), 'tensor', scatter_dime...  332 us
    reduce_scatter x10, waiting for transfers between devices, reduce_branch(): lax.psum_scatter(partial_sum.astype(jnp.bfloat16), 'tensor', scatter_dime...  312 us
    all_gather x10, waiting for transfers between devices, collect_grads(): return lax.all_gather(local_rows, 'tensor', axis=1, tiled=True)  282 us
    unnamed x502, local copies, waits for them, and re-layouts  168 us
    reduce_scatter x5, waiting for transfers between devices, reduce_grads(): lax.psum_scatter(grad_set[2].astype(jnp.bfloat16), ('dp', 'context'), sca...  155 us
    dot_general x10, matrix products, masked_scores(): jnp.einsum('qhe,khe->hqk', query_heads, key_heads, preferred_element_type...  117 us
  transfers between devices with their start and end apart: 90, of which 83 were waited for; matrix products, arithmetic and copies ran while one was open for 11% of the time, Pallas kernels for 0%

commit v1 on v0

v1 whole, which is shorter than its diff:
```python
import functools

import jax
import jax.numpy as jnp
from jax import lax
from jax.experimental import pallas as pl
from jax.experimental.pallas import tpu as pltpu
from jax.sharding import PartitionSpec as P

HEAD_DIM = 64
EPS = 1e-05
NEG = -1e30
BLOCK = 512
SCALE = HEAD_DIM ** (-0.5)
F32 = jnp.float32
BF16 = jnp.bfloat16
VMEM_LIMIT = 48 * 1024 * 1024


def normed(values, gain_row, shift_row):
    center = values - jnp.mean(values, -1, keepdims=True)
    spread = jnp.mean(center * center, -1, keepdims=True)
    return center * lax.rsqrt(spread + EPS) * gain_row + shift_row


def dot(left, right, contract):
    return lax.dot_general(left, right, ((contract[0], contract[1]), ((), ())),
                           preferred_element_type=F32)


def attend_kernel(block, heads, rows_ref, all_ref, mix_ref, log_ref):
    place = pl.program_id(0)
    width = heads * HEAD_DIM
    row_ids = lax.broadcasted_iota(jnp.int32, (block, block), 0)
    col_ids = lax.broadcasted_iota(jnp.int32, (block, block), 1)
    for head in range(heads):
        low = head * HEAD_DIM
        queries = rows_ref[:, low:low + HEAD_DIM] * jnp.asarray(SCALE, BF16)

        def step(index, carry, masked):
            top, total, mixed = carry
            span = pl.ds(pl.multiple_of(index * block, block), block)
            keys = all_ref[span, width + low:width + low + HEAD_DIM]
            values = all_ref[span, 2 * width + low:2 * width + low + HEAD_DIM]
            scores = dot(queries, keys, ((1,), (1,)))
            if masked:
                scores = jnp.where(col_ids <= row_ids, scores, NEG)
            new_top = jnp.maximum(top, jnp.max(scores, -1, keepdims=True))
            grown = jnp.exp(scores - new_top)
            shrink = jnp.exp(top - new_top)
            return (
                new_top,
                total * shrink + jnp.sum(grown, -1, keepdims=True),
                mixed * shrink + dot(grown.astype(BF16), values, ((1,), (0,))),
            )

        carry = (
            jnp.full((block, 1), NEG, F32),
            jnp.zeros((block, 1), F32),
            jnp.zeros((block, HEAD_DIM), F32),
        )
        carry = lax.fori_loop(0, place, lambda i, c: step(i, c, False), carry)
        top, total, mixed = step(place, carry, True)
        mix_ref[:, low:low + HEAD_DIM] = (mixed / total).astype(BF16)
        wide = jnp.broadcast_to(top + jnp.log(total), (block, 128))
        log_ref[head] = wide.T[:1]


def attend(packed, heads):
    length, width = packed.shape
    block = min(BLOCK, length)
    return pl.pallas_call(
        functools.partial(attend_kernel, block, heads),
        grid=(length // block,),
        in_specs=[
            pl.BlockSpec((block, width), lambda i: (i, 0)),
            pl.BlockSpec((length, width), lambda i: (0, 0)),
        ],
        out_specs=[
            pl.BlockSpec((block, width // 3), lambda i: (i, 0)),
            pl.BlockSpec((heads, 1, block), lambda i: (0, 0, i)),
        ],
        out_shape=[
            jax.ShapeDtypeStruct((length, width // 3), BF16),
            jax.ShapeDtypeStruct((heads, 1, length), F32),
        ],
        compiler_params=pltpu.CompilerParams(vmem_limit_bytes=VMEM_LIMIT),
        cost_estimate=pl.CostEstimate(
            flops=2 * 2 * length * length * HEAD_DIM * heads,
            bytes_accessed=length * width * 4,
            transcendentals=length * length * heads // 2,
        ),
        name="attend",
    )(packed, packed)


def attend_back_kernel(block, heads, rows_ref, all_ref, grad_ref, mix_ref, log_ref, out_ref,
                       query_sum, inner):
    place = pl.program_id(0)
    count = pl.num_programs(0)
    width = heads * HEAD_DIM
    key_ids = lax.broadcasted_iota(jnp.int32, (block, block), 0)
    query_ids = lax.broadcasted_iota(jnp.int32, (block, block), 1)

    @pl.when(place == 0)
    def prepare():
        query_sum[...] = jnp.zeros_like(query_sum)

        def one(index, carry):
            span = pl.ds(pl.multiple_of(index * block, block), block)
            product = grad_ref[span, :].astype(F32) * mix_ref[span, :].astype(F32)
            for head in range(heads):
                part = product[:, head * HEAD_DIM:(head + 1) * HEAD_DIM]
                inner[head, :, span] = jnp.sum(part.T, 0, keepdims=True)
            return carry

        lax.fori_loop(0, count, one, 0)

    for head in range(heads):
        low = head * HEAD_DIM
        keys = rows_ref[:, width + low:width + low + HEAD_DIM] * jnp.asarray(SCALE, BF16)
        values = rows_ref[:, 2 * width + low:2 * width + low + HEAD_DIM]

        def step(index, carry, masked):
            key_sum, value_sum = carry
            span = pl.ds(pl.multiple_of(index * block, block), block)
            queries = all_ref[span, low:low + HEAD_DIM]
            grads = grad_ref[span, low:low + HEAD_DIM]
            scores = dot(keys, queries, ((1,), (1,)))
            if masked:
                scores = jnp.where(key_ids <= query_ids, scores, NEG)
            probs = jnp.exp(scores - log_ref[head, :, span])
            grad_probs = dot(values, grads, ((1,), (1,)))
            grad_scores = (probs * (grad_probs - inner[head, :, span])).astype(BF16)
            value_sum = value_sum + dot(probs.astype(BF16), grads, ((1,), (0,)))
            key_sum = key_sum + dot(grad_scores, queries, ((1,), (0,)))
            query_sum[head, span, :] += dot(grad_scores, keys, ((0,), (0,)))
            return key_sum, value_sum

        carry = (jnp.zeros((block, HEAD_DIM), F32), jnp.zeros((block, HEAD_DIM), F32))
        carry = step(place, carry, True)
        key_sum, value_sum = lax.fori_loop(
            place + 1, count, lambda i, c: step(i, c, False), carry)
        own = pl.ds(pl.multiple_of(place * block, block), block)
        out_ref[:, low:low + HEAD_DIM] = query_sum[head, own, :].astype(BF16)
        out_ref[:, width + low:width + low + HEAD_DIM] = (key_sum * SCALE).astype(BF16)
        out_ref[:, 2 * width + low:2 * width + low + HEAD_DIM] = value_sum.astype(BF16)


def attend_back(packed, grads, mixture, logs, heads):
    length, width = packed.shape
    block = min(BLOCK, length)
    third = width // 3
    return pl.pallas_call(
        functools.partial(attend_back_kernel, block, heads),
        grid=(length // block,),
        in_specs=[
            pl.BlockSpec((block, width), lambda i: (i, 0)),
            pl.BlockSpec((length, width), lambda i: (0, 0)),
            pl.BlockSpec((length, third), lambda i: (0, 0)),
            pl.BlockSpec((length, third), lambda i: (0, 0)),
            pl.BlockSpec((heads, 1, length), lambda i: (0, 0, 0)),
        ],
        out_specs=pl.BlockSpec((block, width), lambda i: (i, 0)),
        out_shape=jax.ShapeDtypeStruct((length, width), BF16),
        scratch_shapes=[
            pltpu.VMEM((heads, length, HEAD_DIM), F32),
            pltpu.VMEM((heads, 1, length), F32),
        ],
        compiler_params=pltpu.CompilerParams(vmem_limit_bytes=VMEM_LIMIT),
        cost_estimate=pl.CostEstimate(
            flops=2 * 5 * length * length * HEAD_DIM * heads,
            bytes_accessed=length * width * 8,
            transcendentals=length * length * heads // 2,
        ),
        name="attend_back",
    )(packed, packed, grads, mixture, logs)


def swap(value, axis):
    return lax.ppermute(value, axis, [(0, 1), (1, 0)])


def put(buffer, value, places):
    starts = [0 if place is None else place for place in places]
    starts += [0] * (buffer.ndim - len(starts))
    shape = [buffer.shape[n] if n >= len(places) or places[n] is None else 1
             for n in range(buffer.ndim)]
    return lax.dynamic_update_slice(buffer, value.reshape(shape), starts)


def take(buffer, index, axis=0):
    return lax.dynamic_index_in_dim(buffer, index, axis, keepdims=False)


def line_gather(value, axis):
    count = lax.axis_size(axis)
    place = lax.axis_index(axis)
    up = [(n, n + 1) for n in range(count - 1)]
    down = [(n + 1, n) for n in range(count - 1)]
    from_low, from_high = [value], [value]
    for step in range(1, count):
        from_low.append(lax.ppermute(from_low[-1], axis, up))
        from_high.append(lax.ppermute(from_high[-1], axis, down))
    gathered = jnp.zeros((count,) + value.shape, value.dtype)
    gathered = put(gathered, value, (place,))
    for step in range(1, count):
        piece = from_high[step] + from_low[count - step]
        gathered = put(gathered, piece, (lax.rem(place + step, count),))
    return gathered


def line_reduce(blocks, axis):
    count = lax.axis_size(axis)
    place = lax.axis_index(axis)
    up = [(n, n + 1) for n in range(count - 1)]
    down = [(n + 1, n) for n in range(count - 1)]
    rising = falling = None
    for step in range(1, count):
        ahead = take(blocks, jnp.minimum(place + count - step, count - 1))
        behind = take(blocks, jnp.maximum(place - count + step, 0))
        if rising is not None:
            ahead = (ahead.astype(F32) + rising.astype(F32)).astype(BF16)
            behind = (behind.astype(F32) + falling.astype(F32)).astype(BF16)
        rising = lax.ppermute(ahead, axis, up)
        falling = lax.ppermute(behind, axis, down)
    return take(blocks, place).astype(F32) + rising.astype(F32) + falling.astype(F32)


def spread_tensor(blocks):
    count = lax.axis_size("tensor")
    place = lax.axis_index("tensor")
    result = put(jnp.zeros_like(blocks), take(blocks, place), (place,))
    for step in range(1, count):
        pairs = [(n, (n + step) % count) for n in range(count)]
        piece = lax.ppermute(take(blocks, lax.rem(place + step, count)), "tensor", pairs)
        result = put(result, piece, (lax.rem(place + count - step, count),))
    return result


def group_pairs(count, step):
    return [(n, n ^ step) for n in range(count)]


GROUP = ("section", "context")


def to_heads(blocks):
    count = blocks.shape[0]
    sections = lax.axis_size("section")
    contexts = count // sections
    place = lax.axis_index("section") * contexts + lax.axis_index("context")
    result = jnp.zeros((contexts, blocks.shape[1], sections) + blocks.shape[2:],
                       blocks.dtype)
    for step in range(count):
        other = lax.bitwise_xor(place, step)
        piece = take(blocks, other)
        if step:
            piece = lax.ppermute(piece, GROUP, group_pairs(count, step))
        result = put(result, piece, (lax.rem(other, contexts), None, other // contexts))
    return result


def from_heads(spread):
    contexts, _, sections = spread.shape[:3]
    count = contexts * sections
    place = lax.axis_index("section") * contexts + lax.axis_index("context")
    result = jnp.zeros((count,) + spread.shape[1:2] + spread.shape[3:], spread.dtype)
    for step in range(count):
        other = lax.bitwise_xor(place, step)
        piece = take(take(spread, lax.rem(other, contexts)), other // contexts, 1)
        if step:
            piece = lax.ppermute(piece, GROUP, group_pairs(count, step))
        result = put(result, piece, (other,))
    return result


def gather_rows(half):
    section = lax.axis_index("section")
    sections = lax.axis_size("section")
    dp_count, ctx_count = lax.axis_size("dp"), lax.axis_size("context")
    rows, width = half.shape
    if dp_count == 2 and ctx_count == 2 and rows % 2 == 0:
        dp, ctx = lax.axis_index("dp"), lax.axis_index("context")
        first, second = half[:rows // 2], half[rows // 2:]
        pair_shape = (2,) + first.shape
        near = put(jnp.zeros(pair_shape, half.dtype), first, (ctx,))
        near = put(near, swap(first, "context"), (1 - ctx,))
        other = put(jnp.zeros(pair_shape, half.dtype), second, (dp,))
        other = put(other, swap(second, "dp"), (1 - dp,))
        near_far, other_far = swap(near, "dp"), swap(other, "context")
        whole = jnp.zeros((2, 2, sections, 2, rows // 2, width), half.dtype)
        for value, places in (
            (near, (dp, None, None, 0)),
            (other, (None, ctx, None, 1)),
            (near_far, (1 - dp, None, None, 0)),
            (other_far, (None, 1 - ctx, None, 1)),
        ):
            for held, where in ((value, section), (swap(value, "section"), 1 - section)):
                whole = put(whole, held, (places[0], places[1], where, places[3]))
    else:
        gathered = lax.all_gather(half, ("dp", "context"))
        whole = jnp.zeros((dp_count * ctx_count, sections, rows, width), half.dtype)
        whole = put(whole, gathered, (None, section))
        whole = put(whole, swap(gathered, "section"), (None, 1 - section))
    return whole.reshape(-1, width)


def add_bf16(left, right):
    return (left.astype(F32) + right.astype(F32)).astype(BF16)


def reduce_rows(partial):
    section = lax.axis_index("section")
    sections = lax.axis_size("section")
    dp_count, ctx_count = lax.axis_size("dp"), lax.axis_size("context")
    width = partial.shape[1]
    rows = partial.shape[0] // (dp_count * ctx_count * sections)
    if dp_count == 2 and ctx_count == 2 and rows % 2 == 0:
        dp, ctx = lax.axis_index("dp"), lax.axis_index("context")
        split = partial.reshape(2, 2, sections, rows, width)
        mine = add_bf16(take(split, section, 2), swap(take(split, 1 - section, 2), "section"))
        first, second = mine[:, :, :rows // 2], mine[:, :, rows // 2:]
        first = add_bf16(take(first, dp), swap(take(first, 1 - dp), "dp"))
        second = add_bf16(take(second, ctx, 1), swap(take(second, 1 - ctx, 1), "context"))
        first = add_bf16(take(first, ctx), swap(take(first, 1 - ctx), "context"))
        second = add_bf16(take(second, dp), swap(take(second, 1 - dp), "dp"))
        return jnp.concatenate([first, second])
    split = partial.reshape(-1, sections, rows, width)
    mine = add_bf16(take(split, section, 1), swap(take(split, 1 - section, 1), "section"))
    return lax.psum_scatter(mine, ("dp", "context"), scatter_dimension=0)


def per_device(inputs, cotangent, w_qkv, w_out, w_up, w_down, norm_gains, norm_shifts):
    section = lax.axis_index("section")
    tensors = lax.axis_size("tensor")
    sections = lax.axis_size("section")
    contexts = lax.axis_size("context")
    groups = contexts * sections
    micro, _, span, width = inputs.shape
    assert micro == tensors and sections == 2
    rows = span // sections
    count = tensors * rows
    head_total = width // HEAD_DIM
    heads = -(-head_total // groups)

    slabs = [
        w_qkv[0].transpose(1, 0, 2).reshape(w_qkv.shape[2], -1),
        w_out[0].T,
        w_up[0],
        w_down[0].T,
    ]
    norms = jnp.concatenate([norm_gains[0], norm_shifts[0]]).T
    widths = [slab.shape[1] for slab in slabs]
    slab = jnp.concatenate(slabs + [norms], 1)
    split = slab.reshape(sections, -1, slab.shape[1])
    kept = take(split, section)
    came = swap(take(split, 1 - section), "section")
    half_rows = kept.shape[0]

    def gather_layer(layer):
        half = jnp.where(section == layer, kept, came)
        starts = [sum(widths[:n]) for n in range(5)]
        parts = [half[:, starts[n]:starts[n + 1]] for n in range(4)]
        norm_part = half[:, starts[4]:]
        result = []
        for members in ((0,), (1, 2), (3,)):
            joined = parts[members[0]] if len(members) == 1 else jnp.concatenate(
                [parts[n] for n in members], 1)
            lined = line_gather(joined, "tensor")
            columns, place = [], 0
            for n in members:
                piece = lined[:, :, place:place + widths[n]]
                columns.append(piece.transpose(1, 0, 2).reshape(half_rows, -1))
                place += widths[n]
            if members == (0,):
                columns.append(norm_part)
            sizes = [column.shape[1] for column in columns]
            full = gather_rows(jnp.concatenate(columns, 1) if len(columns) > 1 else columns[0])
            place = 0
            for size in sizes:
                result.append(full[:, place:place + size])
                place += size
        qkv, norm_rows, out, up, down = result
        norm_rows = norm_rows.T.astype(F32)
        return qkv, out, up, down, norm_rows[:2], norm_rows[2:]

    def to_groups(projected):
        if groups == tensors:
            blocks = projected.reshape(tensors, rows, groups, -1)
        else:
            shaped = projected.reshape(count, tensors, 3, -1, HEAD_DIM)
            shaped = shaped.transpose(0, 2, 1, 3, 4).reshape(count, 3, head_total, HEAD_DIM)
            shaped = jnp.pad(shaped, ((0, 0), (0, 0), (0, groups * heads - head_total), (0, 0)))
            shaped = shaped.reshape(count, 3, groups, -1).transpose(0, 2, 1, 3)
            blocks = shaped.reshape(tensors, rows, groups, -1)
        return blocks.transpose(2, 0, 1, 3)

    def from_groups(blocks):
        shaped = blocks.transpose(1, 2, 0, 3)
        if groups == tensors:
            return shaped.reshape(count, -1)
        shaped = shaped.reshape(count, groups, 3, heads * HEAD_DIM).transpose(0, 2, 1, 3)
        shaped = shaped.reshape(count, 3, -1)[:, :, :width]
        return shaped.reshape(count, 3, tensors, -1).transpose(0, 2, 1, 3).reshape(count, -1)

    def mix_to_groups(mixed):
        pad = groups * heads * HEAD_DIM - width
        if pad:
            mixed = jnp.pad(mixed, ((0, 0), (0, pad)))
        return mixed.reshape(tensors, rows, groups, -1).transpose(2, 0, 1, 3)

    def mix_from_groups(blocks):
        return blocks.transpose(1, 2, 0, 3).reshape(count, -1)[:, :width]

    def spread_heads(blocks):
        spread = to_heads(blocks)
        return spread.reshape(-1, spread.shape[-1])

    def collect_heads(flat):
        return from_heads(flat.reshape(contexts, tensors, sections, rows, -1))

    def forward(layer_in, weights):
        qkv, out, up, down, gains, shifts = weights
        residual = layer_in.astype(F32)
        normed_a = normed(residual, gains[0], shifts[0]).astype(BF16)
        projected = dot(normed_a, qkv, ((1,), (0,))).astype(BF16)
        packed = spread_heads(to_groups(projected))
        mixed, logs = attend(packed, heads)
        mixture = mix_from_groups(collect_heads(mixed))
        hidden = residual + dot(mixture, out, ((1,), (1,)))
        normed_b = normed(hidden, gains[1], shifts[1]).astype(BF16)
        pre_act = dot(normed_b, up, ((1,), (0,)))
        activated = jax.nn.gelu(pre_act).astype(BF16)
        layer_out = hidden + dot(activated, down, ((1,), (1,)))
        saved = (residual, normed_a, packed, mixed, logs, mixture, hidden, normed_b, pre_act)
        return layer_out.astype(BF16), saved

    def backward(grad_in, saved, weights):
        qkv, out, up, down, gains, shifts = weights
        residual, normed_a, packed, mixed, logs, mixture, hidden, normed_b, pre_act = saved
        grad_branch = grad_in.astype(BF16)
        grad_in = grad_in.astype(F32)
        grad_act = dot(grad_branch, down, ((1,), (0,)))
        activated, gelu_back = jax.vjp(jax.nn.gelu, pre_act)
        grad_pre = gelu_back(grad_act)[0].astype(BF16)
        grad_down = dot(grad_branch, activated.astype(BF16), ((0,), (0,))).astype(BF16)
        grad_up = dot(normed_b, grad_pre, ((0,), (0,))).astype(BF16)
        grad_second = dot(grad_pre, up, ((1,), (1,)))
        _, second_back = jax.vjp(normed, hidden, gains[1], shifts[1])
        grad_hidden_norm, gain_later, shift_later = second_back(grad_second)
        grad_hidden = grad_in + grad_hidden_norm
        grad_attn = grad_hidden.astype(BF16)
        grad_out = dot(grad_attn, mixture, ((0,), (0,))).astype(BF16)
        grad_mixture = dot(grad_attn, out, ((1,), (0,))).astype(BF16)
        grad_mixed = spread_heads(mix_to_groups(grad_mixture))
        grad_packed = attend_back(packed, grad_mixed, mixed, logs, heads)
        grad_proj = from_groups(collect_heads(grad_packed))
        grad_qkv = dot(normed_a, grad_proj, ((0,), (0,))).astype(BF16)
        grad_first = dot(grad_proj, qkv, ((1,), (1,)))
        _, first_back = jax.vjp(normed, residual, gains[0], shifts[0])
        grad_input_norm, gain_early, shift_early = first_back(grad_first)
        grad_input = (grad_hidden + grad_input_norm).astype(BF16)
        grad_norms = jnp.stack([gain_early, gain_later, shift_early, shift_later], 1)
        return grad_input, (grad_qkv, grad_out, grad_up, grad_down, grad_norms)

    def reduce_layer(grads):
        grad_qkv, grad_out, grad_up, grad_down, grad_norms = grads
        result = []
        for members in ((grad_down,), (grad_out, grad_up), (grad_qkv, grad_norms)):
            joined = jnp.concatenate([part.astype(BF16) for part in members], 1)
            joined = reduce_rows(joined)
            blocks, place = [], 0
            for part in members:
                size = part.shape[1]
                piece = joined[:, place:place + size]
                place += size
                if part is grad_norms:
                    blocks.append(jnp.broadcast_to(piece, (tensors,) + piece.shape))
                else:
                    blocks.append(piece.reshape(half_rows, tensors, -1).transpose(1, 0, 2))
            total = line_reduce(jnp.concatenate(blocks, 2), "tensor")
            place = 0
            for block in blocks:
                result.append(total[:, place:place + block.shape[2]])
                place += block.shape[2]
        down, out, up, qkv, norms = result
        return jnp.concatenate([qkv, out, up, down, norms], 1).astype(BF16)

    def own_rows(value):
        half = take(value.reshape(micro, sections, rows, width), section, 1)
        return spread_tensor(half).reshape(count, width)

    def back_rows(value):
        return spread_tensor(value.reshape(tensors, rows, width))

    def place_layers(lower, upper):
        keep = jnp.where(section == 0, lower, upper)
        came_rows = swap(jnp.where(section == 0, upper, lower), "section")
        whole = jnp.zeros((micro, sections, rows, width), BF16)
        whole = put(whole, keep, (None, section))
        whole = put(whole, came_rows, (None, 1 - section))
        return whole.reshape(1, micro, 1, span, width)

    entries = own_rows(inputs)
    weights_zero = gather_layer(0)
    weights_one = gather_layer(1)
    top_grad = own_rows(cotangent)
    out_zero, saved_zero = forward(entries, weights_zero)
    out_one, saved_one = forward(out_zero, weights_one)
    layer_outputs = place_layers(back_rows(out_zero), back_rows(out_one))
    grad_one, grads_one = backward(top_grad, saved_one, weights_one)
    reduced_one = reduce_layer(grads_one)
    grad_zero, grads_zero = backward(grad_one, saved_zero, weights_zero)
    boundary_grads = place_layers(back_rows(grad_zero), back_rows(grad_one))
    reduced_zero = reduce_layer(grads_zero)

    keep = jnp.where(section == 0, reduced_zero, reduced_one)
    came_half = swap(jnp.where(section == 0, reduced_one, reduced_zero), "section")
    total = jnp.zeros((sections,) + keep.shape, BF16)
    total = put(total, keep, (section,))
    total = put(total, came_half, (1 - section,))
    total = total.reshape(-1, keep.shape[1]).astype(F32)
    starts = [sum(widths[:n]) for n in range(5)]
    grad_qkv, grad_out, grad_up, grad_down = (
        total[:, starts[n]:starts[n + 1]] for n in range(4))
    norms = total[:, starts[4]:].T
    return (
        layer_outputs,
        boundary_grads,
        grad_qkv.reshape(grad_qkv.shape[0], 3, -1).transpose(1, 0, 2)[None],
        grad_out.T[None],
        grad_up[None],
        grad_down.T[None],
        norms[:2][None],
        norms[2:][None],
    )


def solution(mesh):
    in_specs = (
        P(None, "dp", ("context", "tensor"), None),
        P(None, "dp", ("context", "tensor"), None),
        P("section", None, ("dp", "context"), "tensor"),
        P("section", "tensor", ("dp", "context")),
        P("section", ("dp", "context"), "tensor"),
        P("section", "tensor", ("dp", "context")),
        P("section", None, ("dp", "context")),
        P("section", None, ("dp", "context")),
    )
    out_specs = (
        P("section", None, "dp", ("context", "tensor"), None),
        P("section", None, "dp", ("context", "tensor"), None),
        P("section", None, ("dp", "context"), "tensor"),
        P("section", "tensor", ("dp", "context")),
        P("section", ("dp", "context"), "tensor"),
        P("section", "tensor", ("dp", "context")),
        P("section", None, ("dp", "context")),
        P("section", None, ("dp", "context")),
    )
    return jax.shard_map(
        per_device, mesh=mesh, in_specs=in_specs, out_specs=out_specs, check_vma=False
    )
```

time: 3390 us -> 1340 us (0.40)
  waiting for transfers between devices: 2180 us -> 231 us
  matrix products: 593 us -> 98.2 us
  starting transfers between devices: 26.6 us -> 327 us
  local copies, waits for them, and re-layouts: 205 us -> 447 us
  other arithmetic: 287 us -> 92.7 us
  Pallas kernels: 0 us -> 114 us
  blocking collectives: 64.2 us -> 0 us
    reduce_scatter x30 -> x0, waiting for transfers between devices: 861 us -> none  [the longest x10 332 us: reduce_inputs(): lax.psum_scatter(partial_sum.astype(jnp.bfloat16), 'tensor', scatter_dime...]
    all_gather x27 -> x0, waiting for transfers between devices: 737 us -> none  [the longest x10 336 us: collect_rows(): return lax.all_gather(local_rows, 'tensor', axis=1, tiled=True)]
    unnamed x107 -> x0, waiting for transfers between devices: 573 us -> none
    dot_general x90 -> x24, matrix products: 579 us -> 98.2 us  [dot(): lax.dot_general(left, right, ((contract[0], contract[1]), ((), ())), pref...]
    ppermute x8 -> x196, starting transfers between devices: 10.4 us -> 327 us  [the longest x18 83.9 us: line_gather(): from_low.append(lax.ppermute(from_low[-1], axis, up))]
    ppermute x8 -> x196, waiting for transfers between devices: 13.2 us -> 231 us  [the longest x82 105 us: swap(): return lax.ppermute(value, axis, [(0, 1), (1, 0)])]
    dynamic_update_slice x0 -> x143, local copies, waits for them, and re-layouts: none -> 195 us  [put(): return lax.dynamic_update_slice(buffer, value.reshape(shape), starts)]
    unnamed x502 -> x308, local copies, waits for them, and re-layouts: 168 us -> 33.3 us
  transfers between devices with their start and end apart: 90 -> 196, of which waited for: 83 -> 62; matrix products, arithmetic and copies ran while one was open for 11% -> 43% of each run, Pallas kernels for 0% -> 7%
where the time goes in v1:
time: 1340 us; the launch traced here: 1320 us
  local copies, waits for them, and re-layouts  447 us (33%)
  starting transfers between devices  327 us (24%)
  waiting for transfers between devices  231 us (17%)
  Pallas kernels  114 us (9%)
  matrix products  98.2 us (7%)
  other arithmetic  92.7 us (7%)
    dynamic_update_slice x143, local copies, waits for them, and re-layouts, put(): return lax.dynamic_update_slice(buffer, value.reshape(shape), starts)  195 us
    ppermute x82, waiting for transfers between devices, swap(): return lax.ppermute(value, axis, [(0, 1), (1, 0)])  105 us
    dot_general x24, matrix products, dot(): lax.dot_general(left, right, ((contract[0], contract[1]), ((), ())), pref...  98.2 us
    ppermute x18, starting transfers between devices, line_gather(): from_low.append(lax.ppermute(from_low[-1], axis, up))  83.9 us
    ppermute x18, starting transfers between devices, line_reduce(): rising = lax.ppermute(ahead, axis, up)  77 us
    pallas_call x2, Pallas kernels, attend_back(): pl.pallas_call(functools.partial(attend_back_kernel, block, heads), grid=...  66.6 us
    another operation x58, local copies, waits for them, and re-layouts  64.3 us
    ppermute x82, starting transfers between devices, swap(): return lax.ppermute(value, axis, [(0, 1), (1, 0)])  57.9 us
  transfers between devices with their start and end apart: 196, of which 62 were waited for; matrix products, arithmetic and copies ran while one was open for 43% of the time, Pallas kernels for 7%

profile of v1, /device:TPU:0, one launch (start us, length us, event | category | flops | bytes accessed | tf_op | source)
XLA Modules:
  0.0 1315.4 jit_solution(2408403952974038747)
XLA Ops:
  18.6 9.3 collective-permute-start.108
  28.9 10.5 collective-permute-start.109
  47.2 7.2 collective-permute-start.39
  80.4 6.0 dynamic_update_slice.562
  87.4 6.2 dynamic_update_slice.578
  96.2 5.8 collective-permute-start.6
  108.9 5.2 collective-permute-start.25
  135.4 5.9 collective-permute-start.76
  153.3 5.3 collective-permute-start.77
  165.7 5.6 dynamic_update_slice.481
  172.8 5.8 collective-permute-start.41
  191.5 5.4 collective-permute-start.92
  210.0 5.8 dynamic_update_slice.519
  220.0 5.9 dynamic_update_slice.521
  232.3 5.2 collective-permute-start.27
  238.7 6.2 dynamic_update_slice.579
  244.9 6.2 dynamic_update_slice.580
  251.1 6.2 dynamic_update_slice.581
  278.9 6.0 dynamic_update_slice.503
  284.9 6.0 dynamic_update_slice.504
  304.6 6.0 dynamic_update_slice.563
  310.6 6.0 dynamic_update_slice.564
  371.2 9.1 collective-permute-done.65
  395.3 12.4 collective-permute-done.99
  417.4 5.6 reshape.1446
  423.0 6.8 constant_dynamic-slice_fusion.51
  467.5 13.0 collective-permute-done.85
  492.2 12.8 collective-permute-done.18
  510.3 6.4 collective-permute-done.20
  521.5 23.8 %attend.2 = (bf16[2048,192]{1,0:T(8,128)(2,1)S(1)}, f32[3,1,2048]{2,1,0:T(1,128)S(1)}) custom-call(bf16[2048,576]{1,0:T(8,128)(2,1)S(1)} %bitcast.1043, bf16[2048,576]{1,0:T(8,128)(2,1)S(1)} %bitcast.1044), custom_call_target="tpu_custom_call" | custom-call | flops 3221225472 | bytes 4718592 | tf_op jit(solution)/shard_map/attend/pallas_call | solution.py:72
  548.0 5.9 collective-permute-done.21
  555.7 6.6 collective-permute-done.23
  574.5 8.6 convert_reduce_fusion
  592.4 5.8 reshape.1447
  598.2 6.8 constant_dynamic-slice_fusion.43
  634.5 6.5 collective-permute-done.71
  645.8 23.8 %attend.3 = (bf16[2048,192]{1,0:T(8,128)(2,1)S(1)}, f32[3,1,2048]{2,1,0:T(1,128)S(1)}) custom-call(bf16[2048,576]{1,0:T(8,128)(2,1)S(1)} %bitcast.1047, bf16[2048,576]{1,0:T(8,128)(2,1)S(1)} %bitcast.1048), custom_call_target="tpu_custom_call" | custom-call | flops 3221225472 | bytes 4718592 | tf_op jit(solution)/shard_map/attend/pallas_call | solution.py:72
  674.0 4.8 collective-permute-done.72
  689.3 6.3 add_convert_fusion.2
  695.6 7.7 fusion.13
  703.3 5.3 multiply_reduce_fusion
  708.6 4.8 convolution_convert_fusion.1
  733.3 5.3 pad_maximum_fusion.1
  744.1 33.6 %attend_back.2 = bf16[2048,576]{1,0:T(8,128)(2,1)S(1)} custom-call(bf16[2048,576]{1,0:T(8,128)(2,1)} %bitcast.1049, bf16[2048,576]{1,0:T(8,128)(2,1)} %bitcast.1050, bf16[2048,192]{1,0:T(8,128)(2,1)S(1)} %bitcast.1056, bf16[2048,192]{1,0:T(8,128)(2,1)S(1)} %copy-done.5, f32[3,1,2048]{2,1,0:T(1,128)S(1)} %get-tuple-element.14.log_ref), custom_call_target="tpu_custom_call" | custom-call | flops 8053063680 | bytes 9437184 | tf_op jit(solution)/shard_map/attend_back/pallas_call | solution.py:154
  796.3 10.8 collective-permute-done.115
  816.3 8.4 fusion.6
  827.7 4.8 convolution_convert_fusion.4
  849.7 5.3 pad_maximum_fusion
  855.0 9.1 constant_dynamic-slice_fusion.7
  864.1 7.2 constant_dynamic-slice_fusion.5
  882.6 6.6 concatenate.150
  896.9 33.0 %attend_back.3 = bf16[2048,576]{1,0:T(8,128)(2,1)S(1)} custom-call(bf16[2048,576]{1,0:T(8,128)(2,1)} %bitcast.1045, bf16[2048,576]{1,0:T(8,128)(2,1)} %bitcast.1046, bf16[2048,192]{1,0:T(8,128)(2,1)S(1)} %bitcast.1055, bf16[2048,192]{1,0:T(8,128)(2,1)S(1)} %copy-done.3, f32[3,1,2048]{2,1,0:T(1,128)S(1)} %get-tuple-element.15.log_ref), custom_call_target="tpu_custom_call" | custom-call | flops 8053063680 | bytes 9437184 | tf_op jit(solution)/shard_map/attend_back/pallas_call | solution.py:154
  943.3 9.8 collective-permute-done.119
  956.8 7.3 collective-permute-done.121
  977.3 6.6 concatenate.138
  985.7 10.8 collective-permute-done.123
  1036.4 5.2 collective-permute-done.187
  1068.4 24.4 %collective-permute-done.133 = bf16[48,2308]{1,0:T(8,128)(2,1)S(1)} collective-permute-done((bf16[48,2308]{1,0:T(8,128)(2,1)S(1)}, bf16[48,2308]{1,0:T(8,128)(2,1)S(1)}, u32[]{:S(2)}, u32[]{:S(2)}) %collective-permute-start.133) | collective-permute-done | bytes 221600 | tf_op jit(solution)/shard_map/ppermute | solution.py:181
  1093.9 6.3 collective-permute-done.131
  1101.9 4.9 collective-permute-done.166
  1142.4 5.2 collective-permute-start.167
  1256.1 5.9 fusion.109
  1262.7 5.2 collective-permute-start.145
  1277.8 5.2 collective-permute-start.146
  (1186 shorter events, 768.6 us)
Async XLA Ops:
  5.3 38.9 %collective-permute-start.3 = (bf16[96,2308]{1,0:T(8,128)(2,1)S(1)}, bf16[96,2308]{1,0:T(8,128)(2,1)S(1)}, u32[]{:S(2)}, u32[]{:S(2)}) collective-permute-start(bf16[96,2308]{1,0:T(8,128)(2,1)S(1)} %dynamic-slice_bitcast_fusion.12), channel_id=1, source_target_pairs={{0,16},{16,0},{1,17},{17,1},{2,18},{18,2},{3,19},{19,3},{4,20},{20... | collective-permute-start | bytes 1329416 | tf_op jit(solution)/shard_map/ppermute | solution.py:181
  13.0 27.3 %collective-permute-start.2 = (bf16[128,768]{1,0:T(8,128)(2,1)S(1)}, bf16[128,768]{1,0:T(8,128)(2,1)}, u32[]{:S(2)}, u32[]{:S(2)}) collective-permute-start(bf16[128,768]{1,0:T(8,128)(2,1)S(1)} %get-tuple-element.119), channel_id=1, source_target_pairs={{0,3},{1,0},{2,1},{3,2},{4,7},{5,4},{6,5},{7,6},{8,11},{9,8},{10,9... | collective-permute-start | bytes 589832 | tf_op jit(solution)/shard_map/ppermute | solution.py:236
  15.5 26.3 %collective-permute-start.107 = (bf16[128,768]{1,0:T(8,128)(2,1)S(1)}, bf16[128,768]{1,0:T(8,128)(2,1)}, u32[]{:S(2)}, u32[]{:S(2)}) collective-permute-start(bf16[128,768]{1,0:T(8,128)(2,1)S(1)} %get-tuple-element.118), channel_id=1, source_target_pairs={{0,1},{1,2},{2,3},{3,0},{4,5},{5,6},{6,7},{7,4},{8,9},{9,10},{10,1... | collective-permute-start | bytes 589832 | tf_op jit(solution)/shard_map/ppermute | solution.py:236
  18.6 25.0 %collective-permute-start.108 = (bf16[128,768]{1,0:T(8,128)(2,1)S(1)}, bf16[128,768]{1,0:T(8,128)(2,1)S(1)}, u32[]{:S(2)}, u32[]{:S(2)}) collective-permute-start(bf16[128,768]{1,0:T(8,128)(2,1)S(1)} %get-tuple-element.117), channel_id=1, source_target_pairs={{0,2},{1,3},{2,0},{3,1},{4,6},{5,7},{6,4},{7,5},{8,10},{9,11},{10,... | collective-permute-start | bytes 589832 | tf_op jit(solution)/shard_map/ppermute | solution.py:236
  55.9 38.9 %collective-permute-start.89 = (bf16[96,768]{1,0:T(8,128)(2,1)}, bf16[96,768]{1,0:T(8,128)(2,1)S(1)}, u32[]{:S(2)}, u32[]{:S(2)}) collective-permute-start(bf16[96,768]{1,0:T(8,128)(2,1)} %get-tuple-element.203), channel_id=1, source_target_pairs={{1,0},{2,1},{3,2},{5,4},{6,5},{7,6},{9,8},{10,9},{11,10},{13,12},{... | collective-permute-start | bytes 442376 | tf_op jit(solution)/shard_map/ppermute | solution.py:204
  57.2 38.9 %collective-permute-start.90 = (bf16[96,768]{1,0:T(8,128)(2,1)}, bf16[96,768]{1,0:T(8,128)(2,1)S(1)}, u32[]{:S(2)}, u32[]{:S(2)}) collective-permute-start(bf16[96,768]{1,0:T(8,128)(2,1)} %get-tuple-element.203), channel_id=1, source_target_pairs={{0,1},{1,2},{2,3},{4,5},{5,6},{6,7},{8,9},{9,10},{10,11},{12,13},{... | collective-permute-start | bytes 442376 | tf_op jit(solution)/shard_map/ppermute | solution.py:203
  61.8 31.8 %collective-permute-start.5 = (bf16[96,576]{1,0:T(8,128)(2,1)}, bf16[96,576]{1,0:T(8,128)(2,1)}, u32[]{:S(2)}, u32[]{:S(2)}) collective-permute-start(bf16[96,576]{1,0:T(8,128)(2,1)} %slice.320), channel_id=1, source_target_pairs={{0,1},{1,2},{2,3},{4,5},{5,6},{6,7},{8,9},{9,10},{10,11},{12,13},{... | collective-permute-start | bytes 331784 | tf_op jit(solution)/shard_map/ppermute | solution.py:203
  65.8 36.2 %collective-permute-start.40 = (bf16[96,768]{1,0:T(8,128)(2,1)}, bf16[96,768]{1,0:T(8,128)(2,1)}, u32[]{:S(2)}, u32[]{:S(2)}) collective-permute-start(bf16[96,768]{1,0:T(8,128)(2,1)} %collective-permute-done.39), channel_id=1, source_target_pairs={{0,1},{1,2},{2,3},{4,5},{5,6},{6,7},{8,9},{9,10},{10,11},{12,13},{... | collective-permute-start | bytes 442376 | tf_op jit(solution)/shard_map/ppermute | solution.py:203
  67.9 38.7 %collective-permute-start.42 = (bf16[96,768]{1,0:T(8,128)(2,1)}, bf16[96,768]{1,0:T(8,128)(2,1)}, u32[]{:S(2)}, u32[]{:S(2)}) collective-permute-start(bf16[96,768]{1,0:T(8,128)(2,1)} %collective-permute-done.38), channel_id=1, source_target_pairs={{1,0},{2,1},{3,2},{5,4},{6,5},{7,6},{9,8},{10,9},{11,10},{13,12},{... | collective-permute-start | bytes 442376 | tf_op jit(solution)/shard_map/ppermute | solution.py:204
  94.9 40.5 %collective-permute-start.24 = (bf16[96,960]{1,0:T(8,128)(2,1)}, bf16[96,960]{1,0:T(8,128)(2,1)}, u32[]{:S(2)}, u32[]{:S(2)}) collective-permute-start(bf16[96,960]{1,0:T(8,128)(2,1)} %get-tuple-element.209), channel_id=1, source_target_pairs={{1,0},{2,1},{3,2},{5,4},{6,5},{7,6},{9,8},{10,9},{11,10},{13,12},{... | collective-permute-start | bytes 552968 | tf_op jit(solution)/shard_map/ppermute | solution.py:204
  108.9 39.2 %collective-permute-start.25 = (bf16[96,960]{1,0:T(8,128)(2,1)}, bf16[96,960]{1,0:T(8,128)(2,1)}, u32[]{:S(2)}, u32[]{:S(2)}) collective-permute-start(bf16[96,960]{1,0:T(8,128)(2,1)} %get-tuple-element.209), channel_id=1, source_target_pairs={{0,1},{1,2},{2,3},{4,5},{5,6},{6,7},{8,9},{9,10},{10,11},{12,13},{... | collective-permute-start | bytes 552968 | tf_op jit(solution)/shard_map/ppermute | solution.py:203
  148.1 42.0 %collective-permute-start.26 = (bf16[96,960]{1,0:T(8,128)(2,1)}, bf16[96,960]{1,0:T(8,128)(2,1)}, u32[]{:S(2)}, u32[]{:S(2)}) collective-permute-start(bf16[96,960]{1,0:T(8,128)(2,1)} %collective-permute-done.25), channel_id=1, source_target_pairs={{0,1},{1,2},{2,3},{4,5},{5,6},{6,7},{8,9},{9,10},{10,11},{12,13},{... | collective-permute-start | bytes 552968 | tf_op jit(solution)/shard_map/ppermute | solution.py:203
  152.0 39.5 %collective-permute-start.28 = (bf16[96,960]{1,0:T(8,128)(2,1)}, bf16[96,960]{1,0:T(8,128)(2,1)}, u32[]{:S(2)}, u32[]{:S(2)}) collective-permute-start(bf16[96,960]{1,0:T(8,128)(2,1)} %collective-permute-done.24), channel_id=1, source_target_pairs={{1,0},{2,1},{3,2},{5,4},{6,5},{7,6},{9,8},{10,9},{11,10},{13,12},{... | collective-permute-start | bytes 552968 | tf_op jit(solution)/shard_map/ppermute | solution.py:204
  153.3 45.8 %collective-permute-start.77 = (bf16[96,960]{1,0:T(8,128)(2,1)}, bf16[96,960]{1,0:T(8,128)(2,1)}, u32[]{:S(2)}, u32[]{:S(2)}) collective-permute-start(bf16[96,960]{1,0:T(8,128)(2,1)} %collective-permute-done.76), channel_id=1, source_target_pairs={{0,1},{1,2},{2,3},{4,5},{5,6},{6,7},{8,9},{9,10},{10,11},{12,13},{... | collective-permute-start | bytes 552968 | tf_op jit(solution)/shard_map/ppermute | solution.py:203
  158.6 41.8 %collective-permute-start.79 = (bf16[96,960]{1,0:T(8,128)(2,1)}, bf16[96,960]{1,0:T(8,128)(2,1)}, u32[]{:S(2)}, u32[]{:S(2)}) collective-permute-start(bf16[96,960]{1,0:T(8,128)(2,1)} %collective-permute-done.75), channel_id=1, source_target_pairs={{1,0},{2,1},{3,2},{5,4},{6,5},{7,6},{9,8},{10,9},{11,10},{13,12},{... | collective-permute-start | bytes 552968 | tf_op jit(solution)/shard_map/ppermute | solution.py:204
  172.8 31.3 %collective-permute-start.41 = (bf16[96,768]{1,0:T(8,128)(2,1)}, bf16[96,768]{1,0:T(8,128)(2,1)}, u32[]{:S(2)}, u32[]{:S(2)}) collective-permute-start(bf16[96,768]{1,0:T(8,128)(2,1)} %collective-permute-done.40), channel_id=1, source_target_pairs={{0,1},{1,2},{2,3},{4,5},{5,6},{6,7},{8,9},{9,10},{10,11},{12,13},{... | collective-permute-start | bytes 442376 | tf_op jit(solution)/shard_map/ppermute | solution.py:203
  191.5 39.0 %collective-permute-start.92 = (bf16[96,768]{1,0:T(8,128)(2,1)}, bf16[96,768]{1,0:T(8,128)(2,1)}, u32[]{:S(2)}, u32[]{:S(2)}) collective-permute-start(bf16[96,768]{1,0:T(8,128)(2,1)} %collective-permute-done.91), channel_id=1, source_target_pairs={{0,1},{1,2},{2,3},{4,5},{5,6},{6,7},{8,9},{9,10},{10,11},{12,13},{... | collective-permute-start | bytes 442376 | tf_op jit(solution)/shard_map/ppermute | solution.py:203
  199.1 33.2 %collective-permute-start.94 = (bf16[96,768]{1,0:T(8,128)(2,1)}, bf16[96,768]{1,0:T(8,128)(2,1)}, u32[]{:S(2)}, u32[]{:S(2)}) collective-permute-start(bf16[96,768]{1,0:T(8,128)(2,1)} %collective-permute-done.93), channel_id=1, source_target_pairs={{1,0},{2,1},{3,2},{5,4},{6,5},{7,6},{9,8},{10,9},{11,10},{13,12},{... | collective-permute-start | bytes 442376 | tf_op jit(solution)/shard_map/ppermute | solution.py:204
  200.4 127.0 %collective-permute-start.10 = (bf16[48,2308]{1,0:T(8,128)(2,1)}, bf16[48,2308]{1,0:T(8,128)(2,1)}, u32[]{:S(2)}, u32[]{:S(2)}) collective-permute-start(bf16[48,2308]{1,0:T(8,128)(2,1)} %get-tuple-element.73), channel_id=1, source_target_pairs={{0,4},{4,0},{1,5},{5,1},{2,6},{6,2},{3,7},{7,3},{8,12},{12,8},{9,1... | collective-permute-start | bytes 664712 | tf_op jit(solution)/shard_map/ppermute | solution.py:181
  204.0 129.9 %collective-permute-start.12 = (bf16[48,2308]{1,0:T(8,128)(2,1)}, bf16[48,2308]{1,0:T(8,128)(2,1)}, u32[]{:S(2)}, u32[]{:S(2)}) collective-permute-start(bf16[48,2308]{1,0:T(8,128)(2,1)} %get-tuple-element.71), channel_id=1, source_target_pairs={{0,8},{8,0},{1,9},{9,1},{2,10},{10,2},{3,11},{11,3},{4,12},{12,4},... | collective-permute-start | bytes 664712 | tf_op jit(solution)/shard_map/ppermute | solution.py:181
  207.6 124.4 %collective-permute-start.61 = (bf16[48,2308]{1,0:T(8,128)(2,1)}, bf16[48,2308]{1,0:T(8,128)(2,1)}, u32[]{:S(2)}, u32[]{:S(2)}) collective-permute-start(bf16[48,2308]{1,0:T(8,128)(2,1)} %get-tuple-element.69), channel_id=1, source_target_pairs={{0,4},{4,0},{1,5},{5,1},{2,6},{6,2},{3,7},{7,3},{8,12},{12,8},{9,1... | collective-permute-start | bytes 664712 | tf_op jit(solution)/shard_map/ppermute | solution.py:181
  230.6 105.4 %collective-permute-start.63 = (bf16[48,2308]{1,0:T(8,128)(2,1)}, bf16[48,2308]{1,0:T(8,128)(2,1)}, u32[]{:S(2)}, u32[]{:S(2)}) collective-permute-start(bf16[48,2308]{1,0:T(8,128)(2,1)} %get-tuple-element.67), channel_id=1, source_target_pairs={{0,8},{8,0},{1,9},{9,1},{2,10},{10,2},{3,11},{11,3},{4,12},{12,4},... | collective-permute-start | bytes 664712 | tf_op jit(solution)/shard_map/ppermute | solution.py:181
  232.3 35.6 %collective-permute-start.27 = (bf16[96,960]{1,0:T(8,128)(2,1)}, bf16[96,960]{1,0:T(8,128)(2,1)}, u32[]{:S(2)}, u32[]{:S(2)}) collective-permute-start(bf16[96,960]{1,0:T(8,128)(2,1)} %collective-permute-done.26), channel_id=1, source_target_pairs={{0,1},{1,2},{2,3},{4,5},{5,6},{6,7},{8,9},{9,10},{10,11},{12,13},{... | collective-permute-start | bytes 552968 | tf_op jit(solution)/shard_map/ppermute | solution.py:203
  301.8 37.4 %collective-permute-start.44 = (bf16[48,3072]{1,0:T(8,128)(2,1)}, bf16[48,3072]{1,0:T(8,128)(2,1)}, u32[]{:S(2)}, u32[]{:S(2)}) collective-permute-start(bf16[48,3072]{1,0:T(8,128)(2,1)} %bitcast.1151), channel_id=1, source_target_pairs={{0,4},{4,0},{1,5},{5,1},{2,6},{6,2},{3,7},{7,3},{8,12},{12,8},{9,1... | collective-permute-start | bytes 884744 | tf_op jit(solution)/shard_map/ppermute | solution.py:181
  363.7 45.0 %collective-permute-start.16 = (bf16[2,48,2308]{2,1,0:T(8,128)(2,1)S(1)}, bf16[2,48,2308]{2,1,0:T(8,128)(2,1)S(1)}, u32[]{:S(2)}, u32[]{:S(2)}) collective-permute-start(bf16[2,48,2308]{2,1,0:T(8,128)(2,1)S(1)} %bitcast_dynamic-update-slice_fusion.77), channel_id=1, source_target_pairs={{0,4},{4,0},{1,5},{5,1},{2,6},{6,2},{3,7},{7,3},{8,12},{12,8},{9,1... | collective-permute-start | bytes 1329416 | tf_op jit(solution)/shard_map/ppermute | solution.py:181
  369.0 74.6 %collective-permute-start.67 = (bf16[2,48,2308]{2,1,0:T(8,128)(2,1)}, bf16[2,48,2308]{2,1,0:T(8,128)(2,1)}, u32[]{:S(2)}, u32[]{:S(2)}) collective-permute-start(bf16[2,48,2308]{2,1,0:T(8,128)(2,1)} %bitcast_dynamic-update-slice_fusion.73), channel_id=1, source_target_pairs={{0,4},{4,0},{1,5},{5,1},{2,6},{6,2},{3,7},{7,3},{8,12},{12,8},{9,1... | collective-permute-start | bytes 1329416 | tf_op jit(solution)/shard_map/ppermute | solution.py:181
  385.2 96.4 %collective-permute-start.50 = (bf16[2,48,3072]{2,1,0:T(8,128)(2,1)}, bf16[2,48,3072]{2,1,0:T(8,128)(2,1)}, u32[]{:S(2)}, u32[]{:S(2)}) collective-permute-start(bf16[2,48,3072]{2,1,0:T(8,128)(2,1)} %bitcast_dynamic-update-slice_fusion.71), channel_id=1, source_target_pairs={{0,4},{4,0},{1,5},{5,1},{2,6},{6,2},{3,7},{7,3},{8,12},{12,8},{9,1... | collective-permute-start | bytes 1769480 | tf_op jit(solution)/shard_map/ppermute | solution.py:181
  393.9 88.0 %collective-permute-start.101 = (bf16[2,48,3072]{2,1,0:T(8,128)(2,1)}, bf16[2,48,3072]{2,1,0:T(8,128)(2,1)}, u32[]{:S(2)}, u32[]{:S(2)}) collective-permute-start(bf16[2,48,3072]{2,1,0:T(8,128)(2,1)} %bitcast_dynamic-update-slice_fusion.69), channel_id=1, source_target_pairs={{0,4},{4,0},{1,5},{5,1},{2,6},{6,2},{3,7},{7,3},{8,12},{12,8},{9,1... | collective-permute-start | bytes 1769480 | tf_op jit(solution)/shard_map/ppermute | solution.py:181
  408.7 44.2 %collective-permute-start.31 = (bf16[2,48,3840]{2,1,0:T(8,128)(2,1)}, bf16[2,48,3840]{2,1,0:T(8,128)(2,1)}, u32[]{:S(2)}, u32[]{:S(2)}) collective-permute-start(bf16[2,48,3840]{2,1,0:T(8,128)(2,1)} %bitcast_dynamic-update-slice_fusion.67), channel_id=1, source_target_pairs={{0,16},{16,0},{1,17},{17,1},{2,18},{18,2},{3,19},{19,3},{4,20},{20... | collective-permute-start | bytes 2211848 | tf_op jit(solution)/shard_map/ppermute | solution.py:181
  411.6 32.6 %collective-permute-start.66 = (bf16[2,48,2308]{2,1,0:T(8,128)(2,1)}, bf16[2,48,2308]{2,1,0:T(8,128)(2,1)}, u32[]{:S(2)}, u32[]{:S(2)}) collective-permute-start(bf16[2,48,2308]{2,1,0:T(8,128)(2,1)} %collective-permute-done.65), channel_id=1, source_target_pairs={{0,16},{16,0},{1,17},{17,1},{2,18},{18,2},{3,19},{19,3},{4,20},{20... | collective-permute-start | bytes 1329416 | tf_op jit(solution)/shard_map/ppermute | solution.py:181
  457.0 50.2 %collective-permute-start.36 = (bf16[2,48,3840]{2,1,0:T(8,128)(2,1)}, bf16[2,48,3840]{2,1,0:T(8,128)(2,1)}, u32[]{:S(2)}, u32[]{:S(2)}) collective-permute-start(bf16[2,48,3840]{2,1,0:T(8,128)(2,1)} %bitcast_dynamic-update-slice_fusion.65), channel_id=1, source_target_pairs={{0,4},{4,0},{1,5},{5,1},{2,6},{6,2},{3,7},{7,3},{8,12},{12,8},{9,1... | collective-permute-start | bytes 2211848 | tf_op jit(solution)/shard_map/ppermute | solution.py:181
  465.1 42.6 %collective-permute-start.87 = (bf16[2,48,3840]{2,1,0:T(8,128)(2,1)}, bf16[2,48,3840]{2,1,0:T(8,128)(2,1)}, u32[]{:S(2)}, u32[]{:S(2)}) collective-permute-start(bf16[2,48,3840]{2,1,0:T(8,128)(2,1)} %bitcast_dynamic-update-slice_fusion.61), channel_id=1, source_target_pairs={{0,4},{4,0},{1,5},{5,1},{2,6},{6,2},{3,7},{7,3},{8,12},{12,8},{9,1... | collective-permute-start | bytes 2211848 | tf_op jit(solution)/shard_map/ppermute | solution.py:181
  490.9 25.9 %collective-permute-start.20 = (bf16[4,128,576]{1,2,0:T(8,128)(2,1)}, bf16[4,128,576]{1,2,0:T(8,128)(2,1)}, u32[]{:S(2)}, u32[]{:S(2)}) collective-permute-start(bf16[4,128,576]{1,2,0:T(8,128)(2,1)} %bitcast.58), channel_id=1, source_target_pairs={{0,20},{4,16},{16,4},{20,0},{1,21},{5,17},{17,5},{21,1},{2,22},{6,... | collective-permute-start | bytes 1769480 | tf_op jit(solution)/shard_map/ppermute | solution.py:259
  505.0 57.4 %collective-permute-start.35 = (bf16[2,48,3840]{2,1,0:T(8,128)(2,1)}, bf16[2,48,3840]{2,1,0:T(8,128)(2,1)}, u32[]{:S(2)}, u32[]{:S(2)}) collective-permute-start(bf16[2,48,3840]{2,1,0:T(8,128)(2,1)} %collective-permute-done.34), channel_id=1, source_target_pairs={{0,16},{16,0},{1,17},{17,1},{2,18},{18,2},{3,19},{19,3},{4,20},{20... | collective-permute-start | bytes 2211848 | tf_op jit(solution)/shard_map/ppermute | solution.py:181
  507.2 103.4 %collective-permute-start.86 = (bf16[2,48,3840]{2,1,0:T(8,128)(2,1)}, bf16[2,48,3840]{2,1,0:T(8,128)(2,1)}, u32[]{:S(2)}, u32[]{:S(2)}) collective-permute-start(bf16[2,48,3840]{2,1,0:T(8,128)(2,1)} %copy-done.106), channel_id=1, source_target_pairs={{0,16},{16,0},{1,17},{17,1},{2,18},{18,2},{3,19},{19,3},{4,20},{20... | collective-permute-start | bytes 2211848 | tf_op jit(solution)/shard_map/ppermute | solution.py:181
  507.7 59.0 %collective-permute-start.37 = (bf16[2,48,3840]{2,1,0:T(8,128)(2,1)}, bf16[2,48,3840]{2,1,0:T(8,128)(2,1)}, u32[]{:S(2)}, u32[]{:S(2)}) collective-permute-start(bf16[2,48,3840]{2,1,0:T(8,128)(2,1)} %collective-permute-done.36), channel_id=1, source_target_pairs={{0,16},{16,0},{1,17},{17,1},{2,18},{18,2},{3,19},{19,3},{4,20},{20... | collective-permute-start | bytes 2211848 | tf_op jit(solution)/shard_map/ppermute | solution.py:181
  507.8 107.4 %collective-permute-start.88 = (bf16[2,48,3840]{2,1,0:T(8,128)(2,1)}, bf16[2,48,3840]{2,1,0:T(8,128)(2,1)}, u32[]{:S(2)}, u32[]{:S(2)}) collective-permute-start(bf16[2,48,3840]{2,1,0:T(8,128)(2,1)} %collective-permute-done.87), channel_id=1, source_target_pairs={{0,16},{16,0},{1,17},{17,1},{2,18},{18,2},{3,19},{19,3},{4,20},{20... | collective-permute-start | bytes 2211848 | tf_op jit(solution)/shard_map/ppermute | solution.py:181
  584.1 41.4 %collective-permute-start.52 = (bf16[128,768]{1,0:T(8,128)(2,1)}, bf16[128,768]{1,0:T(8,128)(2,1)}, u32[]{:S(2)}, u32[]{:S(2)}) collective-permute-start(bf16[128,768]{1,0:T(8,128)(2,1)} %get-tuple-element.166), channel_id=1, source_target_pairs={{0,1},{1,2},{2,3},{3,0},{4,5},{5,6},{6,7},{7,4},{8,9},{9,10},{10,1... | collective-permute-start | bytes 589832 | tf_op jit(solution)/shard_map/ppermute | solution.py:236
  585.9 42.1 %collective-permute-start.53 = (bf16[128,768]{1,0:T(8,128)(2,1)}, bf16[128,768]{1,0:T(8,128)(2,1)}, u32[]{:S(2)}, u32[]{:S(2)}) collective-permute-start(bf16[128,768]{1,0:T(8,128)(2,1)} %get-tuple-element.165), channel_id=1, source_target_pairs={{0,2},{1,3},{2,0},{3,1},{4,6},{5,7},{6,4},{7,5},{8,10},{9,11},{10,... | collective-permute-start | bytes 589832 | tf_op jit(solution)/shard_map/ppermute | solution.py:236
  585.9 43.0 %collective-permute-start.54 = (bf16[128,768]{1,0:T(8,128)(2,1)}, bf16[128,768]{1,0:T(8,128)(2,1)}, u32[]{:S(2)}, u32[]{:S(2)}) collective-permute-start(bf16[128,768]{1,0:T(8,128)(2,1)} %get-tuple-element.164), channel_id=1, source_target_pairs={{0,3},{1,0},{2,1},{3,2},{4,7},{5,4},{6,5},{7,6},{8,11},{9,8},{10,9... | collective-permute-start | bytes 589832 | tf_op jit(solution)/shard_map/ppermute | solution.py:236
  725.0 56.7 %collective-permute-start.103 = (bf16[128,768]{1,0:T(8,128)(2,1)}, bf16[128,768]{1,0:T(8,128)(2,1)}, u32[]{:S(2)}, u32[]{:S(2)}) collective-permute-start(bf16[128,768]{1,0:T(8,128)(2,1)} %get-tuple-element.162), channel_id=1, source_target_pairs={{0,1},{1,2},{2,3},{3,0},{4,5},{5,6},{6,7},{7,4},{8,9},{9,10},{10,1... | collective-permute-start | bytes 589832 | tf_op jit(solution)/shard_map/ppermute | solution.py:236
  725.2 58.1 %collective-permute-start.104 = (bf16[128,768]{1,0:T(8,128)(2,1)}, bf16[128,768]{1,0:T(8,128)(2,1)}, u32[]{:S(2)}, u32[]{:S(2)}) collective-permute-start(bf16[128,768]{1,0:T(8,128)(2,1)} %get-tuple-element.161), channel_id=1, source_target_pairs={{0,2},{1,3},{2,0},{3,1},{4,6},{5,7},{6,4},{7,5},{8,10},{9,11},{10,... | collective-permute-start | bytes 589832 | tf_op jit(solution)/shard_map/ppermute | solution.py:236
  740.5 44.4 %collective-permute-start.105 = (bf16[128,768]{1,0:T(8,128)(2,1)}, bf16[128,768]{1,0:T(8,128)(2,1)}, u32[]{:S(2)}, u32[]{:S(2)}) collective-permute-start(bf16[128,768]{1,0:T(8,128)(2,1)} %get-tuple-element.160), channel_id=1, source_target_pairs={{0,3},{1,0},{2,1},{3,2},{4,7},{5,4},{6,5},{7,6},{8,11},{9,8},{10,9... | collective-permute-start | bytes 589832 | tf_op jit(solution)/shard_map/ppermute | solution.py:236
  789.1 144.1 %collective-permute-start.106 = (bf16[4,128,768]{2,1,0:T(8,128)(2,1)}, bf16[4,128,768]{2,1,0:T(8,128)(2,1)}, u32[]{:S(2)}, u32[]{:S(2)}) collective-permute-start(bf16[4,128,768]{2,1,0:T(8,128)(2,1)} %broadcast_select_fusion.1), channel_id=1, source_target_pairs={{0,16},{16,0},{1,17},{17,1},{2,18},{18,2},{3,19},{19,3},{4,20},{20... | collective-permute-start | bytes 2359304 | tf_op jit(solution)/shard_map/ppermute | solution.py:181
  844.6 44.8 %collective-permute-start.116 = (bf16[4,128,192]{1,2,0:T(8,128)(2,1)}, bf16[4,128,192]{1,2,0:T(8,128)(2,1)}, u32[]{:S(2)}, u32[]{:S(2)}) collective-permute-start(bf16[4,128,192]{1,2,0:T(8,128)(2,1)} %bitcast.1031), channel_id=1, source_target_pairs={{0,4},{4,0},{16,20},{20,16},{1,5},{5,1},{17,21},{21,17},{2,6},{6,2... | collective-permute-start | bytes 589832 | tf_op jit(solution)/shard_map/ppermute | solution.py:259
  847.4 44.3 %collective-permute-start.117 = (bf16[4,128,192]{1,2,0:T(8,128)(2,1)}, bf16[4,128,192]{1,2,0:T(8,128)(2,1)}, u32[]{:S(2)}, u32[]{:S(2)}) collective-permute-start(bf16[4,128,192]{1,2,0:T(8,128)(2,1)} %bitcast.1030), channel_id=1, source_target_pairs={{0,16},{4,20},{16,0},{20,4},{1,17},{5,21},{17,1},{21,5},{2,18},{6,... | collective-permute-start | bytes 589832 | tf_op jit(solution)/shard_map/ppermute | solution.py:259
  848.1 47.6 %collective-permute-start.118 = (bf16[4,128,192]{1,2,0:T(8,128)(2,1)}, bf16[4,128,192]{1,2,0:T(8,128)(2,1)}, u32[]{:S(2)}, u32[]{:S(2)}) collective-permute-start(bf16[4,128,192]{1,2,0:T(8,128)(2,1)} %bitcast.1029), channel_id=1, source_target_pairs={{0,20},{4,16},{16,4},{20,0},{1,21},{5,17},{17,5},{21,1},{2,22},{6,... | collective-permute-start | bytes 589832 | tf_op jit(solution)/shard_map/ppermute | solution.py:259
  872.3 64.4 %collective-permute-start.125 = (bf16[128,768]{1,0:T(8,128)(2,1)}, bf16[128,768]{1,0:T(8,128)(2,1)}, u32[]{:S(2)}, u32[]{:S(2)}) collective-permute-start(bf16[128,768]{1,0:T(8,128)(2,1)} %get-tuple-element.146), channel_id=1, source_target_pairs={{0,1},{1,2},{2,3},{3,0},{4,5},{5,6},{6,7},{7,4},{8,9},{9,10},{10,1... | collective-permute-start | bytes 589832 | tf_op jit(solution)/shard_map/ppermute | solution.py:236
  889.4 49.4 %collective-permute-start.126 = (bf16[128,768]{1,0:T(8,128)(2,1)}, bf16[128,768]{1,0:T(8,128)(2,1)}, u32[]{:S(2)}, u32[]{:S(2)}) collective-permute-start(bf16[128,768]{1,0:T(8,128)(2,1)} %get-tuple-element.145), channel_id=1, source_target_pairs={{0,2},{1,3},{2,0},{3,1},{4,6},{5,7},{6,4},{7,5},{8,10},{9,11},{10,... | collective-permute-start | bytes 589832 | tf_op jit(solution)/shard_map/ppermute | solution.py:236
  891.6 49.6 %collective-permute-start.127 = (bf16[128,768]{1,0:T(8,128)(2,1)}, bf16[128,768]{1,0:T(8,128)(2,1)}, u32[]{:S(2)}, u32[]{:S(2)}) collective-permute-start(bf16[128,768]{1,0:T(8,128)(2,1)} %get-tuple-element.144), channel_id=1, source_target_pairs={{0,3},{1,0},{2,1},{3,2},{4,7},{5,4},{6,5},{7,6},{8,11},{9,8},{10,9... | collective-permute-start | bytes 589832 | tf_op jit(solution)/shard_map/ppermute | solution.py:236
  895.7 125.7 %collective-permute-start.140 = (bf16[2,2,96,3840]{3,2,0,1:T(8,128)(2,1)}, bf16[2,2,96,3840]{3,2,0,1:T(8,128)(2,1)}, u32[]{:S(2)}, u32[]{:S(2)}) collective-permute-start(bf16[2,2,96,3840]{3,2,0,1:T(8,128)(2,1)} %bitcast.1097), channel_id=1, source_target_pairs={{0,16},{16,0},{1,17},{17,1},{2,18},{18,2},{3,19},{19,3},{4,20},{20... | collective-permute-start | bytes 8847368 | tf_op jit(solution)/shard_map/ppermute | solution.py:181
  933.2 75.5 %collective-permute-start.151 = (bf16[2,2,96,3072]{3,2,0,1:T(8,128)(2,1)}, bf16[2,2,96,3072]{3,2,0,1:T(8,128)(2,1)}, u32[]{:S(2)}, u32[]{:S(2)}) collective-permute-start(bf16[2,2,96,3072]{3,2,0,1:T(8,128)(2,1)} %bitcast.1107), channel_id=1, source_target_pairs={{0,16},{16,0},{1,17},{17,1},{2,18},{18,2},{3,19},{19,3},{4,20},{20... | collective-permute-start | bytes 7077896 | tf_op jit(solution)/shard_map/ppermute | solution.py:181
  953.2 72.5 %collective-permute-start.173 = (bf16[2,2,96,3840]{3,2,0,1:T(8,128)(2,1)}, bf16[2,2,96,3840]{3,2,0,1:T(8,128)(2,1)}, u32[]{:S(2)}, u32[]{:S(2)}) collective-permute-start(bf16[2,2,96,3840]{3,2,0,1:T(8,128)(2,1)} %bitcast.1096), channel_id=1, source_target_pairs={{0,16},{16,0},{1,17},{17,1},{2,18},{18,2},{3,19},{19,3},{4,20},{20... | collective-permute-start | bytes 8847368 | tf_op jit(solution)/shard_map/ppermute | solution.py:181
  954.2 58.5 %collective-permute-start.184 = (bf16[2,2,96,3072]{3,2,0,1:T(8,128)(2,1)}, bf16[2,2,96,3072]{3,2,0,1:T(8,128)(2,1)}, u32[]{:S(2)}, u32[]{:S(2)}) collective-permute-start(bf16[2,2,96,3072]{3,2,0,1:T(8,128)(2,1)} %bitcast.1106), channel_id=1, source_target_pairs={{0,16},{16,0},{1,17},{17,1},{2,18},{18,2},{3,19},{19,3},{4,20},{20... | collective-permute-start | bytes 7077896 | tf_op jit(solution)/shard_map/ppermute | solution.py:181
  1021.4 24.6 %collective-permute-start.185 = (bf16[2,48,3072]{2,1,0:T(8,128)(2,1)S(1)}, bf16[2,48,3072]{2,1,0:T(8,128)(2,1)S(1)}, u32[]{:S(2)}, u32[]{:S(2)}) collective-permute-start(bf16[2,48,3072]{2,1,0:T(8,128)(2,1)S(1)} %dynamic-slice_bitcast_fusion.5), channel_id=1, source_target_pairs={{0,8},{8,0},{1,9},{9,1},{2,10},{10,2},{3,11},{11,3},{4,12},{12,4},... | collective-permute-start | bytes 1769480 | tf_op jit(solution)/shard_map/ppermute | solution.py:181
  1025.7 25.9 %collective-permute-start.132 = (bf16[2,48,2308]{2,1,0:T(8,128)(2,1)S(1)}, bf16[2,48,2308]{2,1,0:T(8,128)(2,1)S(1)}, u32[]{:S(2)}, u32[]{:S(2)}) collective-permute-start(bf16[2,48,2308]{2,1,0:T(8,128)(2,1)S(1)} %dynamic-slice_bitcast_fusion.10), channel_id=1, source_target_pairs={{0,4},{4,0},{1,5},{5,1},{2,6},{6,2},{3,7},{7,3},{8,12},{12,8},{9,1... | collective-permute-start | bytes 1329416 | tf_op jit(solution)/shard_map/ppermute | solution.py:181
  1031.1 24.8 %collective-permute-start.130 = (bf16[2,48,2308]{2,1,0:T(8,128)(2,1)S(1)}, bf16[2,48,2308]{2,1,0:T(8,128)(2,1)S(1)}, u32[]{:S(2)}, u32[]{:S(2)}) collective-permute-start(bf16[2,48,2308]{2,1,0:T(8,128)(2,1)S(1)} %dynamic-slice_bitcast_fusion.11), channel_id=1, source_target_pairs={{0,8},{8,0},{1,9},{9,1},{2,10},{10,2},{3,11},{11,3},{4,12},{12,4},... | collective-permute-start | bytes 1329416 | tf_op jit(solution)/shard_map/ppermute | solution.py:181
  1033.7 27.9 %collective-permute-start.165 = (bf16[2,48,2308]{2,1,0:T(8,128)(2,1)S(1)}, bf16[2,48,2308]{2,1,0:T(8,128)(2,1)S(1)}, u32[]{:S(2)}, u32[]{:S(2)}) collective-permute-start(bf16[2,48,2308]{2,1,0:T(8,128)(2,1)S(1)} %dynamic-slice_bitcast_fusion.8), channel_id=1, source_target_pairs={{0,4},{4,0},{1,5},{5,1},{2,6},{6,2},{3,7},{7,3},{8,12},{12,8},{9,1... | collective-permute-start | bytes 1329416 | tf_op jit(solution)/shard_map/ppermute | solution.py:181
  1045.9 193.3 %collective-permute-start.143 = (bf16[2,48,3840]{2,1,0:T(8,128)(2,1)}, bf16[2,48,3840]{2,1,0:T(8,128)(2,1)}, u32[]{:S(2)}, u32[]{:S(2)}) collective-permute-start(bf16[2,48,3840]{2,1,0:T(8,128)(2,1)} %dynamic-slice_bitcast_fusion.2), channel_id=1, source_target_pairs={{0,4},{4,0},{1,5},{5,1},{2,6},{6,2},{3,7},{7,3},{8,12},{12,8},{9,1... | collective-permute-start | bytes 2211848 | tf_op jit(solution)/shard_map/ppermute | solution.py:181
  1051.6 190.5 %collective-permute-start.141 = (bf16[2,48,3840]{2,1,0:T(8,128)(2,1)}, bf16[2,48,3840]{2,1,0:T(8,128)(2,1)}, u32[]{:S(2)}, u32[]{:S(2)}) collective-permute-start(bf16[2,48,3840]{2,1,0:T(8,128)(2,1)} %dynamic-slice_bitcast_fusion.3), channel_id=1, source_target_pairs={{0,8},{8,0},{1,9},{9,1},{2,10},{10,2},{3,11},{11,3},{4,12},{12,4},... | collective-permute-start | bytes 2211848 | tf_op jit(solution)/shard_map/ppermute | solution.py:181
  1055.9 72.5 %collective-permute-start.155 = (bf16[48,3072]{1,0:T(8,128)(2,1)}, bf16[48,3072]{1,0:T(8,128)(2,1)}, u32[]{:S(2)}, u32[]{:S(2)}) collective-permute-start(bf16[48,3072]{1,0:T(8,128)(2,1)} %dynamic-slice_bitcast_fusion.19), channel_id=1, source_target_pairs={{0,8},{8,0},{1,9},{9,1},{2,10},{10,2},{3,11},{11,3},{4,12},{12,4},... | collective-permute-start | bytes 884744 | tf_op jit(solution)/shard_map/ppermute | solution.py:181
  1061.6 69.5 %collective-permute-start.153 = (bf16[48,3072]{1,0:T(8,128)(2,1)}, bf16[48,3072]{1,0:T(8,128)(2,1)}, u32[]{:S(2)}, u32[]{:S(2)}) collective-permute-start(bf16[48,3072]{1,0:T(8,128)(2,1)} %dynamic-slice_bitcast_fusion.20), channel_id=1, source_target_pairs={{0,4},{4,0},{1,5},{5,1},{2,6},{6,2},{3,7},{7,3},{8,12},{12,8},{9,1... | collective-permute-start | bytes 884744 | tf_op jit(solution)/shard_map/ppermute | solution.py:181
  1066.0 26.8 %collective-permute-start.133 = (bf16[48,2308]{1,0:T(8,128)(2,1)S(1)}, bf16[48,2308]{1,0:T(8,128)(2,1)S(1)}, u32[]{:S(2)}, u32[]{:S(2)}) collective-permute-start(bf16[48,2308]{1,0:T(8,128)(2,1)S(1)} %dynamic-slice_bitcast_fusion.23), channel_id=1, source_target_pairs={{0,8},{8,0},{1,9},{9,1},{2,10},{10,2},{3,11},{11,3},{4,12},{12,4},... | collective-permute-start | bytes 664712 | tf_op jit(solution)/shard_map/ppermute | solution.py:181
  1113.3 131.1 %collective-permute-start.176 = (bf16[2,48,3840]{2,1,0:T(8,128)(2,1)}, bf16[2,48,3840]{2,1,0:T(8,128)(2,1)}, u32[]{:S(2)}, u32[]{:S(2)}) collective-permute-start(bf16[2,48,3840]{2,1,0:T(8,128)(2,1)} %dynamic-slice_bitcast_fusion), channel_id=1, source_target_pairs={{0,4},{4,0},{1,5},{5,1},{2,6},{6,2},{3,7},{7,3},{8,12},{12,8},{9,1... | collective-permute-start | bytes 2211848 | tf_op jit(solution)/shard_map/ppermute | solution.py:181
  (275 other events, 4366.7 us)

commit v2 on v1

v2 whole, which is shorter than its diff:
```python
import functools

import jax
import jax.numpy as jnp
from jax import lax
from jax.experimental import pallas as pl
from jax.experimental.pallas import tpu as pltpu
from jax.experimental.layout import Layout, with_layout_constraint
from jax.sharding import PartitionSpec as P

HEAD_DIM = 64
EPS = 1e-05
NEG = -1e30
BLOCK = 512
SCALE = HEAD_DIM ** (-0.5)
F32 = jnp.float32
BF16 = jnp.bfloat16
VMEM_LIMIT = 48 * 1024 * 1024


def normed(values, gain_row, shift_row):
    center = values - jnp.mean(values, -1, keepdims=True)
    spread = jnp.mean(center * center, -1, keepdims=True)
    return center * lax.rsqrt(spread + EPS) * gain_row + shift_row


def dot(left, right, contract):
    return lax.dot_general(left, right, ((contract[0], contract[1]), ((), ())),
                           preferred_element_type=F32)


def attend_kernel(block, heads, rows_ref, all_ref, mix_ref, log_ref):
    place = pl.program_id(0)
    width = heads * HEAD_DIM
    row_ids = lax.broadcasted_iota(jnp.int32, (block, block), 0)
    col_ids = lax.broadcasted_iota(jnp.int32, (block, block), 1)
    for head in range(heads):
        low = head * HEAD_DIM
        queries = rows_ref[:, low:low + HEAD_DIM] * jnp.asarray(SCALE, BF16)

        def step(index, carry, masked):
            top, total, mixed = carry
            span = pl.ds(pl.multiple_of(index * block, block), block)
            keys = all_ref[span, width + low:width + low + HEAD_DIM]
            values = all_ref[span, 2 * width + low:2 * width + low + HEAD_DIM]
            scores = dot(queries, keys, ((1,), (1,)))
            if masked:
                scores = jnp.where(col_ids <= row_ids, scores, NEG)
            new_top = jnp.maximum(top, jnp.max(scores, -1, keepdims=True))
            grown = jnp.exp(scores - new_top)
            shrink = jnp.exp(top - new_top)
            return (
                new_top,
                total * shrink + jnp.sum(grown, -1, keepdims=True),
                mixed * shrink + dot(grown.astype(BF16), values, ((1,), (0,))),
            )

        carry = (
            jnp.full((block, 1), NEG, F32),
            jnp.zeros((block, 1), F32),
            jnp.zeros((block, HEAD_DIM), F32),
        )
        carry = lax.fori_loop(0, place, lambda i, c: step(i, c, False), carry)
        top, total, mixed = step(place, carry, True)
        mix_ref[:, low:low + HEAD_DIM] = (mixed / total).astype(BF16)
        wide = jnp.broadcast_to(top + jnp.log(total), (block, 128))
        log_ref[head] = wide.T[:1]


def attend(packed, heads):
    length, width = packed.shape
    block = min(BLOCK, length)
    return pl.pallas_call(
        functools.partial(attend_kernel, block, heads),
        grid=(length // block,),
        in_specs=[
            pl.BlockSpec((block, width), lambda i: (i, 0)),
            pl.BlockSpec((length, width), lambda i: (0, 0)),
        ],
        out_specs=[
            pl.BlockSpec((block, width // 3), lambda i: (i, 0)),
            pl.BlockSpec((heads, 1, block), lambda i: (0, 0, i)),
        ],
        out_shape=[
            jax.ShapeDtypeStruct((length, width // 3), BF16),
            jax.ShapeDtypeStruct((heads, 1, length), F32),
        ],
        compiler_params=pltpu.CompilerParams(vmem_limit_bytes=VMEM_LIMIT),
        cost_estimate=pl.CostEstimate(
            flops=2 * 2 * length * length * HEAD_DIM * heads,
            bytes_accessed=length * width * 4,
            transcendentals=length * length * heads // 2,
        ),
        name="attend",
    )(packed, packed)


def attend_back_kernel(block, heads, rows_ref, all_ref, grad_ref, mix_ref, log_ref, out_ref,
                       query_sum, inner):
    place = pl.program_id(0)
    count = pl.num_programs(0)
    width = heads * HEAD_DIM
    key_ids = lax.broadcasted_iota(jnp.int32, (block, block), 0)
    query_ids = lax.broadcasted_iota(jnp.int32, (block, block), 1)

    @pl.when(place == 0)
    def prepare():
        query_sum[...] = jnp.zeros_like(query_sum)

        def one(index, carry):
            span = pl.ds(pl.multiple_of(index * block, block), block)
            product = grad_ref[span, :].astype(F32) * mix_ref[span, :].astype(F32)
            for head in range(heads):
                part = product[:, head * HEAD_DIM:(head + 1) * HEAD_DIM]
                inner[head, :, span] = jnp.sum(part.T, 0, keepdims=True)
            return carry

        lax.fori_loop(0, count, one, 0)

    for head in range(heads):
        low = head * HEAD_DIM
        keys = rows_ref[:, width + low:width + low + HEAD_DIM] * jnp.asarray(SCALE, BF16)
        values = rows_ref[:, 2 * width + low:2 * width + low + HEAD_DIM]

        def step(index, carry, masked):
            key_sum, value_sum = carry
            span = pl.ds(pl.multiple_of(index * block, block), block)
            queries = all_ref[span, low:low + HEAD_DIM]
            grads = grad_ref[span, low:low + HEAD_DIM]
            scores = dot(keys, queries, ((1,), (1,)))
            if masked:
                scores = jnp.where(key_ids <= query_ids, scores, NEG)
            probs = jnp.exp(scores - log_ref[head, :, span])
            grad_probs = dot(values, grads, ((1,), (1,)))
            grad_scores = (probs * (grad_probs - inner[head, :, span])).astype(BF16)
            value_sum = value_sum + dot(probs.astype(BF16), grads, ((1,), (0,)))
            key_sum = key_sum + dot(grad_scores, queries, ((1,), (0,)))
            query_sum[head, span, :] += dot(grad_scores, keys, ((0,), (0,)))
            return key_sum, value_sum

        carry = (jnp.zeros((block, HEAD_DIM), F32), jnp.zeros((block, HEAD_DIM), F32))
        carry = step(place, carry, True)
        key_sum, value_sum = lax.fori_loop(
            place + 1, count, lambda i, c: step(i, c, False), carry)
        own = pl.ds(pl.multiple_of(place * block, block), block)
        out_ref[:, low:low + HEAD_DIM] = query_sum[head, own, :].astype(BF16)
        out_ref[:, width + low:width + low + HEAD_DIM] = (key_sum * SCALE).astype(BF16)
        out_ref[:, 2 * width + low:2 * width + low + HEAD_DIM] = value_sum.astype(BF16)


def attend_back(packed, grads, mixture, logs, heads):
    length, width = packed.shape
    block = min(BLOCK, length)
    third = width // 3
    return pl.pallas_call(
        functools.partial(attend_back_kernel, block, heads),
        grid=(length // block,),
        in_specs=[
            pl.BlockSpec((block, width), lambda i: (i, 0)),
            pl.BlockSpec((length, width), lambda i: (0, 0)),
            pl.BlockSpec((length, third), lambda i: (0, 0)),
            pl.BlockSpec((length, third), lambda i: (0, 0)),
            pl.BlockSpec((heads, 1, length), lambda i: (0, 0, 0)),
        ],
        out_specs=pl.BlockSpec((block, width), lambda i: (i, 0)),
        out_shape=jax.ShapeDtypeStruct((length, width), BF16),
        scratch_shapes=[
            pltpu.VMEM((heads, length, HEAD_DIM), F32),
            pltpu.VMEM((heads, 1, length), F32),
        ],
        compiler_params=pltpu.CompilerParams(vmem_limit_bytes=VMEM_LIMIT),
        cost_estimate=pl.CostEstimate(
            flops=2 * 5 * length * length * HEAD_DIM * heads,
            bytes_accessed=length * width * 8,
            transcendentals=length * length * heads // 2,
        ),
        name="attend_back",
    )(packed, packed, grads, mixture, logs)


def swap(value, axis):
    return lax.ppermute(value, axis, [(0, 1), (1, 0)])


def take(buffer, index, axis=0):
    return lax.dynamic_index_in_dim(buffer, index, axis, keepdims=False)


def paired(near, far, place, axis):
    first = jnp.where(place == 0, near, far)
    second = jnp.where(place == 0, far, near)
    return jnp.concatenate([first, second], axis)


def in_order(blocks, place):
    if len(blocks) == 2:
        return paired(blocks[0][None], blocks[1][None], place, 0)
    stacked = jnp.zeros((len(blocks),) + blocks[0].shape, blocks[0].dtype)
    for step, block in enumerate(blocks):
        stacked = lax.dynamic_update_index_in_dim(
            stacked, block, lax.bitwise_xor(place, step), 0)
    return stacked


def hold(value, *others):
    return lax.optimization_barrier((value,) + others)[0]


def spread_tensor(blocks):
    return lax.all_to_all(blocks, "tensor", 0, 0, tiled=True)


def square():
    return lax.axis_size("dp") == 2 and lax.axis_size("context") == 2


def reorder(values):
    if not square():
        return values
    dp, ctx = lax.axis_index("dp"), lax.axis_index("context")
    size = values.shape[-1] // 4
    half = 2 * size
    values = jnp.where(dp == 1, jnp.concatenate([values[..., half:], values[..., :half]], -1), values)
    blocks = [values[..., n * size:(n + 1) * size] for n in range(4)]
    turned = jnp.concatenate([blocks[1], blocks[0], blocks[3], blocks[2]], -1)
    return jnp.where(ctx == 1, turned, values)


def add_bf16(left, right):
    return (left.astype(F32) + right.astype(F32)).astype(BF16)


def tensor_pieces(value):
    count = lax.axis_size("tensor")
    pieces = [value]
    for step in range(1, count):
        pairs = [(n, (n + step) % count) for n in range(count)]
        pieces.append(lax.ppermute(value, "tensor", pairs))
    return pieces


def rows_layout(value):
    return with_layout_constraint(value, Layout(tuple(range(value.ndim))))


def per_device(inputs, cotangent, w_qkv, w_out, w_up, w_down, norm_gains, norm_shifts):
    section = lax.axis_index("section")
    tensors = lax.axis_size("tensor")
    contexts = lax.axis_size("context")
    ctx = lax.axis_index("context")
    micro, _, span, width = inputs.shape
    assert micro == tensors and lax.axis_size("section") == 2 and tensors % 2 == 0
    half_span = span // 2
    count = tensors * span
    own_rows = w_qkv.shape[2]
    share_heads = w_qkv.shape[3] // HEAD_DIM
    half_heads = share_heads * tensors // 2
    heads = -(-half_heads // contexts)
    fast = square() and contexts * 2 == tensors
    first = share_heads - share_heads // 2
    parts = [n for n in (first, share_heads - first) if n] if fast else [1] * heads
    qkv_cols, out_cols, hidden_cols = w_qkv.shape[3] * 3, w_out.shape[1], w_up.shape[2]


    held = {}

    def stage(compute, *jobs):
        made = {name: job() for name, job in jobs}
        leaves, shape = jax.tree.flatten((compute(), made))
        if not leaves:
            return ()
        result, made = jax.tree.unflatten(shape, lax.optimization_barrier(leaves))
        for name, value in made.items():
            held.update(value if isinstance(value, dict) else {name: value})
        return result


    def head_columns(share, each):
        cut, start = [], 0
        for size in parts:
            cut.append(share[:, start:start + size * each])
            start += size * each
        return cut

    def relative_columns(half, each):
        own, far = take(half, ctx), take(half, 1 - ctx)
        cut = []
        for pair in zip(head_columns(own, each), head_columns(far, each)):
            cut.extend(pair)
        return jnp.concatenate(cut, 1)

    def flipped_columns(value, each):
        cut, start = [], 0
        for size in parts:
            middle, end = start + size * each, start + 2 * size * each
            cut += [value[:, middle:end], value[:, start:middle]]
            start = end
        return cut

    def flipped(value):
        edge = 2 * qkv_cols
        return jnp.concatenate(
            flipped_columns(value[:, :edge], 3 * HEAD_DIM)
            + flipped_columns(value[:, edge:], HEAD_DIM), 1)

    def shares_of_columns(value, each):
        own, far, start = [], [], 0
        for size in parts:
            middle, end = start + size * each, start + 2 * size * each
            own.append(value[:, start:middle])
            far.append(value[:, middle:end])
            start = end
        return paired(jnp.concatenate(own, 1)[None], jnp.concatenate(far, 1)[None], ctx, 0)


    qkv_share = w_qkv[0].reshape(3, own_rows, share_heads, HEAD_DIM).transpose(1, 2, 0, 3)
    if fast:
        pieces, place = [], 0
        for size in parts:
            piece = qkv_share[:, place:place + size].transpose(0, 2, 1, 3)
            pieces.append(piece.reshape(own_rows, -1))
            place += size
    else:
        pieces = [qkv_share.reshape(own_rows, -1)]
    attn_share = jnp.concatenate(pieces + [w_out[0].T], 1)

    def over_tensor(share):
        gathered = lax.all_gather(share, "tensor")
        split = gathered.reshape((2, tensors // 2) + share.shape)
        return take(split, section), take(split, 1 - section)

    def joined_columns(value):
        return value.transpose(1, 0, 2).reshape(own_rows, -1)

    def attn_layer(layer):
        kept, came = held["attn_kept"], held["attn_came"]
        half = jnp.where(section == layer, kept, came)
        split = half[:, :, :qkv_cols], half[:, :, qkv_cols:]
        if fast:
            return rows_layout(jnp.concatenate([
                relative_columns(split[0], 3 * HEAD_DIM), relative_columns(split[1], HEAD_DIM)], 1))
        return jnp.concatenate([joined_columns(piece) for piece in split], 1)

    def hidden_layer(name, layer):
        half = jnp.where(section == layer, held[name + "_kept"], held[name + "_came"])
        return rows_layout(joined_columns(half))

    def near_rows(own, flip=False):
        if not square():
            return own
        return swap(flipped(own) if flip else own, "context")

    def far_rows(rows):
        return swap(rows, "dp") if square() else rows

    def all_rows(own, near, own_far, near_far):
        if not square():
            return lax.all_gather(own, ("dp", "context"), axis=0, tiled=True)
        return jnp.concatenate([own, near, own_far, near_far])

    def reduce_dp(partial, block):
        if not square():
            return partial
        rows = partial.shape[0] // 4
        kept = partial[block * rows:(block + 1) * rows]
        return add_bf16(kept, swap(partial[(block + 2) * rows:(block + 3) * rows], "dp"))

    def reduce_ctx(kept, sent, flip=False):
        if not square():
            return lax.psum_scatter(sent, ("dp", "context"), scatter_dimension=0, tiled=True)
        return add_bf16(kept, swap(flipped(sent) if flip else sent, "context"))

    def both_halves(partial):
        return partial + swap(partial.astype(BF16), "section").astype(F32)


    def split_heads(projected, each):
        if fast:
            result, start = [], 0
            for size in parts:
                middle, end = start + size * each, start + 2 * size * each
                result.append([projected[:, start:middle], projected[:, middle:end]])
                start = end
            return result
        shaped = projected.reshape(count, half_heads, -1)
        shaped = jnp.pad(shaped, ((0, 0), (0, contexts * heads - half_heads), (0, 0)))
        shaped = shaped.reshape(count, contexts, heads, -1)
        return [[take(shaped[:, :, n], lax.bitwise_xor(ctx, step), 1) for step in range(contexts)]
                for n in range(heads)]

    def join_heads(parts_list):
        if fast:
            return jnp.concatenate([block for blocks in parts_list for block in blocks], 1)
        shaped = jnp.stack([in_order(blocks, ctx) for blocks in parts_list])
        shaped = shaped.transpose(2, 1, 0, 3).reshape(count, contexts * heads, -1)
        return shaped[:, :half_heads].reshape(count, -1)

    def exchanged(blocks):
        moved = [blocks[0]]
        for step in range(1, contexts):
            pairs = [(n, n ^ step) for n in range(contexts)]
            moved.append(lax.ppermute(blocks[step], "context", pairs))
        return moved

    def to_all_rows(blocks):
        moved = in_order(exchanged(blocks), ctx)
        return moved.reshape(contexts * count, -1)

    def to_own_rows(full):
        shaped = full.reshape(contexts, count, -1)
        return exchanged([take(shaped, lax.bitwise_xor(ctx, step)) for step in range(contexts)])


    norms_share = jnp.concatenate([norm_gains[0], norm_shifts[0]])
    if square():
        norms_near = jnp.concatenate([norms_share, swap(norms_share, "context")], 1)
        norms_own = jnp.concatenate([norms_near, swap(norms_near, "dp")], 1)
    else:
        norms_own = lax.all_gather(norms_share, ("dp", "context"), axis=1, tiled=True)
    norms_other = swap(norms_own, "section")

    def norms_of(layer):
        chosen = jnp.where(section == layer, norms_own, norms_other).astype(F32)
        return chosen[:2], chosen[2:]

    last = len(parts) - 1

    def forward(layer_in, norms, finish_attn, finish_up, finish_down, jobs):
        gains, shifts = norms

        def begin():
            residual = layer_in.astype(F32)
            return residual, normed(residual, gains[0], shifts[0]).astype(BF16)

        residual, normed_a = stage(begin, *jobs[0])
        qkv, out = attn = finish_attn()

        def spread():
            projected = dot(normed_a, qkv, ((1,), (0,))).astype(BF16)
            blocks = split_heads(projected, 3 * HEAD_DIM)
            return [to_all_rows(blocks[0])], blocks[1:]

        packed, blocks = stage(spread, *jobs[1])
        attended, mixed_own = [], []
        for number in range(last + 1):
            if number:
                mixed_own.append(to_own_rows(attended[number - 1][0]))

            def work():
                done = attend(packed[number], parts[number])
                more = [to_all_rows(blocks[number])] if number < last else []
                return done, more
            done, more = stage(work, *(jobs[number + 2] if number < 2 else []))
            attended.append(done)
            packed += more
        if last == 0:
            stage(lambda: (), *jobs[3])
        mixed_own = stage(lambda: mixed_own + [to_own_rows(attended[-1][0])], *jobs[4])
        mixture = join_heads(mixed_own)
        hidden = stage(
            lambda: residual + both_halves(dot(mixture, out, ((1,), (1,)))), *jobs[5])
        normed_b = stage(
            lambda: normed(hidden, gains[1], shifts[1]).astype(BF16), *jobs[6])
        up = finish_up()

        def expand():
            pre_act = dot(normed_b, up, ((1,), (0,)))
            return pre_act, jax.nn.gelu(pre_act).astype(BF16)

        pre_act, activated = stage(expand, *jobs[7])
        down = finish_down()
        layer_out = stage(
            lambda: (hidden + both_halves(dot(activated, down, ((1,), (1,))))).astype(BF16),
            *jobs[8])
        saved = (residual, normed_a, packed, attended, mixture, hidden, normed_b, pre_act)
        return layer_out, saved, attn + (up, down)

    def backward(tag, grad_branch, saved, norms, weights, jobs):
        gains, shifts = norms
        qkv, out, up, down = weights
        residual, normed_a, packed, attended, mixture, hidden, normed_b, pre_act = saved
        grad_in = grad_branch.astype(F32)
        down_name, up_name, attn_name = (tag + name for name in ("down", "up", "attn"))

        def first():
            grad_act = dot(grad_branch, down, ((1,), (0,)))
            activated, gelu_back = jax.vjp(jax.nn.gelu, pre_act)
            grad_pre = gelu_back(grad_act)[0].astype(BF16)
            grad_down = dot(grad_branch, activated.astype(BF16), ((0,), (0,))).astype(BF16)
            return grad_pre, grad_down

        grad_pre, grad_down = stage(first, *jobs[0])

        def second():
            grad_second = both_halves(dot(grad_pre, up, ((1,), (1,))))
            return grad_second, dot(normed_b, grad_pre, ((0,), (0,))).astype(BF16)

        grad_second, grad_up = stage(second, *jobs[1])

        def third():
            _, second_back = jax.vjp(normed, hidden, gains[1], shifts[1])
            grad_hidden_norm, gain_later, shift_later = second_back(grad_second)
            grad_hidden = grad_in + grad_hidden_norm
            grad_attn = grad_hidden.astype(BF16)
            grad_mixture = dot(grad_attn, out, ((1,), (0,))).astype(BF16)
            return grad_hidden, grad_attn, split_heads(grad_mixture, HEAD_DIM), gain_later, shift_later

        late = hold(grad_down, grad_second)
        grad_hidden, grad_attn, blocks, gain_later, shift_later = stage(
            third, (down_name + "1", lambda: reduce_dp(late, 1)), *jobs[2])
        after = hold(grad_down, grad_attn)
        grad_mixed, blocks = stage(
            lambda: ([to_all_rows(blocks[0])], blocks[1:]),
            (down_name + "0", lambda: reduce_dp(after, 0)), *jobs[3])
        grad_packed, returned, grad_out = [], [], None
        held_up = hold(grad_up, grad_mixed[0])

        def reduce_up():
            sent = reduce_dp(held_up, 1)
            return reduce_ctx(reduce_dp(held_up, 0), sent)

        for number in range(last + 1):
            if number:
                returned.append(to_own_rows(grad_packed[number - 1]))

            def work():
                done = attend_back(packed[number], grad_mixed[number], attended[number][0],
                                   attended[number][1], parts[number])
                more = [to_all_rows(blocks[number])] if number < last else []
                extra = grad_out
                if number == 0:
                    extra = dot(grad_attn, mixture, ((0,), (0,))).astype(BF16)
                return done, more, extra
            beside = jobs[5] if number == 1 else []
            if number == 0:
                beside = [
                    (down_name, lambda: reduce_ctx(held[down_name + "0"], held[down_name + "1"])),
                    (up_name, reduce_up)] + list(jobs[4])
            done, more, grad_out = stage(work, *beside)
            grad_packed.append(done)
            grad_mixed += more
        if last == 0:
            stage(lambda: (), *jobs[5])
        returned = stage(lambda: returned + [to_own_rows(grad_packed[-1])], *jobs[6])
        grad_proj = join_heads(returned)

        def fourth():
            grad_first = both_halves(dot(grad_proj, qkv, ((1,), (1,))))
            grad_qkv = dot(normed_a, grad_proj, ((0,), (0,))).astype(BF16)
            return grad_first, jnp.concatenate([grad_qkv, grad_out], 1)

        grad_first, grad_heads = stage(fourth, *jobs[7])

        def fifth():
            _, first_back = jax.vjp(normed, residual, gains[0], shifts[0])
            grad_input_norm, gain_early, shift_early = first_back(grad_first)
            grad_input = (grad_hidden + grad_input_norm).astype(BF16)
            grad_norms = jnp.stack([gain_early, gain_later, shift_early, shift_later])
            return grad_input, grad_norms

        heads_late = hold(grad_heads, grad_first)
        grad_input, grad_norms = stage(
            fifth, (attn_name + "1", lambda: reduce_dp(heads_late, 1)), *jobs[8])
        return grad_input, grad_norms, grad_heads

    def sum_norms(lower, upper):
        chosen = jnp.where(section == 0, lower, upper)
        if not square():
            total = lax.psum(chosen, ("dp", "context", "tensor"))
            place = lax.axis_index("dp") * contexts + ctx
            return lax.dynamic_slice_in_dim(total, place * own_rows, own_rows, 1)
        half = width // 2
        total = chosen[:, :half] + swap(chosen[:, half:], "dp")
        total = total[:, :own_rows] + swap(total[:, own_rows:], "context")
        return functools.reduce(jnp.add, tensor_pieces(total))

    def entry_half(value):
        half = take(value.reshape(micro, 2, half_span, width), section, 1)
        return spread_tensor(reorder(half))

    def entry_rows(mine):
        other = swap(mine, "section")
        return paired(mine[:, None], other[:, None], section, 1).reshape(count, width)

    def exit_rows(value):
        half = take(value.reshape(tensors, 2, half_span, width), section, 1)
        return spread_tensor(reorder(half))

    def place_layers(lower, upper):
        keep = jnp.where(section == 0, lower, upper)
        came = swap(jnp.where(section == 0, upper, lower), "section")
        whole = paired(keep[:, None], came[:, None], section, 1)
        return whole.reshape(1, micro, 1, span, width)

    def own_layer(lower, upper):
        keep = jnp.where(section == 0, lower, upper)
        came = swap(jnp.where(section == 0, upper, lower), "section")
        return paired(keep, came, section, 0)

    def reduce_tensor(blocks):
        return lax.psum_scatter(blocks, "tensor", scatter_dimension=0)

    def hidden_shares(value):
        return value.reshape(own_rows, tensors // 2, hidden_cols).transpose(1, 0, 2)

    def attn_shares(value):
        edge = value.shape[1] * qkv_cols // (qkv_cols + out_cols)
        if fast:
            cut = [shares_of_columns(value[:, :edge], 3 * HEAD_DIM),
                   shares_of_columns(value[:, edge:], HEAD_DIM)]
        else:
            cut = [piece.reshape(own_rows, tensors // 2, -1).transpose(1, 0, 2)
                   for piece in (value[:, :edge], value[:, edge:])]
        return jnp.concatenate(cut, 2)


    attn_both = stage(lambda: over_tensor(attn_share))
    ffn_share = jnp.concatenate([w_up[0], rows_layout(w_down[0].T)], 1)
    norms_zero, norms_one = norms_of(0), norms_of(1)

    def start():
        held["attn_kept"], held["attn_came"] = attn_both[0], swap(attn_both[1], "section")
        own = attn_layer(0)
        near = near_rows(own, True)
        full = all_rows(own, near, far_rows(own), far_rows(near))
        return entry_half(hold(inputs, attn_both)), full

    entry, attn_zero = stage(start)
    entries = entry_rows(entry)
    cut_at = qkv_cols * tensors // 2

    def cut(full):
        return full[:, :cut_at], full[:, cut_at:]

    def ffn_begin():
        half, other = held["ffn"]
        other = swap(other, "section")
        made = {}
        for layer in range(2):
            mine = jnp.where(section == layer, half, other)
            made[f"up{layer}_own"] = rows_layout(joined_columns(mine[:, :, :hidden_cols]))
            made[f"down{layer}_own"] = rows_layout(joined_columns(mine[:, :, hidden_cols:]))
        made["up0_near"] = near_rows(made["up0_own"])
        made["up0_own_far"] = far_rows(made["up0_own"])
        return made

    def near_job(name):
        return (name + "_near", lambda: near_rows(held[name + "_own"], name == "attn1"))

    def far_job(name, which):
        return (f"{name}_{which}_far", lambda: far_rows(held[f"{name}_{which}"]))

    def finish(name):
        return lambda: all_rows(*[held[f"{name}_{end}"]
                                  for end in ("own", "near", "own_far", "near_far")])

    out_zero, saved_zero, weights_zero = forward(
        entries, norms_zero, lambda: cut(attn_zero), finish("up0"), finish("down0"), [
            [],
            [("ffn", lambda: over_tensor(hold(ffn_share, attn_both)))],
            [("begin", ffn_begin)],
            [far_job("up0", "near"), ("attn1_own", lambda: attn_layer(1))],
            [far_job("down0", "own")],
            [],
            [near_job("down0"), far_job("attn1", "own")],
            [far_job("down0", "near"), near_job("attn1")],
            [],
        ])
    out_one, saved_one, weights_one = forward(
        out_zero, norms_one, lambda: cut(finish("attn1")()), finish("up1"), finish("down1"), [
            [far_job("attn1", "near")],
            [far_job("up1", "own")],
            [near_job("up1"), far_job("down1", "own"), ("exit0", lambda: exit_rows(out_zero))],
            [far_job("up1", "near")],
            [("top", lambda: entry_half(hold(cotangent, held["up1_near"])))],
            [],
            [near_job("down1")],
            [far_job("down1", "near")],
            [],
        ])
    top_grad = entry_rows(held["top"])
    grad_one, norm_sum_one, grad_heads_one = backward(
        "one_", top_grad, saved_one, norms_one, weights_one,
        [[], [], [], [], [("exit1", lambda: exit_rows(out_one))], [], [], [], []])
    layer_outputs = place_layers(held["exit0"], held["exit1"])
    grad_zero, norm_sum_zero, grad_heads_zero = backward(
        "zero_", grad_one, saved_zero, norms_zero, weights_zero, [
            [("one_attn0", lambda: reduce_dp(grad_heads_one, 0))],
            [],
            [("one_attn", lambda: reduce_ctx(held["one_attn0"], held["one_attn1"], True))],
            [],
            [("back1", lambda: exit_rows(grad_one))],
            [("down_all", lambda: own_layer(hidden_shares(held["zero_down"]),
                                            hidden_shares(held["one_down"]))),
             ("up_all", lambda: own_layer(hidden_shares(held["zero_up"]),
                                          hidden_shares(held["one_up"])))],
            [],
            [("down_sum", lambda: reduce_tensor(held["down_all"]))],
            [],
        ])

    def finish_up():
        attn_kept = reduce_dp(grad_heads_zero, 0)
        back_zero = exit_rows(grad_zero)
        attn_zero_sum = reduce_ctx(attn_kept, held["zero_attn1"], True)
        attn_all = own_layer(attn_shares(attn_zero_sum), attn_shares(held["one_attn"]))
        return (back_zero, attn_all, reduce_tensor(held["up_all"]),
                sum_norms(norm_sum_zero, norm_sum_one))

    back_zero, attn_all, grad_up, norm_sums = finish_up()
    boundary_grads = place_layers(back_zero, held["back1"])
    attn_total = reduce_tensor(attn_all).astype(F32)
    grad_up = grad_up.astype(F32)
    grad_down = held["down_sum"].astype(F32)
    grad_qkv, grad_out = attn_total[:, :qkv_cols], attn_total[:, qkv_cols:]
    cut_list, place = [], 0
    for size in (parts if fast else [1] * share_heads):
        columns = size * 3 * HEAD_DIM
        cut_list.append(grad_qkv[:, place:place + columns].reshape(own_rows, 3, size, HEAD_DIM))
        place += columns
    grad_qkv = jnp.concatenate(cut_list, 2).transpose(1, 0, 2, 3).reshape(3, own_rows, -1)
    return (
        layer_outputs,
        boundary_grads,
        grad_qkv[None],
        grad_out.T[None],
        grad_up[None],
        grad_down.T[None],
        norm_sums[:2][None],
        norm_sums[2:][None],
    )


def solution(mesh):
    in_specs = (
        P(None, "dp", ("context", "tensor"), None),
        P(None, "dp", ("context", "tensor"), None),
        P("section", None, ("dp", "context"), "tensor"),
        P("section", "tensor", ("dp", "context")),
        P("section", ("dp", "context"), "tensor"),
        P("section", "tensor", ("dp", "context")),
        P("section", None, ("dp", "context")),
        P("section", None, ("dp", "context")),
    )
    out_specs = (
        P("section", None, "dp", ("context", "tensor"), None),
        P("section", None, "dp", ("context", "tensor"), None),
        P("section", None, ("dp", "context"), "tensor"),
        P("section", "tensor", ("dp", "context")),
        P("section", ("dp", "context"), "tensor"),
        P("section", "tensor", ("dp", "context")),
        P("section", None, ("dp", "context")),
        P("section", None, ("dp", "context")),
    )
    return jax.shard_map(
        per_device, mesh=mesh, in_specs=in_specs, out_specs=out_specs, check_vma=False
    )
```

time: 1340 us -> 851 us (0.64); the launches traced: 1320 us -> 846 us
  local copies, waits for them, and re-layouts: 447 us -> 105 us
  starting transfers between devices: 327 us -> 94 us
  waiting for transfers between devices: 231 us -> 309 us
  other arithmetic: 92.7 us -> 120 us
    ppermute x114 -> x19, starting transfers between devices: 270 us -> 19.8 us  [the longest x16 17.6 us: exchanged(): moved.append(lax.ppermute(blocks[step], 'context', pairs))]
    dynamic_update_slice x143 -> x0, local copies, waits for them, and re-layouts: 195 us -> none  [put(): return lax.dynamic_update_slice(buffer, value.reshape(shape), starts)]
    another operation x66 -> x4, local copies, waits for them, and re-layouts: 68.4 us -> 0.02 us  [fifth(): grad_norms = jnp.stack([gain_early, gain_later, shift_early, shift_later])]
    ppermute x114 -> x19, waiting for transfers between devices: 126 us -> 65.3 us  [the longest x16 63 us: exchanged(): moved.append(lax.ppermute(blocks[step], 'context', pairs))]
    reshape x55 -> x4, local copies, waits for them, and re-layouts: 57.7 us -> 0.01 us  [normed(): return center * lax.rsqrt(spread + EPS) * gain_row + shift_row]
    ppermute x82 -> x58, waiting for transfers between devices: 105 us -> 162 us  [swap(): return lax.ppermute(value, axis, [(0, 1), (1, 0)])]
    all_gather x0 -> x2, waiting for transfers between devices: none -> 55.1 us  [over_tensor(): gathered = lax.all_gather(share, 'tensor')]
    dynamic_slice x29 -> x3, local copies, waits for them, and re-layouts: 37.4 us -> 5.22 us  [take(): return lax.dynamic_index_in_dim(buffer, index, axis, keepdims=False)]
  transfers between devices with their start and end apart: 196 -> 88, of which waited for: 62 -> 41; matrix products, arithmetic and copies ran while one was open for 43% -> 29% of each run, Pallas kernels for 7% -> 13%
where the time goes in v2:
time: 851 us; the launch traced here: 846 us
  waiting for transfers between devices  309 us (36%)
  other arithmetic  120 us (14%)
  Pallas kernels  111 us (13%)
  local copies, waits for them, and re-layouts  105 us (12%)
  starting transfers between devices  94 us (11%)
  matrix products  90.2 us (11%)
  between operations  16.8 us (2%)
    ppermute x58, waiting for transfers between devices, swap(): return lax.ppermute(value, axis, [(0, 1), (1, 0)])  162 us
    dot_general x24, matrix products, dot(): lax.dot_general(left, right, ((contract[0], contract[1]), ((), ())), pref...  90.2 us
    pallas_call x4, Pallas kernels, attend_back(): pl.pallas_call(functools.partial(attend_back_kernel, block, heads), grid=...  64.1 us
    ppermute x16, waiting for transfers between devices, exchanged(): moved.append(lax.ppermute(blocks[step], 'context', pairs))  63 us
    all_gather x2, waiting for transfers between devices, over_tensor(): gathered = lax.all_gather(share, 'tensor')  55.1 us
    pallas_call x4, Pallas kernels, attend(): pl.pallas_call(functools.partial(attend_kernel, block, heads), grid=(leng...  46.9 us
    ppermute x58, starting transfers between devices, swap(): return lax.ppermute(value, axis, [(0, 1), (1, 0)])  46.5 us
    unnamed x264, local copies, waits for them, and re-layouts  35.4 us
  transfers between devices with their start and end apart: 88, of which 41 were waited for; matrix products, arithmetic and copies ran while one was open for 29% of the time, Pallas kernels for 13%

profile of v2, /device:TPU:0, one launch (start us, length us, event | category | flops | bytes accessed | tf_op | source)
XLA Modules:
  0.0 846.0 jit_solution(18156305871814671699)
XLA Ops:
  10.2 33.3 %all-gather.5.cloned.1.call-done = bf16[768,768]{1,0:T(8,128)(2,1)} async-done(((bf16[192,768]{1,0:T(8,128)(2,1)}), bf16[768,768]{1,0:T(8,128)(2,1)}) %all-gather.5.cloned.1.call-update) | async-done | bytes 1179664 | tf_op jit(solution)/shard_map/all_gather | solution.py:328
  53.0 3.5 all-to-all-start
  58.9 7.0 collective-permute-done.1
  68.9 4.7 collective-permute-done.2
  73.6 11.9 %collective-permute-done.3 = bf16[192,1536]{1,0:T(8,128)(2,1)S(1)} collective-permute-done((bf16[192,1536]{1,0:T(8,128)(2,1)S(1)}, bf16[192,1536]{1,0:T(8,128)(2,1)S(1)}, u32[]{:S(2)}, u32[]{:S(2)}) %collective-permute-start.3) | collective-permute-done | bytes 589856 | tf_op jit(solution)/shard_map/ppermute | solution.py:182
  102.8 16.6 %collective-permute-done.8 = bf16[1024,384]{1,0:T(8,128)(2,1)S(1)} collective-permute-done((bf16[1024,384]{1,0:T(8,128)(2,1)S(1)}, bf16[1024,384]{1,0:T(8,128)(2,1)S(1)}, u32[]{:S(2)}, u32[]{:S(2)}) %collective-permute-start.8) | collective-permute-done | bytes 786464 | tf_op jit(solution)/shard_map/ppermute | solution.py:402
  120.9 21.8 %all-gather.7.cloned.1.call-done = bf16[768,1536]{1,0:T(8,128)(2,1)} async-done(((bf16[192,1536]{1,0:T(8,128)(2,1)}), bf16[768,1536]{1,0:T(8,128)(2,1)}) %all-gather.7.cloned.1.call-update) | async-done | bytes 2359312 | tf_op jit(solution)/shard_map/all_gather | solution.py:328
  157.6 15.7 %attend.4 = (bf16[2048,128]{1,0:T(8,128)(2,1)S(1)}, f32[2,1,2048]{2,1,0:T(1,128)S(1)}) custom-call(bf16[2048,384]{1,0:T(8,128)(2,1)S(1)} %bitcast.326, bf16[2048,384]{1,0:T(8,128)(2,1)S(1)} %bitcast.327), custom_call_target="tpu_custom_call" | custom-call | flops 2147483648 | bytes 3145728 | tf_op jit(solution)/shard_map/attend/pallas_call | solution.py:73
  180.9 10.5 %collective-permute-done.12 = bf16[192,1536]{1,0:T(8,128)(2,1)S(1)} collective-permute-done((bf16[192,1536]{1,0:T(8,128)(2,1)S(1)}, bf16[192,1536]{1,0:T(8,128)(2,1)S(1)}, u32[]{:S(2)}, u32[]{:S(2)}) %collective-permute-start.12) | collective-permute-done | bytes 589856 | tf_op jit(solution)/shard_map/ppermute | solution.py:182
  196.7 7.8 attend.5
  205.5 3.3 collective-permute-done.14
  209.6 5.5 collective-permute-done.13
  215.0 4.5 collective-permute-done.16
  219.5 4.6 fusion.109
  229.4 6.3 multiply_reduce_fusion.2
  243.9 5.7 fusion.21
  249.6 7.3 collective-permute-done.21
  257.0 2.6 fusion.110
  267.4 21.0 %collective-permute-done.23 = bf16[192,1536]{1,0:T(8,128)(2,1)S(1)} collective-permute-done((bf16[192,1536]{1,0:T(8,128)(2,1)S(1)}, bf16[192,1536]{1,0:T(8,128)(2,1)S(1)}, u32[]{:S(2)}, u32[]{:S(2)}) %collective-permute-start.23) | collective-permute-done | bytes 589856 | tf_op jit(solution)/shard_map/ppermute | solution.py:182
  294.1 4.2 all-to-all-start.1
  299.7 10.3 %collective-permute-done.24 = bf16[1024,384]{1,0:T(8,128)(2,1)S(1)} collective-permute-done((bf16[1024,384]{1,0:T(8,128)(2,1)S(1)}, bf16[1024,384]{1,0:T(8,128)(2,1)S(1)}, u32[]{:S(2)}, u32[]{:S(2)}) %collective-permute-start.24) | collective-permute-done | bytes 786464 | tf_op jit(solution)/shard_map/ppermute | solution.py:402
  314.2 15.5 %attend.6 = (bf16[2048,128]{1,0:T(8,128)(2,1)S(1)}, f32[2,1,2048]{2,1,0:T(1,128)S(1)}) custom-call(bf16[2048,384]{1,0:T(8,128)(2,1)S(1)} %bitcast.330, bf16[2048,384]{1,0:T(8,128)(2,1)S(1)} %bitcast.331), custom_call_target="tpu_custom_call" | custom-call | flops 2147483648 | bytes 3145728 | tf_op jit(solution)/shard_map/attend/pallas_call | solution.py:73
  331.8 5.2 collective-permute-done.28
  340.5 4.6 all-to-all-start.2
  350.1 7.8 attend.7
  363.5 4.0 collective-permute-done.29
  367.4 2.8 collective-permute-done.31
  370.2 4.6 fusion.111
  387.8 3.9 multiply_reduce_fusion.7
  401.0 3.5 fusion.29
  404.5 8.3 collective-permute-done.35
  412.9 3.2 convolution_convert_fusion.5
  416.1 8.3 fusion.6
  427.2 2.6 fusion.113
  430.4 4.0 convolution_convert_fusion.4
  446.1 4.1 collective-permute-done.37
  455.9 5.0 all-to-all-start.3
  472.6 2.9 convolution_convert_fusion.11
  479.0 8.4 collective-permute-done.44
  490.3 21.7 %attend_back.4 = bf16[2048,384]{1,0:T(8,128)(2,1)S(1)} custom-call(bf16[2048,384]{1,0:T(8,128)(2,1)S(1)} %bitcast.332, bf16[2048,384]{1,0:T(8,128)(2,1)S(1)} %bitcast.333, bf16[2048,128]{1,0:T(8,128)(2,1)S(1)} %bitcast.352, bf16[2048,128]{1,0:T(8,128)(2,1)S(1)} %copy-done.11, f32[2,1,2048]{2,1,0:T(1,128)S(1)} %get-tuple-element.240.log_ref), custom_call_target="tpu_custom_call" | custom-call | flops 5368709120 | bytes 6291456 | tf_op jit(solution)/shard_map/attend_back/pallas_call | solution.py:155
  519.0 10.4 %attend_back.5 = bf16[2048,192]{1,0:T(8,128)(2,1)S(1)} custom-call(bf16[2048,192]{1,0:T(8,128)(2,1)S(1)} %bitcast.342, bf16[2048,192]{1,0:T(8,128)(2,1)S(1)} %bitcast.343, bf16[2048,64]{1,0:T(8,128)(2,1)S(1)} %bitcast.351, bf16[2048,64]{1,0:T(8,128)(2,1)S(1)} %copy-done.13, f32[1,1,2048]{2,1,0:T(1,128)S(1)} %get-tuple-element.252.log_ref), custom_call_target="tpu_custom_call" | custom-call | flops 2684354560 | bytes 3145728 | tf_op jit(solution)/shard_map/attend_back/pallas_call | solution.py:155
  531.1 11.1 %collective-permute-done.48 = bf16[1024,192]{1,0:T(8,128)(2,1)S(1)} collective-permute-done((bf16[1024,192]{1,0:T(8,128)(2,1)S(1)}, bf16[1024,192]{1,0:T(8,128)(2,1)S(1)}, u32[]{:S(2)}, u32[]{:S(2)}) %collective-permute-start.48) | collective-permute-done | bytes 393248 | tf_op jit(solution)/shard_map/ppermute | solution.py:402
  542.2 5.2 concatenate.374
  547.4 4.6 fusion.114
  564.3 12.3 %collective-permute-done.50 = bf16[192,1536]{1,0:T(8,128)(2,1)S(1)} collective-permute-done((bf16[192,1536]{1,0:T(8,128)(2,1)S(1)}, bf16[192,1536]{1,0:T(8,128)(2,1)S(1)}, u32[]{:S(2)}, u32[]{:S(2)}) %collective-permute-start.50) | collective-permute-done | bytes 589856 | tf_op jit(solution)/shard_map/ppermute | solution.py:182
  582.0 8.6 %fusion.13 = bf16[1024,1536]{1,0:T(8,128)(2,1)S(1)} fusion(f32[1024,1536]{1,0:T(8,128)} %get-tuple-element.266, bf16[1024,768]{1,0:T(8,128)(2,1)S(1)} %add_convert_fusion.1, bf16[768,1536]{1,0:T(8,128)(2,1)} %copy-done.94), kind=kOutput, calls=%fused_computation.19 | convolution fusion | flops 2447376384 | bytes 13369344 | tf_op jit(solution)/shard_map/dot_general | solution.py:28
  590.5 5.8 convolution_convert_fusion.3
  602.8 4.0 convolution_convert_fusion.2
  619.4 9.7 %collective-permute-done.54 = bf16[192,1536]{1,0:T(8,128)(2,1)S(1)} collective-permute-done((bf16[192,1536]{1,0:T(8,128)(2,1)S(1)}, bf16[192,1536]{1,0:T(8,128)(2,1)S(1)}, u32[]{:S(2)}, u32[]{:S(2)}) %collective-permute-start.54) | collective-permute-done | bytes 589856 | tf_op jit(solution)/shard_map/ppermute | solution.py:182
  633.8 4.8 all-to-all-start.4
  641.2 4.9 collective-permute-done.56
  656.8 9.1 %collective-permute-done.60 = bf16[192,1536]{1,0:T(8,128)(2,1)S(1)} collective-permute-done((bf16[192,1536]{1,0:T(8,128)(2,1)S(1)}, bf16[192,1536]{1,0:T(8,128)(2,1)S(1)}, u32[]{:S(2)}, u32[]{:S(2)}) %collective-permute-start.60) | collective-permute-done | bytes 589856 | tf_op jit(solution)/shard_map/ppermute | solution.py:182
  669.1 21.6 %attend_back.6 = bf16[2048,384]{1,0:T(8,128)(2,1)S(1)} custom-call(bf16[2048,384]{1,0:T(8,128)(2,1)S(1)} %bitcast.328, bf16[2048,384]{1,0:T(8,128)(2,1)S(1)} %bitcast.329, bf16[2048,128]{1,0:T(8,128)(2,1)S(1)} %bitcast.353, bf16[2048,128]{1,0:T(8,128)(2,1)S(1)} %copy-done.7, f32[2,1,2048]{2,1,0:T(1,128)S(1)} %get-tuple-element.281.log_ref), custom_call_target="tpu_custom_call" | custom-call | flops 5368709120 | bytes 6291456 | tf_op jit(solution)/shard_map/attend_back/pallas_call | solution.py:155
  698.4 10.4 %attend_back.7 = bf16[2048,192]{1,0:T(8,128)(2,1)S(1)} custom-call(bf16[2048,192]{1,0:T(8,128)(2,1)S(1)} %bitcast.338, bf16[2048,192]{1,0:T(8,128)(2,1)S(1)} %bitcast.339, bf16[2048,64]{1,0:T(8,128)(2,1)S(1)} %bitcast.350, bf16[2048,64]{1,0:T(8,128)(2,1)S(1)} %copy-done.9, f32[1,1,2048]{2,1,0:T(1,128)S(1)} %get-tuple-element.290.log_ref), custom_call_target="tpu_custom_call" | custom-call | flops 2684354560 | bytes 3145728 | tf_op jit(solution)/shard_map/attend_back/pallas_call | solution.py:155
  718.1 10.4 %collective-permute-done.65 = bf16[1024,192]{1,0:T(8,128)(2,1)S(1)} collective-permute-done((bf16[1024,192]{1,0:T(8,128)(2,1)}, bf16[1024,192]{1,0:T(8,128)(2,1)S(1)}, u32[]{:S(2)}, u32[]{:S(2)}) %collective-permute-start.65) | collective-permute-done | bytes 393248 | tf_op jit(solution)/shard_map/ppermute | solution.py:402
  728.5 3.4 concatenate.383
  731.9 4.6 fusion.116
  745.4 3.7 multiply_reduce_fusion
  755.7 12.4 %collective-permute-done.67 = bf16[192,1536]{1,0:T(8,128)(2,1)S(1)} collective-permute-done((bf16[192,1536]{1,0:T(8,128)(2,1)S(1)}, bf16[192,1536]{1,0:T(8,128)(2,1)S(1)}, u32[]{:S(2)}, u32[]{:S(2)}) %collective-permute-start.67) | collective-permute-done | bytes 589856 | tf_op jit(solution)/shard_map/ppermute | solution.py:182
  772.9 6.6 collective-permute-done.69
  779.5 3.0 collective-permute-done.70
  787.6 4.6 all-to-all-start.5
  800.8 17.3 %all-to-all-done.5 = bf16[4,128,768]{2,1,0:T(8,128)(2,1)S(1)} async-done(((bf16[4,128,768]{2,1,0:T(8,128)(2,1)}), bf16[4,128,768]{2,1,0:T(8,128)(2,1)S(1)}, u32[]{:S(2)}, u32[]{:S(2)}) %all-to-all-start.5) | async-done | bytes 786464 | tf_op jit(solution)/shard_map/all_to_all | solution.py:210
  828.8 7.1 reduce-scatter.6.cloned.1.call-done
  (689 shorter events, 305.4 us)
Async XLA Ops:
  7.2 36.4 %all-gather.5.cloned.1.call-start = ((), (), s32[]{:S(2)}) async-start(), calls=%async_computation.12 | async-start | bytes 1474560 | tf_op jit(solution)/shard_map/all_gather | solution.py:328
  49.9 15.9 %collective-permute-start.1 = (bf16[192,1536]{1,0:T(8,128)(2,1)}, bf16[192,1536]{1,0:T(8,128)(2,1)S(1)}, u32[]{:S(2)}, u32[]{:S(2)}) collective-permute-start(bf16[192,1536]{1,0:T(8,128)(2,1)} %concatenate.344), channel_id=1, source_target_pairs={{0,4},{4,0},{1,5},{5,1},{2,6},{6,2},{3,7},{7,3},{8,12},{12,8},{9,1... | collective-permute-start | bytes 1769480 | tf_op jit(solution)/shard_map/ppermute | solution.py:182
  53.0 34.1 %all-to-all-start = ((bf16[4,128,768]{2,1,0:T(8,128)(2,1)}), bf16[4,128,768]{2,1,0:T(8,128)(2,1)S(1)}, u32[]{:S(2)}, u32[]{:S(2)}) async-start(bf16[4,128,768]{2,1,0:T(8,128)(2,1)} %maximum_select_fusion.1), calls=%async_computation | async-start | bytes 1572864 | tf_op jit(solution)/shard_map/all_to_all | solution.py:210
  56.5 86.3 %all-gather.7.cloned.1.call-start = ((), (), s32[]{:S(2)}) async-start(), calls=%async_computation.13 | async-start | bytes 2949120 | tf_op jit(solution)/shard_map/all_gather | solution.py:328
  57.3 16.2 %collective-permute-start.2 = (bf16[192,1536]{1,0:T(8,128)(2,1)S(1)}, bf16[192,1536]{1,0:T(8,128)(2,1)S(1)}, u32[]{:S(2)}, u32[]{:S(2)}) collective-permute-start(bf16[192,1536]{1,0:T(8,128)(2,1)S(1)} %concatenate.343), channel_id=1, source_target_pairs={{0,8},{8,0},{1,9},{9,1},{2,10},{10,2},{3,11},{11,3},{4,12},{12,4},... | collective-permute-start | bytes 1769480 | tf_op jit(solution)/shard_map/ppermute | solution.py:182
  65.8 19.6 %collective-permute-start.3 = (bf16[192,1536]{1,0:T(8,128)(2,1)S(1)}, bf16[192,1536]{1,0:T(8,128)(2,1)S(1)}, u32[]{:S(2)}, u32[]{:S(2)}) collective-permute-start(bf16[192,1536]{1,0:T(8,128)(2,1)S(1)} %collective-permute-done.1), channel_id=1, source_target_pairs={{0,8},{8,0},{1,9},{9,1},{2,10},{10,2},{3,11},{11,3},{4,12},{12,4},... | collective-permute-start | bytes 1769480 | tf_op jit(solution)/shard_map/ppermute | solution.py:182
  67.4 19.7 %collective-permute-start.5 = (bf16[4,192]{1,0:T(4,128)(2,1)S(1)}, bf16[4,192]{1,0:T(4,128)(2,1)S(1)}, u32[]{:S(2)}, u32[]{:S(2)}) collective-permute-start(bf16[4,192]{1,0:T(4,128)(2,1)S(1)} %pad_maximum_fusion.38), channel_id=1, source_target_pairs={{0,4},{4,0},{1,5},{5,1},{2,6},{6,2},{3,7},{7,3},{8,12},{12,8},{9,1... | collective-permute-start | bytes 4616 | tf_op jit(solution)/shard_map/ppermute | solution.py:182
  99.7 19.7 %collective-permute-start.8 = (bf16[1024,384]{1,0:T(8,128)(2,1)S(1)}, bf16[1024,384]{1,0:T(8,128)(2,1)S(1)}, u32[]{:S(2)}, u32[]{:S(2)}) collective-permute-start(bf16[1024,384]{1,0:T(8,128)(2,1)S(1)} %slice.784), channel_id=1, source_target_pairs={{0,4},{4,0},{1,5},{5,1},{2,6},{6,2},{3,7},{7,3},{8,12},{12,8},{9,1... | collective-permute-start | bytes 2359304 | tf_op jit(solution)/shard_map/ppermute | solution.py:402
  147.9 25.4 %collective-permute-start.10 = (bf16[2,192,1536]{2,0,1:T(2,128)(2,1)}, bf16[2,192,1536]{2,0,1:T(2,128)(2,1)}, u32[]{:S(2)}, u32[]{:S(2)}) collective-permute-start(bf16[2,192,1536]{2,0,1:T(2,128)(2,1)} %bitcast.316), channel_id=1, source_target_pairs={{0,16},{16,0},{1,17},{17,1},{2,18},{18,2},{3,19},{19,3},{4,20},{20... | collective-permute-start | bytes 3538952 | tf_op jit(solution)/shard_map/ppermute | solution.py:182
  156.1 21.9 %collective-permute-start.9 = (bf16[1024,192]{1,0:T(8,128)(2,1)}, bf16[1024,192]{1,0:T(8,128)(2,1)S(1)}, u32[]{:S(2)}, u32[]{:S(2)}) collective-permute-start(bf16[1024,192]{1,0:T(8,128)(2,1)} %get-tuple-element.174), channel_id=1, source_target_pairs={{0,4},{4,0},{1,5},{5,1},{2,6},{6,2},{3,7},{7,3},{8,12},{12,8},{9,1... | collective-permute-start | bytes 1179656 | tf_op jit(solution)/shard_map/ppermute | solution.py:402
  175.9 15.5 %collective-permute-start.12 = (bf16[192,1536]{1,0:T(8,128)(2,1)S(1)}, bf16[192,1536]{1,0:T(8,128)(2,1)S(1)}, u32[]{:S(2)}, u32[]{:S(2)}) collective-permute-start(bf16[192,1536]{1,0:T(8,128)(2,1)S(1)} %bitcast.382), channel_id=1, source_target_pairs={{0,8},{8,0},{1,9},{9,1},{2,10},{10,2},{3,11},{11,3},{4,12},{12,4},... | collective-permute-start | bytes 1769480 | tf_op jit(solution)/shard_map/ppermute | solution.py:182
  177.4 15.2 %collective-permute-start.11 = (bf16[192,1536]{1,0:T(8,128)(2,1)S(1)}, bf16[192,1536]{1,0:T(8,128)(2,1)S(1)}, u32[]{:S(2)}, u32[]{:S(2)}) collective-permute-start(bf16[192,1536]{1,0:T(8,128)(2,1)S(1)} %bitcast.383), channel_id=1, source_target_pairs={{0,4},{4,0},{1,5},{5,1},{2,6},{6,2},{3,7},{7,3},{8,12},{12,8},{9,1... | collective-permute-start | bytes 1769480 | tf_op jit(solution)/shard_map/ppermute | solution.py:182
  192.6 16.3 %collective-permute-start.14 = (bf16[192,1536]{1,0:T(8,128)(2,1)S(1)}, bf16[192,1536]{1,0:T(8,128)(2,1)S(1)}, u32[]{:S(2)}, u32[]{:S(2)}) collective-permute-start(bf16[192,1536]{1,0:T(8,128)(2,1)S(1)} %collective-permute-done.11), channel_id=1, source_target_pairs={{0,8},{8,0},{1,9},{9,1},{2,10},{10,2},{3,11},{11,3},{4,12},{12,4},... | collective-permute-start | bytes 1769480 | tf_op jit(solution)/shard_map/ppermute | solution.py:182
  193.1 48.1 %collective-permute-start.19 = (bf16[192,1536]{1,0:T(8,128)(2,1)S(1)}, bf16[192,1536]{1,0:T(8,128)(2,1)}, u32[]{:S(2)}, u32[]{:S(2)}) collective-permute-start(bf16[192,1536]{1,0:T(8,128)(2,1)S(1)} %bitcast.379), channel_id=1, source_target_pairs={{0,4},{4,0},{1,5},{5,1},{2,6},{6,2},{3,7},{7,3},{8,12},{12,8},{9,1... | collective-permute-start | bytes 1769480 | tf_op jit(solution)/shard_map/ppermute | solution.py:182
  193.7 25.8 %collective-permute-start.16 = (bf16[192,1536]{1,0:T(8,128)(2,1)S(1)}, bf16[192,1536]{1,0:T(8,128)(2,1)S(1)}, u32[]{:S(2)}, u32[]{:S(2)}) collective-permute-start(bf16[192,1536]{1,0:T(8,128)(2,1)S(1)} %bitcast.380), channel_id=1, source_target_pairs={{0,8},{8,0},{1,9},{9,1},{2,10},{10,2},{3,11},{11,3},{4,12},{12,4},... | collective-permute-start | bytes 1769480 | tf_op jit(solution)/shard_map/ppermute | solution.py:182
  195.2 19.8 %collective-permute-start.13 = (bf16[1024,128]{1,0:T(8,128)(2,1)S(1)}, bf16[1024,128]{1,0:T(8,128)(2,1)S(1)}, u32[]{:S(2)}, u32[]{:S(2)}) collective-permute-start(bf16[1024,128]{1,0:T(8,128)(2,1)S(1)} %get-tuple-element.535), channel_id=1, source_target_pairs={{0,4},{4,0},{1,5},{5,1},{2,6},{6,2},{3,7},{7,3},{8,12},{12,8},{9,1... | collective-permute-start | bytes 786440 | tf_op jit(solution)/shard_map/ppermute | solution.py:402
  224.3 16.9 %collective-permute-start.18 = (bf16[192,1536]{1,0:T(8,128)(2,1)S(1)}, bf16[192,1536]{1,0:T(8,128)(2,1)}, u32[]{:S(2)}, u32[]{:S(2)}) collective-permute-start(bf16[192,1536]{1,0:T(8,128)(2,1)S(1)} %concatenate.353), channel_id=1, source_target_pairs={{0,8},{8,0},{1,9},{9,1},{2,10},{10,2},{3,11},{11,3},{4,12},{12,4},... | collective-permute-start | bytes 1769480 | tf_op jit(solution)/shard_map/ppermute | solution.py:182
  226.9 22.7 %collective-permute-start.20 = (bf16[192,1536]{1,0:T(8,128)(2,1)}, bf16[192,1536]{1,0:T(8,128)(2,1)S(1)}, u32[]{:S(2)}, u32[]{:S(2)}) collective-permute-start(bf16[192,1536]{1,0:T(8,128)(2,1)} %concatenate.356), channel_id=1, source_target_pairs={{0,4},{4,0},{1,5},{5,1},{2,6},{6,2},{3,7},{7,3},{8,12},{12,8},{9,1... | collective-permute-start | bytes 1769480 | tf_op jit(solution)/shard_map/ppermute | solution.py:182
  241.2 15.7 %collective-permute-start.21 = (bf16[192,1536]{1,0:T(8,128)(2,1)}, bf16[192,1536]{1,0:T(8,128)(2,1)S(1)}, u32[]{:S(2)}, u32[]{:S(2)}) collective-permute-start(bf16[192,1536]{1,0:T(8,128)(2,1)} %collective-permute-done.19), channel_id=1, source_target_pairs={{0,8},{8,0},{1,9},{9,1},{2,10},{10,2},{3,11},{11,3},{4,12},{12,4},... | collective-permute-start | bytes 1769480 | tf_op jit(solution)/shard_map/ppermute | solution.py:182
  259.8 51.7 %collective-permute-start.25 = (bf16[192,1536]{1,0:T(8,128)(2,1)}, bf16[192,1536]{1,0:T(8,128)(2,1)}, u32[]{:S(2)}, u32[]{:S(2)}) collective-permute-start(bf16[192,1536]{1,0:T(8,128)(2,1)} %bitcast.163), channel_id=1, source_target_pairs={{0,8},{8,0},{1,9},{9,1},{2,10},{10,2},{3,11},{11,3},{4,12},{12,4},... | collective-permute-start | bytes 1769480 | tf_op jit(solution)/shard_map/ppermute | solution.py:182
  260.5 27.9 %collective-permute-start.23 = (bf16[192,1536]{1,0:T(8,128)(2,1)S(1)}, bf16[192,1536]{1,0:T(8,128)(2,1)S(1)}, u32[]{:S(2)}, u32[]{:S(2)}) collective-permute-start(bf16[192,1536]{1,0:T(8,128)(2,1)S(1)} %collective-permute-done.20), channel_id=1, source_target_pairs={{0,8},{8,0},{1,9},{9,1},{2,10},{10,2},{3,11},{11,3},{4,12},{12,4},... | collective-permute-start | bytes 1769480 | tf_op jit(solution)/shard_map/ppermute | solution.py:182
  290.8 19.2 %collective-permute-start.24 = (bf16[1024,384]{1,0:T(8,128)(2,1)S(1)}, bf16[1024,384]{1,0:T(8,128)(2,1)S(1)}, u32[]{:S(2)}, u32[]{:S(2)}) collective-permute-start(bf16[1024,384]{1,0:T(8,128)(2,1)S(1)} %slice.807), channel_id=1, source_target_pairs={{0,4},{4,0},{1,5},{5,1},{2,6},{6,2},{3,7},{7,3},{8,12},{12,8},{9,1... | collective-permute-start | bytes 2359304 | tf_op jit(solution)/shard_map/ppermute | solution.py:402
  294.1 43.0 %all-to-all-start.1 = ((bf16[4,128,768]{2,1,0:T(8,128)(2,1)}), bf16[4,128,768]{2,1,0:T(8,128)(2,1)}, u32[]{:S(2)}, u32[]{:S(2)}) async-start(bf16[4,128,768]{2,1,0:T(8,128)(2,1)} %maximum_select_fusion.3), calls=%async_computation.1 | async-start | bytes 1572864 | tf_op jit(solution)/shard_map/all_to_all | solution.py:210
  311.5 19.1 %collective-permute-start.26 = (bf16[1024,192]{1,0:T(8,128)(2,1)S(1)}, bf16[1024,192]{1,0:T(8,128)(2,1)S(1)}, u32[]{:S(2)}, u32[]{:S(2)}) collective-permute-start(bf16[1024,192]{1,0:T(8,128)(2,1)S(1)} %get-tuple-element.206), channel_id=1, source_target_pairs={{0,4},{4,0},{1,5},{5,1},{2,6},{6,2},{3,7},{7,3},{8,12},{12,8},{9,1... | collective-permute-start | bytes 1179656 | tf_op jit(solution)/shard_map/ppermute | solution.py:402
  313.0 24.1 %collective-permute-start.28 = (bf16[192,1536]{1,0:T(8,128)(2,1)}, bf16[192,1536]{1,0:T(8,128)(2,1)}, u32[]{:S(2)}, u32[]{:S(2)}) collective-permute-start(bf16[192,1536]{1,0:T(8,128)(2,1)} %bitcast.163), channel_id=1, source_target_pairs={{0,4},{4,0},{1,5},{5,1},{2,6},{6,2},{3,7},{7,3},{8,12},{12,8},{9,1... | collective-permute-start | bytes 1769480 | tf_op jit(solution)/shard_map/ppermute | solution.py:182
  313.6 23.5 %collective-permute-start.27 = (bf16[192,1536]{1,0:T(8,128)(2,1)S(1)}, bf16[192,1536]{1,0:T(8,128)(2,1)}, u32[]{:S(2)}, u32[]{:S(2)}) collective-permute-start(bf16[192,1536]{1,0:T(8,128)(2,1)S(1)} %bitcast.377), channel_id=1, source_target_pairs={{0,8},{8,0},{1,9},{9,1},{2,10},{10,2},{3,11},{11,3},{4,12},{12,4},... | collective-permute-start | bytes 1769480 | tf_op jit(solution)/shard_map/ppermute | solution.py:182
  340.5 29.8 %all-to-all-start.2 = ((bf16[4,128,768]{2,1,0:T(8,128)(2,1)}), bf16[4,128,768]{2,1,0:T(8,128)(2,1)}, u32[]{:S(2)}, u32[]{:S(2)}) async-start(bf16[4,128,768]{2,1,0:T(8,128)(2,1)} %maximum_select_fusion.5), calls=%async_computation.2 | async-start | bytes 1572864 | tf_op jit(solution)/shard_map/all_to_all | solution.py:210
  345.1 13.5 %collective-permute-start.30 = (bf16[192,1536]{1,0:T(8,128)(2,1)}, bf16[192,1536]{1,0:T(8,128)(2,1)S(1)}, u32[]{:S(2)}, u32[]{:S(2)}) collective-permute-start(bf16[192,1536]{1,0:T(8,128)(2,1)} %collective-permute-done.28), channel_id=1, source_target_pairs={{0,8},{8,0},{1,9},{9,1},{2,10},{10,2},{3,11},{11,3},{4,12},{12,4},... | collective-permute-start | bytes 1769480 | tf_op jit(solution)/shard_map/ppermute | solution.py:182
  345.7 51.5 %collective-permute-start.34 = (bf16[192,1536]{1,0:T(8,128)(2,1)}, bf16[192,1536]{1,0:T(8,128)(2,1)}, u32[]{:S(2)}, u32[]{:S(2)}) collective-permute-start(bf16[192,1536]{1,0:T(8,128)(2,1)} %bitcast.376), channel_id=1, source_target_pairs={{0,4},{4,0},{1,5},{5,1},{2,6},{6,2},{3,7},{7,3},{8,12},{12,8},{9,1... | collective-permute-start | bytes 1769480 | tf_op jit(solution)/shard_map/ppermute | solution.py:182
  348.1 19.3 %collective-permute-start.29 = (bf16[1024,128]{1,0:T(8,128)(2,1)S(1)}, bf16[1024,128]{1,0:T(8,128)(2,1)}, u32[]{:S(2)}, u32[]{:S(2)}) collective-permute-start(bf16[1024,128]{1,0:T(8,128)(2,1)S(1)} %get-tuple-element.531), channel_id=1, source_target_pairs={{0,4},{4,0},{1,5},{5,1},{2,6},{6,2},{3,7},{7,3},{8,12},{12,8},{9,1... | collective-permute-start | bytes 786440 | tf_op jit(solution)/shard_map/ppermute | solution.py:402
  397.2 15.6 %collective-permute-start.35 = (bf16[192,1536]{1,0:T(8,128)(2,1)}, bf16[192,1536]{1,0:T(8,128)(2,1)S(1)}, u32[]{:S(2)}, u32[]{:S(2)}) collective-permute-start(bf16[192,1536]{1,0:T(8,128)(2,1)} %collective-permute-done.34), channel_id=1, source_target_pairs={{0,8},{8,0},{1,9},{9,1},{2,10},{10,2},{3,11},{11,3},{4,12},{12,4},... | collective-permute-start | bytes 1769480 | tf_op jit(solution)/shard_map/ppermute | solution.py:182
  434.8 15.3 %collective-permute-start.37 = (bf16[192,1536]{1,0:T(8,128)(2,1)S(1)}, bf16[192,1536]{1,0:T(8,128)(2,1)S(1)}, u32[]{:S(2)}, u32[]{:S(2)}) collective-permute-start(bf16[192,1536]{1,0:T(8,128)(2,1)S(1)} %slice.677), channel_id=1, source_target_pairs={{0,8},{8,0},{1,9},{9,1},{2,10},{10,2},{3,11},{11,3},{4,12},{12,4},... | collective-permute-start | bytes 1769480 | tf_op jit(solution)/shard_map/ppermute | solution.py:182
  453.2 14.5 %collective-permute-start.39 = (bf16[192,1536]{1,0:T(8,128)(2,1)}, bf16[192,1536]{1,0:T(8,128)(2,1)}, u32[]{:S(2)}, u32[]{:S(2)}) collective-permute-start(bf16[192,1536]{1,0:T(8,128)(2,1)} %slice.679), channel_id=1, source_target_pairs={{0,8},{8,0},{1,9},{9,1},{2,10},{10,2},{3,11},{11,3},{4,12},{12,4},... | collective-permute-start | bytes 1769480 | tf_op jit(solution)/shard_map/ppermute | solution.py:182
  455.9 60.8 %all-to-all-start.3 = ((bf16[4,128,768]{2,1,0:T(8,128)(2,1)}), bf16[4,128,768]{2,1,0:T(8,128)(2,1)}, u32[]{:S(2)}, u32[]{:S(2)}) async-start(bf16[4,128,768]{2,1,0:T(8,128)(2,1)} %maximum_select_fusion.7), calls=%async_computation.3 | async-start | bytes 1572864 | tf_op jit(solution)/shard_map/all_to_all | solution.py:210
  460.9 16.0 %collective-permute-start.42 = (bf16[192,1536]{1,0:T(8,128)(2,1)}, bf16[192,1536]{1,0:T(8,128)(2,1)}, u32[]{:S(2)}, u32[]{:S(2)}) collective-permute-start(bf16[192,1536]{1,0:T(8,128)(2,1)} %add_convert_fusion.25), channel_id=1, source_target_pairs={{0,4},{4,0},{1,5},{5,1},{2,6},{6,2},{3,7},{7,3},{8,12},{12,8},{9,1... | collective-permute-start | bytes 1769480 | tf_op jit(solution)/shard_map/ppermute | solution.py:182
  471.2 16.3 %collective-permute-start.44 = (bf16[192,1536]{1,0:T(8,128)(2,1)S(1)}, bf16[192,1536]{1,0:T(8,128)(2,1)S(1)}, u32[]{:S(2)}, u32[]{:S(2)}) collective-permute-start(bf16[192,1536]{1,0:T(8,128)(2,1)S(1)} %get-tuple-element.396), channel_id=1, source_target_pairs={{0,8},{8,0},{1,9},{9,1},{2,10},{10,2},{3,11},{11,3},{4,12},{12,4},... | collective-permute-start | bytes 1769480 | tf_op jit(solution)/shard_map/ppermute | solution.py:182
  475.5 37.6 %collective-permute-start.40 = (bf16[1024,64]{0,1:T(8,128)(2,1)S(1)}, bf16[1024,64]{0,1:T(8,128)(2,1)S(1)}, u32[]{:S(2)}, u32[]{:S(2)}) collective-permute-start(bf16[1024,64]{0,1:T(8,128)(2,1)S(1)} %copy-done.100), channel_id=1, source_target_pairs={{0,4},{4,0},{1,5},{5,1},{2,6},{6,2},{3,7},{7,3},{8,12},{12,8},{9,1... | collective-permute-start | bytes 393224 | tf_op jit(solution)/shard_map/ppermute | solution.py:402
  476.4 37.8 %collective-permute-start.43 = (bf16[192,1536]{1,0:T(8,128)(2,1)}, bf16[192,1536]{1,0:T(8,128)(2,1)}, u32[]{:S(2)}, u32[]{:S(2)}) collective-permute-start(bf16[192,1536]{1,0:T(8,128)(2,1)} %get-tuple-element.395), channel_id=1, source_target_pairs={{0,8},{8,0},{1,9},{9,1},{2,10},{10,2},{3,11},{11,3},{4,12},{12,4},... | collective-permute-start | bytes 1769480 | tf_op jit(solution)/shard_map/ppermute | solution.py:182
  489.5 24.8 %collective-permute-start.45 = (bf16[192,1536]{1,0:T(8,128)(2,1)}, bf16[192,1536]{1,0:T(8,128)(2,1)}, u32[]{:S(2)}, u32[]{:S(2)}) collective-permute-start(bf16[192,1536]{1,0:T(8,128)(2,1)} %add_convert_fusion.21), channel_id=1, source_target_pairs={{0,4},{4,0},{1,5},{5,1},{2,6},{6,2},{3,7},{7,3},{8,12},{12,8},{9,1... | collective-permute-start | bytes 1769480 | tf_op jit(solution)/shard_map/ppermute | solution.py:182
  517.7 24.4 %collective-permute-start.47 = (bf16[1024,384]{1,0:T(8,128)(2,1)S(1)}, bf16[1024,384]{1,0:T(8,128)(2,1)}, u32[]{:S(2)}, u32[]{:S(2)}) collective-permute-start(bf16[1024,384]{1,0:T(8,128)(2,1)S(1)} %get-tuple-element.409), channel_id=1, source_target_pairs={{0,4},{4,0},{1,5},{5,1},{2,6},{6,2},{3,7},{7,3},{8,12},{12,8},{9,1... | collective-permute-start | bytes 2359304 | tf_op jit(solution)/shard_map/ppermute | solution.py:402
  560.4 16.2 %collective-permute-start.50 = (bf16[192,1536]{1,0:T(8,128)(2,1)S(1)}, bf16[192,1536]{1,0:T(8,128)(2,1)S(1)}, u32[]{:S(2)}, u32[]{:S(2)}) collective-permute-start(bf16[192,1536]{1,0:T(8,128)(2,1)S(1)} %slice.691), channel_id=1, source_target_pairs={{0,8},{8,0},{1,9},{9,1},{2,10},{10,2},{3,11},{11,3},{4,12},{12,4},... | collective-permute-start | bytes 1769480 | tf_op jit(solution)/shard_map/ppermute | solution.py:182
  562.7 33.7 %collective-permute-start.51 = (bf16[192,1536]{1,0:T(8,128)(2,1)}, bf16[192,1536]{1,0:T(8,128)(2,1)}, u32[]{:S(2)}, u32[]{:S(2)}) collective-permute-start(bf16[192,1536]{1,0:T(8,128)(2,1)} %slice.693), channel_id=1, source_target_pairs={{0,8},{8,0},{1,9},{9,1},{2,10},{10,2},{3,11},{11,3},{4,12},{12,4},... | collective-permute-start | bytes 1769480 | tf_op jit(solution)/shard_map/ppermute | solution.py:182
  580.7 26.2 %collective-permute-start.53 = (bf16[192,1536]{1,0:T(8,128)(2,1)}, bf16[192,1536]{1,0:T(8,128)(2,1)S(1)}, u32[]{:S(2)}, u32[]{:S(2)}) collective-permute-start(bf16[192,1536]{1,0:T(8,128)(2,1)} %concatenate.376), channel_id=1, source_target_pairs={{0,4},{4,0},{1,5},{5,1},{2,6},{6,2},{3,7},{7,3},{8,12},{12,8},{9,1... | collective-permute-start | bytes 1769480 | tf_op jit(solution)/shard_map/ppermute | solution.py:182
  613.4 15.8 %collective-permute-start.54 = (bf16[192,1536]{1,0:T(8,128)(2,1)S(1)}, bf16[192,1536]{1,0:T(8,128)(2,1)S(1)}, u32[]{:S(2)}, u32[]{:S(2)}) collective-permute-start(bf16[192,1536]{1,0:T(8,128)(2,1)S(1)} %slice.707), channel_id=1, source_target_pairs={{0,8},{8,0},{1,9},{9,1},{2,10},{10,2},{3,11},{11,3},{4,12},{12,4},... | collective-permute-start | bytes 1769480 | tf_op jit(solution)/shard_map/ppermute | solution.py:182
  631.1 15.0 %collective-permute-start.56 = (bf16[192,1536]{1,0:T(8,128)(2,1)}, bf16[192,1536]{1,0:T(8,128)(2,1)}, u32[]{:S(2)}, u32[]{:S(2)}) collective-permute-start(bf16[192,1536]{1,0:T(8,128)(2,1)} %slice.709), channel_id=1, source_target_pairs={{0,8},{8,0},{1,9},{9,1},{2,10},{10,2},{3,11},{11,3},{4,12},{12,4},... | collective-permute-start | bytes 1769480 | tf_op jit(solution)/shard_map/ppermute | solution.py:182
  633.8 60.4 %all-to-all-start.4 = ((bf16[4,128,768]{2,1,0:T(8,128)(2,1)}), bf16[4,128,768]{2,1,0:T(8,128)(2,1)}, u32[]{:S(2)}, u32[]{:S(2)}) async-start(bf16[4,128,768]{2,1,0:T(8,128)(2,1)} %maximum_select_fusion.9), calls=%async_computation.4 | async-start | bytes 1572864 | tf_op jit(solution)/shard_map/all_to_all | solution.py:210
  638.6 106.8 %reduce-scatter.4.cloned.1.call-start = ((), (), s32[]{:S(2)}) async-start(), calls=%async_computation.9 | async-start | bytes 1474560 | tf_op jit(solution)/shard_map/reduce_scatter | solution.py:601
  638.8 15.9 %collective-permute-start.58 = (bf16[192,1536]{1,0:T(8,128)(2,1)S(1)}, bf16[192,1536]{1,0:T(8,128)(2,1)}, u32[]{:S(2)}, u32[]{:S(2)}) collective-permute-start(bf16[192,1536]{1,0:T(8,128)(2,1)S(1)} %add_convert_fusion.16), channel_id=1, source_target_pairs={{0,4},{4,0},{1,5},{5,1},{2,6},{6,2},{3,7},{7,3},{8,12},{12,8},{9,1... | collective-permute-start | bytes 1769480 | tf_op jit(solution)/shard_map/ppermute | solution.py:182
  649.6 16.3 %collective-permute-start.60 = (bf16[192,1536]{1,0:T(8,128)(2,1)S(1)}, bf16[192,1536]{1,0:T(8,128)(2,1)S(1)}, u32[]{:S(2)}, u32[]{:S(2)}) collective-permute-start(bf16[192,1536]{1,0:T(8,128)(2,1)S(1)} %get-tuple-element.392), channel_id=1, source_target_pairs={{0,8},{8,0},{1,9},{9,1},{2,10},{10,2},{3,11},{11,3},{4,12},{12,4},... | collective-permute-start | bytes 1769480 | tf_op jit(solution)/shard_map/ppermute | solution.py:182
  652.9 37.8 %collective-permute-start.57 = (bf16[1024,64]{0,1:T(8,128)(2,1)S(1)}, bf16[1024,64]{0,1:T(8,128)(2,1)S(1)}, u32[]{:S(2)}, u32[]{:S(2)}) collective-permute-start(bf16[1024,64]{0,1:T(8,128)(2,1)S(1)} %get-tuple-element.283), channel_id=1, source_target_pairs={{0,4},{4,0},{1,5},{5,1},{2,6},{6,2},{3,7},{7,3},{8,12},{12,8},{9,1... | collective-permute-start | bytes 393224 | tf_op jit(solution)/shard_map/ppermute | solution.py:402
  654.2 37.6 %collective-permute-start.59 = (bf16[192,1536]{1,0:T(8,128)(2,1)}, bf16[192,1536]{1,0:T(8,128)(2,1)}, u32[]{:S(2)}, u32[]{:S(2)}) collective-permute-start(bf16[192,1536]{1,0:T(8,128)(2,1)} %get-tuple-element.391), channel_id=1, source_target_pairs={{0,8},{8,0},{1,9},{9,1},{2,10},{10,2},{3,11},{11,3},{4,12},{12,4},... | collective-permute-start | bytes 1769480 | tf_op jit(solution)/shard_map/ppermute | solution.py:182
  667.9 23.9 %collective-permute-start.61 = (bf16[192,1536]{1,0:T(8,128)(2,1)}, bf16[192,1536]{1,0:T(8,128)(2,1)}, u32[]{:S(2)}, u32[]{:S(2)}) collective-permute-start(bf16[192,1536]{1,0:T(8,128)(2,1)} %add_convert_fusion.12), channel_id=1, source_target_pairs={{0,4},{4,0},{1,5},{5,1},{2,6},{6,2},{3,7},{7,3},{8,12},{12,8},{9,1... | collective-permute-start | bytes 1769480 | tf_op jit(solution)/shard_map/ppermute | solution.py:182
  695.7 13.1 %collective-permute-start.64 = (bf16[2,192,768]{2,1,0:T(8,128)(2,1)S(1)}, bf16[2,192,768]{2,1,0:T(8,128)(2,1)S(1)}, u32[]{:S(2)}, u32[]{:S(2)}) collective-permute-start(bf16[2,192,768]{2,1,0:T(8,128)(2,1)S(1)} %bitcast.403), channel_id=1, source_target_pairs={{0,16},{16,0},{1,17},{17,1},{2,18},{18,2},{3,19},{19,3},{4,20},{20... | collective-permute-start | bytes 1769480 | tf_op jit(solution)/shard_map/ppermute | solution.py:182
  695.7 13.1 %collective-permute-start.63 = (bf16[2,192,768]{2,1,0:T(8,128)(2,1)S(1)}, bf16[2,192,768]{2,1,0:T(8,128)(2,1)S(1)}, u32[]{:S(2)}, u32[]{:S(2)}) collective-permute-start(bf16[2,192,768]{2,1,0:T(8,128)(2,1)S(1)} %bitcast.402), channel_id=1, source_target_pairs={{0,16},{16,0},{1,17},{17,1},{2,18},{18,2},{3,19},{19,3},{4,20},{20... | collective-permute-start | bytes 1769480 | tf_op jit(solution)/shard_map/ppermute | solution.py:182
  697.5 20.6 %collective-permute-start.62 = (bf16[1024,384]{1,0:T(8,128)(2,1)}, bf16[1024,384]{1,0:T(8,128)(2,1)S(1)}, u32[]{:S(2)}, u32[]{:S(2)}) collective-permute-start(bf16[1024,384]{1,0:T(8,128)(2,1)} %get-tuple-element.407), channel_id=1, source_target_pairs={{0,4},{4,0},{1,5},{5,1},{2,6},{6,2},{3,7},{7,3},{8,12},{12,8},{9,1... | collective-permute-start | bytes 2359304 | tf_op jit(solution)/shard_map/ppermute | solution.py:402
  712.1 16.4 %collective-permute-start.65 = (bf16[1024,192]{1,0:T(8,128)(2,1)}, bf16[1024,192]{1,0:T(8,128)(2,1)S(1)}, u32[]{:S(2)}, u32[]{:S(2)}) collective-permute-start(bf16[1024,192]{1,0:T(8,128)(2,1)} %get-tuple-element.431), channel_id=1, source_target_pairs={{0,4},{4,0},{1,5},{5,1},{2,6},{6,2},{3,7},{7,3},{8,12},{12,8},{9,1... | collective-permute-start | bytes 1179656 | tf_op jit(solution)/shard_map/ppermute | solution.py:402
  715.5 79.4 %collective-permute-start.46 = (bf16[4,128,768]{2,1,0:T(8,128)(2,1)}, bf16[4,128,768]{2,1,0:T(8,128)(2,1)}, u32[]{:S(2)}, u32[]{:S(2)}) collective-permute-start(bf16[4,128,768]{2,1,0:T(8,128)(2,1)} %broadcast_select_fusion.4), channel_id=1, source_target_pairs={{0,16},{16,0},{1,17},{17,1},{2,18},{18,2},{3,19},{19,3},{4,20},{20... | collective-permute-start | bytes 2359304 | tf_op jit(solution)/shard_map/ppermute | solution.py:182
  715.5 107.0 %reduce-scatter.8.cloned.1.call-start = ((), (), s32[]{:S(2)}) async-start(), calls=%async_computation.11 | async-start | bytes 1474560 | tf_op jit(solution)/shard_map/reduce_scatter | solution.py:601
  751.8 16.3 %collective-permute-start.67 = (bf16[192,1536]{1,0:T(8,128)(2,1)S(1)}, bf16[192,1536]{1,0:T(8,128)(2,1)S(1)}, u32[]{:S(2)}, u32[]{:S(2)}) collective-permute-start(bf16[192,1536]{1,0:T(8,128)(2,1)S(1)} %slice.721), channel_id=1, source_target_pairs={{0,8},{8,0},{1,9},{9,1},{2,10},{10,2},{3,11},{11,3},{4,12},{12,4},... | collective-permute-start | bytes 1769480 | tf_op jit(solution)/shard_map/ppermute | solution.py:182
  754.2 25.3 %collective-permute-start.69 = (bf16[192,1536]{1,0:T(8,128)(2,1)}, bf16[192,1536]{1,0:T(8,128)(2,1)}, u32[]{:S(2)}, u32[]{:S(2)}) collective-permute-start(bf16[192,1536]{1,0:T(8,128)(2,1)} %slice.729), channel_id=1, source_target_pairs={{0,8},{8,0},{1,9},{9,1},{2,10},{10,2},{3,11},{11,3},{4,12},{12,4},... | collective-permute-start | bytes 1769480 | tf_op jit(solution)/shard_map/ppermute | solution.py:182
  769.5 13.0 %collective-permute-start.70 = (bf16[192,1536]{1,0:T(8,128)(2,1)}, bf16[192,1536]{1,0:T(8,128)(2,1)}, u32[]{:S(2)}, u32[]{:S(2)}) collective-permute-start(bf16[192,1536]{1,0:T(8,128)(2,1)} %concatenate.388), channel_id=1, source_target_pairs={{0,4},{4,0},{1,5},{5,1},{2,6},{6,2},{3,7},{7,3},{8,12},{12,8},{9,1... | collective-permute-start | bytes 1769480 | tf_op jit(solution)/shard_map/ppermute | solution.py:182
  787.6 30.5 %all-to-all-start.5 = ((bf16[4,128,768]{2,1,0:T(8,128)(2,1)}), bf16[4,128,768]{2,1,0:T(8,128)(2,1)S(1)}, u32[]{:S(2)}, u32[]{:S(2)}) async-start(bf16[4,128,768]{2,1,0:T(8,128)(2,1)} %maximum_select_fusion.11), calls=%async_computation.6 | async-start | bytes 1572864 | tf_op jit(solution)/shard_map/all_to_all | solution.py:210
  792.2 43.7 %reduce-scatter.6.cloned.1.call-start = ((), (), s32[]{:S(2)}) async-start(), calls=%async_computation.10 | async-start | bytes 1474560 | tf_op jit(solution)/shard_map/reduce_scatter | solution.py:601
  800.2 19.2 %collective-permute-start.73 = (f32[4,192]{1,0:T(4,128)S(1)}, f32[4,192]{1,0:T(4,128)S(1)}, u32[]{:S(2)}, u32[]{:S(2)}) collective-permute-start(f32[4,192]{1,0:T(4,128)S(1)} %slice.865), channel_id=1, source_target_pairs={{0,4},{4,0},{1,5},{5,1},{2,6},{6,2},{3,7},{7,3},{8,12},{12,8},{9,1... | collective-permute-start | bytes 9224 | tf_op jit(solution)/shard_map/ppermute | solution.py:182
  (145 other events, 1167.6 us)
Sparse Core Ops, SparseCore 0:
  10.4 33.1 all-gather.4
  91.9 50.7 all-gather.6
  715.6 29.7 reduce-scatter.3
  772.8 29.0 reduce-scatter.7
  804.1 31.7 reduce-scatter.5

commit v3 on v2

--- a/solution.py
+++ b/solution.py
@@ -16,12 +16,92 @@
 F32 = jnp.float32
 BF16 = jnp.bfloat16
 VMEM_LIMIT = 48 * 1024 * 1024
-
-
-def normed(values, gain_row, shift_row):
+SEC, DP, CTX, TEN = "section", "dp", "context", "tensor"
+ATTN, UP, DOWN, FFN, ENTRY, EXIT, LAST = range(7)
+OWN, NEAR, OWN_FAR, NEAR_FAR, KEPT, CAME, SUM_0, SUM_1, SUM, ALL, DONE = range(11)
+
+
+def centred(values):
     center = values - jnp.mean(values, -1, keepdims=True)
     spread = jnp.mean(center * center, -1, keepdims=True)
-    return center * lax.rsqrt(spread + EPS) * gain_row + shift_row
+    return center, lax.rsqrt(spread + EPS)
+
+
+def norm_kernel(summed, *refs):
+    if summed:
+        base_ref, own_ref, far_ref, gain_ref, shift_ref, sum_ref, out_ref = refs
+        values = base_ref[...].astype(F32) + own_ref[...] + far_ref[...].astype(F32)
+        sum_ref[...] = values
+    else:
+        base_ref, gain_ref, shift_ref, out_ref = refs
+        values = base_ref[...].astype(F32)
+    center, scale = centred(values)
+    out_ref[...] = (center * scale * gain_ref[...] + shift_ref[...]).astype(BF16)
+
+
+def norm(base, gain, shift, own=None, far=None):
+    count, width = base.shape
+    rows = min(256, count)
+    wide = pl.BlockSpec((rows, width), lambda i: (i, 0))
+    single = pl.BlockSpec((1, width), lambda i: (0, 0))
+    summed = own is not None
+    values = [base, own, far] if summed else [base]
+    shapes = [jax.ShapeDtypeStruct((count, width), BF16)]
+    if summed:
+        shapes.insert(0, jax.ShapeDtypeStruct((count, width), F32))
+    result = pl.pallas_call(
+        functools.partial(norm_kernel, summed),
+        grid=(count // rows,),
+        in_specs=[wide] * len(values) + [single] * 2,
+        out_specs=[wide] * len(shapes),
+        out_shape=shapes,
+        compiler_params=pltpu.CompilerParams(vmem_limit_bytes=VMEM_LIMIT),
+        cost_estimate=pl.CostEstimate(
+            flops=count * width * 12, bytes_accessed=count * width * 14, transcendentals=count),
+        name="norm",
+    )(*values, gain[None], shift[None])
+    return result if summed else result[0]
+
+
+def norm_back_kernel(both, value_ref, own_ref, far_ref, base_ref, gain_ref, *outs):
+    sums_ref = outs[-1]
+
+    @pl.when(pl.program_id(0) == 0)
+    def clear():
+        sums_ref[...] = jnp.zeros_like(sums_ref)
+
+    grad = own_ref[...] + far_ref[...].astype(F32)
+    center, scale = centred(value_ref[...].astype(F32))
+    unit = center * scale
+    sums_ref[0:1] += jnp.sum(grad * unit, 0, keepdims=True)
+    sums_ref[1:2] += jnp.sum(grad, 0, keepdims=True)
+    scaled = grad * gain_ref[...]
+    inner = jnp.mean(scaled * unit, -1, keepdims=True)
+    total = base_ref[...].astype(F32) + scale * (
+        scaled - jnp.mean(scaled, -1, keepdims=True) - unit * inner)
+    if both:
+        outs[0][...] = total
+    outs[-2][...] = total.astype(BF16)
+
+
+def norm_back(value, own, far, base, gain, both):
+    count, width = value.shape
+    rows = min(256, count)
+    wide = pl.BlockSpec((rows, width), lambda i: (i, 0))
+    shapes = [jax.ShapeDtypeStruct((count, width), BF16), jax.ShapeDtypeStruct((2, width), F32)]
+    if both:
+        shapes.insert(0, jax.ShapeDtypeStruct((count, width), F32))
+    return pl.pallas_call(
+        functools.partial(norm_back_kernel, both),
+        grid=(count // rows,),
+        in_specs=[wide] * 4 + [pl.BlockSpec((1, width), lambda i: (0, 0))],
+        out_specs=[wide] * (len(shapes) - 1) + [pl.BlockSpec((2, width), lambda i: (0, 0))],
+        out_shape=shapes,
+        compiler_params=pltpu.CompilerParams(vmem_limit_bytes=VMEM_LIMIT),
+        cost_estimate=pl.CostEstimate(
+            flops=count * width * 20, bytes_accessed=count * width * 16, transcendentals=count),
+        name="norm_back",
+    )(value, own, far, base, gain[None])
 
 
 def dot(left, right, contract):
@@ -207,17 +287,17 @@
 
 
 def spread_tensor(blocks):
-    return lax.all_to_all(blocks, "tensor", 0, 0, tiled=True)
+    return lax.all_to_all(blocks, TEN, 0, 0, tiled=True)
 
 
 def square():
-    return lax.axis_size("dp") == 2 and lax.axis_size("context") == 2
+    return lax.axis_size(DP) == 2 and lax.axis_size(CTX) == 2
 
 
 def reorder(values):
     if not square():
         return values
-    dp, ctx = lax.axis_index("dp"), lax.axis_index("context")
+    dp, ctx = lax.axis_index(DP), lax.axis_index(CTX)
     size = values.shape[-1] // 4
     half = 2 * size
     values = jnp.where(dp == 1, jnp.concatenate([values[..., half:], values[..., :half]], -1), values)
@@ -231,11 +311,11 @@
 
 
 def tensor_pieces(value):
-    count = lax.axis_size("tensor")
+    count = lax.axis_size(TEN)
     pieces = [value]
     for step in range(1, count):
         pairs = [(n, (n + step) % count) for n in range(count)]
-        pieces.append(lax.ppermute(value, "tensor", pairs))
+        pieces.append(lax.ppermute(value, TEN, pairs))
     return pieces
 
 
@@ -244,12 +324,12 @@
 
 
 def per_device(inputs, cotangent, w_qkv, w_out, w_up, w_down, norm_gains, norm_shifts):
-    section = lax.axis_index("section")
-    tensors = lax.axis_size("tensor")
-    contexts = lax.axis_size("context")
-    ctx = lax.axis_index("context")
+    section = lax.axis_index(SEC)
+    tensors = lax.axis_size(TEN)
+    contexts = lax.axis_size(CTX)
+    ctx = lax.axis_index(CTX)
     micro, _, span, width = inputs.shape
-    assert micro == tensors and lax.axis_size("section") == 2 and tensors % 2 == 0
+    assert micro == tensors and lax.axis_size(SEC) == 2 and tensors % 2 == 0
     half_span = span // 2
     count = tensors * span
     own_rows = w_qkv.shape[2]
@@ -265,13 +345,16 @@
     held = {}
 
     def stage(compute, *jobs):
-        made = {name: job() for name, job in jobs}
-        leaves, shape = jax.tree.flatten((compute(), made))
+        made = {}
+        for key, job in jobs:
+            value = job()
+            made.update(value if isinstance(value, dict) else {key: value})
+        leaves, shape = jax.tree.flatten((compute(), [*made.values()]))
         if not leaves:
             return ()
-        result, made = jax.tree.unflatten(shape, lax.optimization_barrier(leaves))
-        for name, value in made.items():
-            held.update(value if isinstance(value, dict) else {name: value})
+        result, new = jax.tree.unflatten(shape, lax.optimization_barrier(leaves))
+        held.update(zip(made, new))
+        held[LAST] = jax.tree.leaves((result, new))[0]
         return result
 
 
@@ -325,7 +408,7 @@
     attn_share = jnp.concatenate(pieces + [w_out[0].T], 1)
 
     def over_tensor(share):
-        gathered = lax.all_gather(share, "tensor")
+        gathered = lax.all_gather(share, TEN)
         split = gathered.reshape((2, tensors // 2) + share.shape)
         return take(split, section), take(split, 1 - section)
 
@@ -333,29 +416,24 @@
         return value.transpose(1, 0, 2).reshape(own_rows, -1)
 
     def attn_layer(layer):
-        kept, came = held["attn_kept"], held["attn_came"]
-        half = jnp.where(section == layer, kept, came)
+        half = jnp.where(section == layer, held[ATTN, KEPT], held[ATTN, CAME])
         split = half[:, :, :qkv_cols], half[:, :, qkv_cols:]
         if fast:
             return rows_layout(jnp.concatenate([
                 relative_columns(split[0], 3 * HEAD_DIM), relative_columns(split[1], HEAD_DIM)], 1))
         return jnp.concatenate([joined_columns(piece) for piece in split], 1)
 
-    def hidden_layer(name, layer):
-        half = jnp.where(section == layer, held[name + "_kept"], held[name + "_came"])
-        return rows_layout(joined_columns(half))
-
     def near_rows(own, flip=False):
         if not square():
             return own
-        return swap(flipped(own) if flip else own, "context")
+        return swap(flipped(own) if flip else own, CTX)
 
     def far_rows(rows):
-        return swap(rows, "dp") if square() else rows
+        return swap(rows, DP) if square() else rows
 
     def all_rows(own, near, own_far, near_far):
         if not square():
-            return lax.all_gather(own, ("dp", "context"), axis=0, tiled=True)
+            return lax.all_gather(own, (DP, CTX), axis=0, tiled=True)
         return jnp.concatenate([own, near, own_far, near_far])
 
     def reduce_dp(partial, block):
@@ -363,15 +441,15 @@
             return partial
         rows = partial.shape[0] // 4
         kept = partial[block * rows:(block + 1) * rows]
-        return add_bf16(kept, swap(partial[(block + 2) * rows:(block + 3) * rows], "dp"))
+        return add_bf16(kept, swap(partial[(block + 2) * rows:(block + 3) * rows], DP))
 
     def reduce_ctx(kept, sent, flip=False):
         if not square():
-            return lax.psum_scatter(sent, ("dp", "context"), scatter_dimension=0, tiled=True)
-        return add_bf16(kept, swap(flipped(sent) if flip else sent, "context"))
+            return lax.psum_scatter(sent, (DP, CTX), scatter_dimension=0, tiled=True)
+        return add_bf16(kept, swap(flipped(sent) if flip else sent, CTX))
 
     def both_halves(partial):
-        return partial + swap(partial.astype(BF16), "section").astype(F32)
+        return partial, swap(partial.astype(BF16), SEC)
 
 
     def split_heads(projected, each):
@@ -390,7 +468,8 @@
 
     def join_heads(parts_list):
         if fast:
-            return jnp.concatenate([block for blocks in parts_list for block in blocks], 1)
+            joined = [jnp.concatenate(blocks, 1) for blocks in parts_list]
+            return jnp.concatenate(lax.optimization_barrier(joined), 1)
         shaped = jnp.stack([in_order(blocks, ctx) for blocks in parts_list])
         shaped = shaped.transpose(2, 1, 0, 3).reshape(count, contexts * heads, -1)
         return shaped[:, :half_heads].reshape(count, -1)
@@ -399,7 +478,7 @@
         moved = [blocks[0]]
         for step in range(1, contexts):
             pairs = [(n, n ^ step) for n in range(contexts)]
-            moved.append(lax.ppermute(blocks[step], "context", pairs))
+            moved.append(lax.ppermute(blocks[step], CTX, pairs))
         return moved
 
     def to_all_rows(blocks):
@@ -411,16 +490,17 @@
         return exchanged([take(shaped, lax.bitwise_xor(ctx, step)) for step in range(contexts)])
 
 
-    norms_share = jnp.concatenate([norm_gains[0], norm_shifts[0]])
-    if square():
-        norms_near = jnp.concatenate([norms_share, swap(norms_share, "context")], 1)
-        norms_own = jnp.concatenate([norms_near, swap(norms_near, "dp")], 1)
-    else:
-        norms_own = lax.all_gather(norms_share, ("dp", "context"), axis=1, tiled=True)
-    norms_other = swap(norms_own, "section")
+    def gather_norms():
+        share = jnp.concatenate([norm_gains[0], norm_shifts[0]])
+        if not square():
+            own = lax.all_gather(share, (DP, CTX), axis=1, tiled=True)
+        else:
+            near = jnp.concatenate([share, swap(share, CTX)], 1)
+            own = jnp.concatenate([near, swap(near, DP)], 1)
+        return own, swap(own, SEC)
 
     def norms_of(layer):
-        chosen = jnp.where(section == layer, norms_own, norms_other).astype(F32)
+        chosen = jnp.where(section == layer, *norms).astype(F32)
         return chosen[:2], chosen[2:]
 
     last = len(parts) - 1
@@ -428,11 +508,7 @@
     def forward(layer_in, norms, finish_attn, finish_up, finish_down, jobs):
         gains, shifts = norms
 
-        def begin():
-            residual = layer_in.astype(F32)
-            return residual, normed(residual, gains[0], shifts[0]).astype(BF16)
-
-        residual, normed_a = stage(begin, *jobs[0])
+        normed_a = stage(lambda: norm(layer_in, gains[0], shifts[0]), *jobs[0])
         qkv, out = attn = finish_attn()
 
         def spread():
@@ -443,24 +519,22 @@
         packed, blocks = stage(spread, *jobs[1])
         attended, mixed_own = [], []
         for number in range(last + 1):
-            if number:
-                mixed_own.append(to_own_rows(attended[number - 1][0]))
-
             def work():
                 done = attend(packed[number], parts[number])
                 more = [to_all_rows(blocks[number])] if number < last else []
-                return done, more
-            done, more = stage(work, *(jobs[number + 2] if number < 2 else []))
+                back = [to_own_rows(attended[number - 1][0])] if number else []
+                return done, more, back
+            done, more, back = stage(work, *(jobs[number + 2] if number < 2 else []))
             attended.append(done)
             packed += more
+            mixed_own += back
         if last == 0:
             stage(lambda: (), *jobs[3])
         mixed_own = stage(lambda: mixed_own + [to_own_rows(attended[-1][0])], *jobs[4])
         mixture = join_heads(mixed_own)
-        hidden = stage(
-            lambda: residual + both_halves(dot(mixture, out, ((1,), (1,)))), *jobs[5])
-        normed_b = stage(
-            lambda: normed(hidden, gains[1], shifts[1]).astype(BF16), *jobs[6])
+        halves = stage(lambda: both_halves(dot(mixture, out, ((1,), (1,)))), *jobs[5])
+        hidden, normed_b = stage(
+            lambda: norm(layer_in, gains[1], shifts[1], *halves), *jobs[6])
         up = finish_up()
 
         def expand():
@@ -469,24 +543,22 @@
 
         pre_act, activated = stage(expand, *jobs[7])
         down = finish_down()
-        layer_out = stage(
-            lambda: (hidden + both_halves(dot(activated, down, ((1,), (1,))))).astype(BF16),
-            *jobs[8])
-        saved = (residual, normed_a, packed, attended, mixture, hidden, normed_b, pre_act)
+        own, far = stage(
+            lambda: both_halves(dot(activated, down, ((1,), (1,)))), *jobs[8])
+        layer_out = (hidden + own + far.astype(F32)).astype(BF16)
+        saved = (layer_in, normed_a, packed, attended, mixture, hidden, normed_b, pre_act, activated)
         return layer_out, saved, attn + (up, down)
 
-    def backward(tag, grad_branch, saved, norms, weights, jobs):
+    def backward(layer, grad_branch, saved, norms, weights, jobs):
         gains, shifts = norms
         qkv, out, up, down = weights
-        residual, normed_a, packed, attended, mixture, hidden, normed_b, pre_act = saved
-        grad_in = grad_branch.astype(F32)
-        down_name, up_name, attn_name = (tag + name for name in ("down", "up", "attn"))
+        layer_in, normed_a, packed, attended, mixture, hidden, normed_b, pre_act, activated = saved
 
         def first():
             grad_act = dot(grad_branch, down, ((1,), (0,)))
-            activated, gelu_back = jax.vjp(jax.nn.gelu, pre_act)
+            _, gelu_back = jax.vjp(jax.nn.gelu, pre_act)
             grad_pre = gelu_back(grad_act)[0].astype(BF16)
-            grad_down = dot(grad_branch, activated.astype(BF16), ((0,), (0,))).astype(BF16)
+            grad_down = dot(grad_branch, activated, ((0,), (0,))).astype(BF16)
             return grad_pre, grad_down
 
         grad_pre, grad_down = stage(first, *jobs[0])
@@ -498,26 +570,25 @@
         grad_second, grad_up = stage(second, *jobs[1])
 
         def third():
-            _, second_back = jax.vjp(normed, hidden, gains[1], shifts[1])
-            grad_hidden_norm, gain_later, shift_later = second_back(grad_second)
-            grad_hidden = grad_in + grad_hidden_norm
-            grad_attn = grad_hidden.astype(BF16)
+            grad_hidden, grad_attn, sums = norm_back(
+                hidden, *grad_second, grad_branch, gains[1], True)
             grad_mixture = dot(grad_attn, out, ((1,), (0,))).astype(BF16)
-            return grad_hidden, grad_attn, split_heads(grad_mixture, HEAD_DIM), gain_later, shift_later
-
-        late = hold(grad_down, grad_second)
-        grad_hidden, grad_attn, blocks, gain_later, shift_later = stage(
-            third, (down_name + "1", lambda: reduce_dp(late, 1)), *jobs[2])
+            return grad_hidden, grad_attn, split_heads(grad_mixture, HEAD_DIM), sums
+
+        late = hold(grad_down, *grad_second)
+        grad_hidden, grad_attn, blocks, later = stage(
+            third, ((DOWN, layer, SUM_1), lambda: reduce_dp(late, 1)), *jobs[2])
         after = hold(grad_down, grad_attn)
         grad_mixed, blocks = stage(
             lambda: ([to_all_rows(blocks[0])], blocks[1:]),
-            (down_name + "0", lambda: reduce_dp(after, 0)), *jobs[3])
+            ((DOWN, layer, SUM_0), lambda: reduce_dp(after, 0)), *jobs[3])
         grad_packed, returned, grad_out = [], [], None
         held_up = hold(grad_up, grad_mixed[0])
 
         def reduce_up():
             sent = reduce_dp(held_up, 1)
             return reduce_ctx(reduce_dp(held_up, 0), sent)
+
 
         for number in range(last + 1):
             if number:
@@ -534,8 +605,9 @@
             beside = jobs[5] if number == 1 else []
             if number == 0:
                 beside = [
-                    (down_name, lambda: reduce_ctx(held[down_name + "0"], held[down_name + "1"])),
-                    (up_name, reduce_up)] + list(jobs[4])
+                    ((DOWN, layer, SUM), lambda: reduce_ctx(
+                        held[DOWN, layer, SUM_0], held[DOWN, layer, SUM_1])),
+                    ((UP, layer, SUM), reduce_up)] + list(jobs[4])
             done, more, grad_out = stage(work, *beside)
             grad_packed.append(done)
             grad_mixed += more
@@ -552,26 +624,24 @@
         grad_first, grad_heads = stage(fourth, *jobs[7])
 
         def fifth():
-            _, first_back = jax.vjp(normed, residual, gains[0], shifts[0])
-            grad_input_norm, gain_early, shift_early = first_back(grad_first)
-            grad_input = (grad_hidden + grad_input_norm).astype(BF16)
-            grad_norms = jnp.stack([gain_early, gain_later, shift_early, shift_later])
-            return grad_input, grad_norms
-
-        heads_late = hold(grad_heads, grad_first)
+            grad_input, early = norm_back(
+                layer_in, *grad_first, grad_hidden, gains[0], False)
+            return grad_input, jnp.stack([early[0], later[0], early[1], later[1]])
+
+        heads_late = hold(grad_heads, *grad_first)
         grad_input, grad_norms = stage(
-            fifth, (attn_name + "1", lambda: reduce_dp(heads_late, 1)), *jobs[8])
+            fifth, ((ATTN, layer, SUM_1), lambda: reduce_dp(heads_late, 1)), *jobs[8])
         return grad_input, grad_norms, grad_heads
 
     def sum_norms(lower, upper):
         chosen = jnp.where(section == 0, lower, upper)
         if not square():
-            total = lax.psum(chosen, ("dp", "context", "tensor"))
-            place = lax.axis_index("dp") * contexts + ctx
+            total = lax.psum(chosen, (DP, CTX, TEN))
+            place = lax.axis_index(DP) * contexts + ctx
             return lax.dynamic_slice_in_dim(total, place * own_rows, own_rows, 1)
         half = width // 2
-        total = chosen[:, :half] + swap(chosen[:, half:], "dp")
-        total = total[:, :own_rows] + swap(total[:, own_rows:], "context")
+        total = chosen[:, :half] + swap(chosen[:, half:], DP)
+        total = total[:, :own_rows] + swap(total[:, own_rows:], CTX)
         return functools.reduce(jnp.add, tensor_pieces(total))
 
     def entry_half(value):
@@ -579,7 +649,7 @@
         return spread_tensor(reorder(half))
 
     def entry_rows(mine):
-        other = swap(mine, "section")
+        other = swap(mine, SEC)
         return paired(mine[:, None], other[:, None], section, 1).reshape(count, width)
 
     def exit_rows(value):
@@ -588,17 +658,26 @@
 
     def place_layers(lower, upper):
         keep = jnp.where(section == 0, lower, upper)
-        came = swap(jnp.where(section == 0, upper, lower), "section")
+        came = swap(jnp.where(section == 0, upper, lower), SEC)
         whole = paired(keep[:, None], came[:, None], section, 1)
         return whole.reshape(1, micro, 1, span, width)
 
     def own_layer(lower, upper):
         keep = jnp.where(section == 0, lower, upper)
-        came = swap(jnp.where(section == 0, upper, lower), "section")
+        came = swap(jnp.where(section == 0, upper, lower), SEC)
         return paired(keep, came, section, 0)
 
     def reduce_tensor(blocks):
-        return lax.psum_scatter(blocks, "tensor", scatter_dimension=0)
+        return lax.psum_scatter(blocks, TEN, scatter_dimension=0)
+
+    def reduce_direct(blocks):
+        count, place = tensors, lax.axis_index(TEN)
+        total = take(blocks, place).astype(F32)
+        for step in range(1, count):
+            pairs = [(n, (n + step) % count) for n in range(count)]
+            sent = take(blocks, lax.rem(place + step, count))
+            total = total + lax.ppermute(sent, TEN, pairs).astype(F32)
+        return total
 
     def hidden_shares(value):
         return value.reshape(own_rows, tensors // 2, hidden_cols).transpose(1, 0, 2)
@@ -614,104 +693,114 @@
         return jnp.concatenate(cut, 2)
 
 
-    attn_both = stage(lambda: over_tensor(attn_share))
+    attn_both, entry, norms = stage(
+        lambda: (over_tensor(attn_share), entry_half(inputs), gather_norms()))
     ffn_share = jnp.concatenate([w_up[0], rows_layout(w_down[0].T)], 1)
     norms_zero, norms_one = norms_of(0), norms_of(1)
 
     def start():
-        held["attn_kept"], held["attn_came"] = attn_both[0], swap(attn_both[1], "section")
+        held[ATTN, KEPT], held[ATTN, CAME] = attn_both[0], swap(attn_both[1], SEC)
         own = attn_layer(0)
         near = near_rows(own, True)
         full = all_rows(own, near, far_rows(own), far_rows(near))
-        return entry_half(hold(inputs, attn_both)), full
-
-    entry, attn_zero = stage(start)
-    entries = entry_rows(entry)
+        return entry_rows(entry), full, norms_zero, norms_one
+
+    entries, attn_zero, norms_zero, norms_one = stage(start)
     cut_at = qkv_cols * tensors // 2
 
     def cut(full):
         return full[:, :cut_at], full[:, cut_at:]
 
     def ffn_begin():
-        half, other = held["ffn"]
-        other = swap(other, "section")
+        half, other = over_tensor(ffn_share)
+        other = swap(other, SEC)
         made = {}
         for layer in range(2):
             mine = jnp.where(section == layer, half, other)
-            made[f"up{layer}_own"] = rows_layout(joined_columns(mine[:, :, :hidden_cols]))
-            made[f"down{layer}_own"] = rows_layout(joined_columns(mine[:, :, hidden_cols:]))
-        made["up0_near"] = near_rows(made["up0_own"])
-        made["up0_own_far"] = far_rows(made["up0_own"])
+            made[UP, layer, OWN] = rows_layout(joined_columns(mine[:, :, :hidden_cols]))
+            made[DOWN, layer, OWN] = rows_layout(joined_columns(mine[:, :, hidden_cols:]))
         return made
 
-    def near_job(name):
-        return (name + "_near", lambda: near_rows(held[name + "_own"], name == "attn1"))
-
-    def far_job(name, which):
-        return (f"{name}_{which}_far", lambda: far_rows(held[f"{name}_{which}"]))
-
-    def finish(name):
-        return lambda: all_rows(*[held[f"{name}_{end}"]
-                                  for end in ("own", "near", "own_far", "near_far")])
+    def late(value):
+        return hold(value, held[LAST])
+
+    def near_job(what, layer):
+        return (what, layer, NEAR), lambda: near_rows(late(held[what, layer, OWN]), what == ATTN)
+
+    def far_job(what, layer, state, start=late):
+        return ((what, layer, OWN_FAR if state == OWN else NEAR_FAR),
+                lambda: far_rows(start(held[what, layer, state])))
+
+    def finish(what, layer):
+        return lambda: all_rows(*[held.pop((what, layer, state))
+                                  for state in (OWN, NEAR, OWN_FAR, NEAR_FAR)])
 
     out_zero, saved_zero, weights_zero = forward(
-        entries, norms_zero, lambda: cut(attn_zero), finish("up0"), finish("down0"), [
+        entries, norms_zero, lambda: cut(attn_zero), finish(UP, 0), finish(DOWN, 0), [
             [],
-            [("ffn", lambda: over_tensor(hold(ffn_share, attn_both)))],
-            [("begin", ffn_begin)],
-            [far_job("up0", "near"), ("attn1_own", lambda: attn_layer(1))],
-            [far_job("down0", "own")],
+            [(FFN, ffn_begin)],
+            [near_job(UP, 0), far_job(UP, 0, OWN)],
+            [far_job(UP, 0, NEAR), ((ATTN, 1, OWN), lambda: attn_layer(1))],
+            [far_job(DOWN, 0, OWN)],
             [],
-            [near_job("down0"), far_job("attn1", "own")],
-            [far_job("down0", "near"), near_job("attn1")],
+            [near_job(DOWN, 0), far_job(ATTN, 1, OWN)],
+            [far_job(DOWN, 0, NEAR), near_job(ATTN, 1)],
             [],
         ])
+    held[EXIT, 0, OWN] = out_zero
     out_one, saved_one, weights_one = forward(
-        out_zero, norms_one, lambda: cut(finish("attn1")()), finish("up1"), finish("down1"), [
-            [far_job("attn1", "near")],
-            [far_job("up1", "own")],
-            [near_job("up1"), far_job("down1", "own"), ("exit0", lambda: exit_rows(out_zero))],
-            [far_job("up1", "near")],
-            [("top", lambda: entry_half(hold(cotangent, held["up1_near"])))],
+        out_zero, norms_one, lambda: cut(finish(ATTN, 1)()), finish(UP, 1), finish(DOWN, 1), [
+            [far_job(ATTN, 1, NEAR, lambda value: value)],
+            [far_job(UP, 1, OWN)],
+            [near_job(UP, 1), far_job(DOWN, 1, OWN),
+             ((EXIT, 0), lambda: exit_rows(late(held.pop((EXIT, 0, OWN)))))],
+            [far_job(UP, 1, NEAR)],
+            [((ENTRY, 1), lambda: entry_half(hold(cotangent, held[UP, 1, NEAR_FAR])))],
             [],
-            [near_job("down1")],
-            [far_job("down1", "near")],
+            [near_job(DOWN, 1)],
+            [far_job(DOWN, 1, NEAR)],
             [],
         ])
-    top_grad = entry_rows(held["top"])
+    top_grad = entry_rows(held.pop((ENTRY, 1)))
+    held[EXIT, 1, OWN] = out_one
     grad_one, norm_sum_one, grad_heads_one = backward(
-        "one_", top_grad, saved_one, norms_one, weights_one,
-        [[], [], [], [], [("exit1", lambda: exit_rows(out_one))], [], [], [], []])
-    layer_outputs = place_layers(held["exit0"], held["exit1"])
+        1, top_grad, saved_one, norms_one, weights_one, [
+            [], [], [], [], [((EXIT, 1), lambda: exit_rows(held.pop((EXIT, 1, OWN))))],
+            [], [], [], []])
+    held[EXIT, 0, OWN] = grad_one
+
+    def all_shares(what):
+        return (what, ALL), lambda: own_layer(hidden_shares(held.pop((what, 0, SUM))),
+                                              hidden_shares(held.pop((what, 1, SUM))))
+
+    def sum_shares(what):
+        return (what, DONE), lambda: reduce_tensor(held.pop((what, ALL)))
+
     grad_zero, norm_sum_zero, grad_heads_zero = backward(
-        "zero_", grad_one, saved_zero, norms_zero, weights_zero, [
-            [("one_attn0", lambda: reduce_dp(grad_heads_one, 0))],
+        0, grad_one, saved_zero, norms_zero, weights_zero, [
+            [((ATTN, 1, SUM_0), lambda: reduce_dp(grad_heads_one, 0))],
             [],
-            [("one_attn", lambda: reduce_ctx(held["one_attn0"], held["one_attn1"], True))],
+            [((ATTN, 1, SUM), lambda: reduce_ctx(
+                held[ATTN, 1, SUM_0], held[ATTN, 1, SUM_1], True))],
             [],
-            [("back1", lambda: exit_rows(grad_one))],
-            [("down_all", lambda: own_layer(hidden_shares(held["zero_down"]),
-                                            hidden_shares(held["one_down"]))),
-             ("up_all", lambda: own_layer(hidden_shares(held["zero_up"]),
-                                          hidden_shares(held["one_up"])))],
+            [((EXIT, 2), lambda: exit_rows(held.pop((EXIT, 0, OWN))))],
             [],
-            [("down_sum", lambda: reduce_tensor(held["down_all"]))],
+            [all_shares(DOWN), all_shares(UP)],
             [],
+            [sum_shares(DOWN)],
         ])
 
-    def finish_up():
-        attn_kept = reduce_dp(grad_heads_zero, 0)
-        back_zero = exit_rows(grad_zero)
-        attn_zero_sum = reduce_ctx(attn_kept, held["zero_attn1"], True)
-        attn_all = own_layer(attn_shares(attn_zero_sum), attn_shares(held["one_attn"]))
-        return (back_zero, attn_all, reduce_tensor(held["up_all"]),
-                sum_norms(norm_sum_zero, norm_sum_one))
-
-    back_zero, attn_all, grad_up, norm_sums = finish_up()
-    boundary_grads = place_layers(back_zero, held["back1"])
-    attn_total = reduce_tensor(attn_all).astype(F32)
-    grad_up = grad_up.astype(F32)
-    grad_down = held["down_sum"].astype(F32)
+    def last_rows():
+        sent = held[ATTN, 0, SUM_1]
+        return reduce_ctx(reduce_dp(grad_heads_zero, 0), sent, True), exit_rows(grad_zero)
+
+    attn_zero_sum, back_zero = stage(last_rows, sum_shares(UP))
+    attn_all = own_layer(attn_shares(attn_zero_sum), attn_shares(held[ATTN, 1, SUM]))
+    attn_total = reduce_direct(attn_all)
+    layer_outputs = place_layers(held[EXIT, 0], held[EXIT, 1])
+    boundary_grads = place_layers(back_zero, held[EXIT, 2])
+    grad_down, grad_up = held[DOWN, DONE].astype(F32).T, held[UP, DONE].astype(F32)
+    norm_sums = sum_norms(hold(norm_sum_zero, attn_all), norm_sum_one)
     grad_qkv, grad_out = attn_total[:, :qkv_cols], attn_total[:, qkv_cols:]
     cut_list, place = [], 0
     for size in (parts if fast else [1] * share_heads):
@@ -725,7 +814,7 @@
         grad_qkv[None],
         grad_out.T[None],
         grad_up[None],
-        grad_down.T[None],
+        grad_down[None],
         norm_sums[:2][None],
         norm_sums[2:][None],
     )
@@ -733,24 +822,24 @@
 
 def solution(mesh):
     in_specs = (
-        P(None, "dp", ("context", "tensor"), None),
-        P(None, "dp", ("context", "tensor"), None),
-        P("section", None, ("dp", "context"), "tensor"),
-        P("section", "tensor", ("dp", "context")),
-        P("section", ("dp", "context"), "tensor"),
-        P("section", "tensor", ("dp", "context")),
-        P("section", None, ("dp", "context")),
-        P("section", None, ("dp", "context")),
+        P(None, DP, (CTX, TEN), None),
+        P(None, DP, (CTX, TEN), None),
+        P(SEC, None, (DP, CTX), TEN),
+        P(SEC, TEN, (DP, CTX)),
+        P(SEC, (DP, CTX), TEN),
+        P(SEC, TEN, (DP, CTX)),
+        P(SEC, None, (DP, CTX)),
+        P(SEC, None, (DP, CTX)),
     )
     out_specs = (
-        P("section", None, "dp", ("context", "tensor"), None),
-        P("section", None, "dp", ("context", "tensor"), None),
-        P("section", None, ("dp", "context"), "tensor"),
-        P("section", "tensor", ("dp", "context")),
-        P("section", ("dp", "context"), "tensor"),
-        P("section", "tensor", ("dp", "context")),
-        P("section", None, ("dp", "context")),
-        P("section", None, ("dp", "context")),
+        P(SEC, None, DP, (CTX, TEN), None),
+        P(SEC, None, DP, (CTX, TEN), None),
+        P(SEC, None, (DP, CTX), TEN),
+        P(SEC, TEN, (DP, CTX)),
+        P(SEC, (DP, CTX), TEN),
+        P(SEC, TEN, (DP, CTX)),
+        P(SEC, None, (DP, CTX)),
+        P(SEC, None, (DP, CTX)),
     )
     return jax.shard_map(
         per_device, mesh=mesh, in_specs=in_specs, out_specs=out_specs, check_vma=False

time: 851 us -> 830 us (0.975)
  other arithmetic: 120 us -> 79.7 us
  Pallas kernels: 111 us -> 147 us
  local copies, waits for them, and re-layouts: 105 us -> 86.7 us
    reduce_sum x20 -> x0, other arithmetic: 40.2 us -> none  [the longest x6 16.4 us: normed(): spread = jnp.mean(center * center, -1, keepdims=True)]
    pallas_call x0 -> x8, Pallas kernels: none -> 34.7 us  [the longest x4 22.2 us: norm_back(): pl.pallas_call(functools.partial(norm_back_kernel, both), grid=(count //...]
    ppermute x19 -> x22, waiting for transfers between devices: 65.3 us -> 90.8 us  [the longest x16 55.6 us: exchanged(): moved.append(lax.ppermute(blocks[step], CTX, pairs))]
    all_gather x2, waiting for transfers between devices: 55.1 us -> 40.9 us  [over_tensor(): gathered = lax.all_gather(share, TEN)]
    ppermute x19 -> x22, starting transfers between devices: 19.8 us -> 29.1 us  [the longest x16 19.4 us: exchanged(): moved.append(lax.ppermute(blocks[step], CTX, pairs))]
    reduce_scatter x3 -> x2, waiting for transfers between devices: 9.02 us -> 0.04 us  [reduce_tensor(): return lax.psum_scatter(blocks, TEN, scatter_dimension=0)]
    unnamed x264 -> x240, local copies, waits for them, and re-layouts: 35.4 us -> 27.8 us
  transfers between devices with their start and end apart: 88 -> 90, of which waited for: 41 -> 43; matrix products, arithmetic and copies ran while one was open for 29% -> 22% of each run, Pallas kernels for 13% -> 16%
where the time goes in v3:
time: 830 us; the launch traced here: 822 us
  waiting for transfers between devices  304 us (37%)
  Pallas kernels  147 us (18%)
  starting transfers between devices  102 us (12%)
  local copies, waits for them, and re-layouts  86.7 us (10%)
  matrix products  86.6 us (10%)
  other arithmetic  79.7 us (10%)
  between operations  16.4 us (2%)
    ppermute x58, waiting for transfers between devices, swap(): return lax.ppermute(value, axis, [(0, 1), (1, 0)])  162 us
    dot_general x24, matrix products, dot(): lax.dot_general(left, right, ((contract[0], contract[1]), ((), ())), pref...  86.6 us
    pallas_call x4, Pallas kernels, attend_back(): pl.pallas_call(functools.partial(attend_back_kernel, block, heads), grid=...  64.6 us
    ppermute x16, waiting for transfers between devices, exchanged(): moved.append(lax.ppermute(blocks[step], CTX, pairs))  55.6 us
    pallas_call x4, Pallas kernels, attend(): pl.pallas_call(functools.partial(attend_kernel, block, heads), grid=(leng...  47.2 us
    ppermute x58, starting transfers between devices, swap(): return lax.ppermute(value, axis, [(0, 1), (1, 0)])  45.3 us
    all_gather x2, waiting for transfers between devices, over_tensor(): gathered = lax.all_gather(share, TEN)  40.9 us
    unnamed x240, local copies, waits for them, and re-layouts  27.8 us
  transfers between devices with their start and end apart: 90, of which 43 were waited for; matrix products, arithmetic and copies ran while one was open for 22% of the time, Pallas kernels for 16%

profile of v3, /device:TPU:0, one launch (start us, length us, event | category | flops | bytes accessed | tf_op | source)
XLA Modules:
  0.0 821.5 jit_solution(3012440313707739708)
XLA Ops:
  12.3 6.4 all-to-all-start
  26.2 32.0 %all-gather.5.cloned.1.call-done = bf16[768,768]{1,0:T(8,128)(2,1)} async-done(((bf16[192,768]{1,0:T(8,128)(2,1)}), bf16[768,768]{1,0:T(8,128)(2,1)}) %all-gather.5.cloned.1.call-update) | async-done | bytes 1179664 | tf_op jit(solution)/shard_map/all_gather | solution.py:411
  67.7 12.1 %collective-permute-done.5 = bf16[192,1536]{1,0:T(8,128)(2,1)S(1)} collective-permute-done((bf16[192,1536]{1,0:T(8,128)(2,1)}, bf16[192,1536]{1,0:T(8,128)(2,1)S(1)}, u32[]{:S(2)}, u32[]{:S(2)}) %collective-permute-start.5) | collective-permute-done | bytes 589856 | tf_op jit(solution)/shard_map/ppermute | solution.py:262
  81.9 12.6 %collective-permute-done.7 = bf16[192,1536]{1,0:T(8,128)(2,1)S(1)} collective-permute-done((bf16[192,1536]{1,0:T(8,128)(2,1)S(1)}, bf16[192,1536]{1,0:T(8,128)(2,1)S(1)}, u32[]{:S(2)}, u32[]{:S(2)}) %collective-permute-start.7) | collective-permute-done | bytes 589856 | tf_op jit(solution)/shard_map/ppermute | solution.py:262
  101.5 8.9 %all-gather.7.cloned.1.call-done = bf16[768,1536]{1,0:T(8,128)(2,1)} async-done(((bf16[192,1536]{1,0:T(8,128)(2,1)}), bf16[768,1536]{1,0:T(8,128)(2,1)}) %all-gather.7.cloned.1.call-update) | async-done | bytes 2359312 | tf_op jit(solution)/shard_map/all_gather | solution.py:411
  120.2 4.0 broadcast_select_fusion
  132.2 16.0 %attend.4 = (bf16[2048,128]{1,0:T(8,128)(2,1)S(1)}, f32[2,1,2048]{2,1,0:T(1,128)S(1)}) custom-call(bf16[2048,384]{1,0:T(8,128)(2,1)S(1)} %bitcast.345, bf16[2048,384]{1,0:T(8,128)(2,1)S(1)} %bitcast.346), custom_call_target="tpu_custom_call" | custom-call | flops 2147483648 | bytes 3145728 | tf_op jit(solution)/shard_map/attend/pallas_call | solution.py:153
  148.6 4.6 collective-permute-done.11
  163.2 7.8 attend.5
  172.3 5.8 collective-permute-done.15
  178.1 4.7 collective-permute-done.16
  185.0 4.0 fusion.100
  195.8 5.1 norm.5
  200.9 7.0 collective-permute-done.19
  213.0 7.2 fusion.21
  220.2 4.4 collective-permute-done.21
  233.3 10.3 %collective-permute-done.23 = bf16[192,1536]{1,0:T(8,128)(2,1)S(1)} collective-permute-done((bf16[192,1536]{1,0:T(8,128)(2,1)S(1)}, bf16[192,1536]{1,0:T(8,128)(2,1)S(1)}, u32[]{:S(2)}, u32[]{:S(2)}) %collective-permute-start.23) | collective-permute-done | bytes 589856 | tf_op jit(solution)/shard_map/ppermute | solution.py:262
  250.2 15.0 %collective-permute-done.24 = bf16[1024,384]{1,0:T(8,128)(2,1)S(1)} collective-permute-done((bf16[1024,384]{1,0:T(8,128)(2,1)S(1)}, bf16[1024,384]{1,0:T(8,128)(2,1)S(1)}, u32[]{:S(2)}, u32[]{:S(2)}) %collective-permute-start.24) | collective-permute-done | bytes 786464 | tf_op jit(solution)/shard_map/ppermute | solution.py:481
  267.9 4.2 all-to-all-start.1
  275.5 15.5 %attend.6 = (bf16[2048,128]{1,0:T(8,128)(2,1)S(1)}, f32[2,1,2048]{2,1,0:T(1,128)S(1)}) custom-call(bf16[2048,384]{1,0:T(8,128)(2,1)S(1)} %bitcast.349, bf16[2048,384]{1,0:T(8,128)(2,1)S(1)} %bitcast.350), custom_call_target="tpu_custom_call" | custom-call | flops 2147483648 | bytes 3145728 | tf_op jit(solution)/shard_map/attend/pallas_call | solution.py:153
  293.2 4.6 collective-permute-done.27
  303.7 7.8 attend.7
  314.4 4.9 all-to-all-start.2
  321.3 5.7 collective-permute-done.31
  326.9 9.8 %all-to-all-done.2 = bf16[4,128,768]{2,1,0:T(8,128)(2,1)} async-done(((bf16[4,128,768]{2,1,0:T(8,128)(2,1)}), bf16[4,128,768]{2,1,0:T(8,128)(2,1)}, u32[]{:S(2)}, u32[]{:S(2)}) %all-to-all-start.2) | async-done | bytes 786464 | tf_op jit(solution)/shard_map/all_to_all | solution.py:290
  339.1 4.0 fusion.102
  349.6 4.6 norm.7
  354.2 7.7 collective-permute-done.33
  368.8 8.5 %collective-permute-done.35 = bf16[192,1536]{1,0:T(8,128)(2,1)S(1)} collective-permute-done((bf16[192,1536]{1,0:T(8,128)(2,1)S(1)}, bf16[192,1536]{1,0:T(8,128)(2,1)S(1)}, u32[]{:S(2)}, u32[]{:S(2)}) %collective-permute-start.35) | collective-permute-done | bytes 589856 | tf_op jit(solution)/shard_map/ppermute | solution.py:262
  378.2 4.3 fusion.104
  382.5 4.3 fusion.108
  386.8 4.2 fusion.6
  394.4 4.4 fusion.103
  399.3 4.0 convolution_convert_fusion.4
  404.0 6.1 norm_back.4
  414.6 10.8 %collective-permute-done.37 = bf16[192,1536]{1,0:T(8,128)(2,1)S(1)} collective-permute-done((bf16[192,1536]{1,0:T(8,128)(2,1)S(1)}, bf16[192,1536]{1,0:T(8,128)(2,1)S(1)}, u32[]{:S(2)}, u32[]{:S(2)}) %collective-permute-start.37) | collective-permute-done | bytes 589856 | tf_op jit(solution)/shard_map/ppermute | solution.py:262
  430.6 4.4 all-to-all-start.3
  452.1 9.6 %collective-permute-done.43 = bf16[192,1536]{1,0:T(8,128)(2,1)S(1)} collective-permute-done((bf16[192,1536]{1,0:T(8,128)(2,1)S(1)}, bf16[192,1536]{1,0:T(8,128)(2,1)S(1)}, u32[]{:S(2)}, u32[]{:S(2)}) %collective-permute-start.43) | collective-permute-done | bytes 589856 | tf_op jit(solution)/shard_map/ppermute | solution.py:262
  464.5 21.6 %attend_back.4 = bf16[2048,384]{1,0:T(8,128)(2,1)S(1)} custom-call(bf16[2048,384]{1,0:T(8,128)(2,1)S(1)} %bitcast.351, bf16[2048,384]{1,0:T(8,128)(2,1)S(1)} %bitcast.352, bf16[2048,128]{1,0:T(8,128)(2,1)S(1)} %bitcast.373, bf16[2048,128]{1,0:T(8,128)(2,1)S(1)} %copy-done.23, f32[2,1,2048]{2,1,0:T(1,128)S(1)} %get-tuple-element.335.log_ref), custom_call_target="tpu_custom_call" | custom-call | flops 5368709120 | bytes 6291456 | tf_op jit(solution)/shard_map/attend_back/pallas_call | solution.py:235
  492.3 10.6 %attend_back.5 = bf16[2048,192]{1,0:T(8,128)(2,1)S(1)} custom-call(bf16[2048,192]{1,0:T(8,128)(2,1)S(1)} %bitcast.363, bf16[2048,192]{1,0:T(8,128)(2,1)S(1)} %bitcast.364, bf16[2048,64]{1,0:T(8,128)(2,1)S(1)} %bitcast.372, bf16[2048,64]{1,0:T(8,128)(2,1)S(1)} %copy-done.21, f32[1,1,2048]{2,1,0:T(1,128)S(1)} %get-tuple-element.347.log_ref), custom_call_target="tpu_custom_call" | custom-call | flops 2684354560 | bytes 3145728 | tf_op jit(solution)/shard_map/attend_back/pallas_call | solution.py:235
  504.3 11.7 %collective-permute-done.48 = bf16[1024,192]{1,0:T(8,128)(2,1)S(1)} collective-permute-done((bf16[1024,192]{1,0:T(8,128)(2,1)S(1)}, bf16[1024,192]{1,0:T(8,128)(2,1)S(1)}, u32[]{:S(2)}, u32[]{:S(2)}) %collective-permute-start.48) | collective-permute-done | bytes 393248 | tf_op jit(solution)/shard_map/ppermute | solution.py:481
  518.1 4.4 fusion.105
  524.4 3.9 convolution_convert_fusion.7
  534.2 5.1 norm_back.5
  539.9 4.9 collective-permute-done.50
  550.0 4.2 fusion.13
  554.3 4.0 convolution_convert_fusion.3
  560.4 4.5 fusion.106
  570.2 5.8 convolution_convert_fusion.2
  576.1 7.3 collective-permute-done.54
  584.3 6.2 norm_back.6
  593.9 11.7 %collective-permute-done.53 = bf16[192,1536]{1,0:T(8,128)(2,1)S(1)} collective-permute-done((bf16[192,1536]{1,0:T(8,128)(2,1)S(1)}, bf16[192,1536]{1,0:T(8,128)(2,1)S(1)}, u32[]{:S(2)}, u32[]{:S(2)}) %collective-permute-start.53) | collective-permute-done | bytes 589856 | tf_op jit(solution)/shard_map/ppermute | solution.py:262
  618.0 3.8 collective-permute-done.56
  632.5 9.1 %collective-permute-done.60 = bf16[192,1536]{1,0:T(8,128)(2,1)S(1)} collective-permute-done((bf16[192,1536]{1,0:T(8,128)(2,1)S(1)}, bf16[192,1536]{1,0:T(8,128)(2,1)S(1)}, u32[]{:S(2)}, u32[]{:S(2)}) %collective-permute-start.60) | collective-permute-done | bytes 589856 | tf_op jit(solution)/shard_map/ppermute | solution.py:262
  644.9 22.0 %attend_back.6 = bf16[2048,384]{1,0:T(8,128)(2,1)S(1)} custom-call(bf16[2048,384]{1,0:T(8,128)(2,1)S(1)} %bitcast.347, bf16[2048,384]{1,0:T(8,128)(2,1)S(1)} %bitcast.348, bf16[2048,128]{1,0:T(8,128)(2,1)S(1)} %bitcast.374, bf16[2048,128]{1,0:T(8,128)(2,1)S(1)} %copy-done.17, f32[2,1,2048]{2,1,0:T(1,128)S(1)} %get-tuple-element.384.log_ref), custom_call_target="tpu_custom_call" | custom-call | flops 5368709120 | bytes 6291456 | tf_op jit(solution)/shard_map/attend_back/pallas_call | solution.py:235
  675.2 10.4 %attend_back.7 = bf16[2048,192]{1,0:T(8,128)(2,1)S(1)} custom-call(bf16[2048,192]{1,0:T(8,128)(2,1)S(1)} %bitcast.359, bf16[2048,192]{1,0:T(8,128)(2,1)S(1)} %bitcast.360, bf16[2048,64]{1,0:T(8,128)(2,1)S(1)} %bitcast.371, bf16[2048,64]{1,0:T(8,128)(2,1)S(1)} %copy-done.19, f32[1,1,2048]{2,1,0:T(1,128)S(1)} %get-tuple-element.393.log_ref), custom_call_target="tpu_custom_call" | custom-call | flops 2684354560 | bytes 3145728 | tf_op jit(solution)/shard_map/attend_back/pallas_call | solution.py:235
  690.5 14.9 %collective-permute-done.63 = bf16[1024,192]{1,0:T(8,128)(2,1)} collective-permute-done((bf16[1024,192]{1,0:T(8,128)(2,1)}, bf16[1024,192]{1,0:T(8,128)(2,1)}, u32[]{:S(2)}, u32[]{:S(2)}) %collective-permute-start.63) | collective-permute-done | bytes 393248 | tf_op jit(solution)/shard_map/ppermute | solution.py:481
  710.9 5.8 fusion.107
  730.9 4.8 norm_back.7
  735.8 5.5 collective-permute-done.68
  745.6 8.0 collective-permute-done.75
  766.3 13.4 %collective-permute-done.77 = f32[4,192]{1,0:T(4,128)S(1)} collective-permute-done((f32[4,192]{1,0:T(4,128)S(1)}, f32[4,192]{1,0:T(4,128)S(1)}, u32[]{:S(2)}, u32[]{:S(2)}) %collective-permute-start.77) | collective-permute-done | bytes 3104 | tf_op jit(solution)/shard_map/ppermute | solution.py:318
  793.8 6.4 collective-permute-done.72
  800.2 12.0 %collective-permute-done.73 = bf16[192,768]{1,0:T(8,128)(2,1)S(1)} collective-permute-done((bf16[192,768]{1,0:T(8,128)(2,1)S(1)}, bf16[192,768]{1,0:T(8,128)(2,1)S(1)}, u32[]{:S(2)}, u32[]{:S(2)}) %collective-permute-start.73) | collective-permute-done | bytes 294944 | tf_op jit(solution)/shard_map/ppermute | solution.py:679
  (636 shorter events, 285.6 us)
Async XLA Ops:
  7.2 51.0 %all-gather.5.cloned.1.call-start = ((), (), s32[]{:S(2)}) async-start(), calls=%async_computation.10 | async-start | bytes 1474560 | tf_op jit(solution)/shard_map/all_gather | solution.py:411
  12.3 47.2 %all-to-all-start = ((bf16[4,128,768]{2,1,0:T(8,128)(2,1)}), bf16[4,128,768]{2,1,0:T(8,128)(2,1)S(1)}, u32[]{:S(2)}, u32[]{:S(2)}) async-start(bf16[4,128,768]{2,1,0:T(8,128)(2,1)} %maximum_select_fusion.1), calls=%async_computation | async-start | bytes 1572864 | tf_op jit(solution)/shard_map/all_to_all | solution.py:290
  18.8 91.6 %all-gather.7.cloned.1.call-start = ((), (), s32[]{:S(2)}) async-start(), calls=%async_computation.11 | async-start | bytes 2949120 | tf_op jit(solution)/shard_map/all_gather | solution.py:411
  26.2 33.3 %collective-permute-start.2 = (bf16[4,768]{1,0:T(4,128)(2,1)S(1)}, bf16[4,768]{1,0:T(4,128)(2,1)S(1)}, u32[]{:S(2)}, u32[]{:S(2)}) collective-permute-start(bf16[4,768]{1,0:T(4,128)(2,1)S(1)} %pad_maximum_fusion.39), channel_id=1, source_target_pairs={{0,16},{16,0},{1,17},{17,1},{2,18},{18,2},{3,19},{19,3},{4,20},{20... | collective-permute-start | bytes 18440 | tf_op jit(solution)/shard_map/ppermute | solution.py:262
  64.2 15.6 %collective-permute-start.5 = (bf16[192,1536]{1,0:T(8,128)(2,1)}, bf16[192,1536]{1,0:T(8,128)(2,1)S(1)}, u32[]{:S(2)}, u32[]{:S(2)}) collective-permute-start(bf16[192,1536]{1,0:T(8,128)(2,1)} %concatenate.372), channel_id=1, source_target_pairs={{0,4},{4,0},{1,5},{5,1},{2,6},{6,2},{3,7},{7,3},{8,12},{12,8},{9,1... | collective-permute-start | bytes 1769480 | tf_op jit(solution)/shard_map/ppermute | solution.py:262
  65.7 15.6 %collective-permute-start.3 = (bf16[4,128,768]{2,1,0:T(8,128)(2,1)S(1)}, bf16[4,128,768]{2,1,0:T(8,128)(2,1)S(1)}, u32[]{:S(2)}, u32[]{:S(2)}) collective-permute-start(bf16[4,128,768]{2,1,0:T(8,128)(2,1)S(1)} %all-to-all-done), channel_id=1, source_target_pairs={{0,16},{16,0},{1,17},{17,1},{2,18},{18,2},{3,19},{19,3},{4,20},{20... | collective-permute-start | bytes 2359304 | tf_op jit(solution)/shard_map/ppermute | solution.py:262
  66.1 15.8 %collective-permute-start.6 = (bf16[192,1536]{1,0:T(8,128)(2,1)S(1)}, bf16[192,1536]{1,0:T(8,128)(2,1)S(1)}, u32[]{:S(2)}, u32[]{:S(2)}) collective-permute-start(bf16[192,1536]{1,0:T(8,128)(2,1)S(1)} %concatenate.371), channel_id=1, source_target_pairs={{0,8},{8,0},{1,9},{9,1},{2,10},{10,2},{3,11},{11,3},{4,12},{12,4},... | collective-permute-start | bytes 1769480 | tf_op jit(solution)/shard_map/ppermute | solution.py:262
  79.8 14.7 %collective-permute-start.7 = (bf16[192,1536]{1,0:T(8,128)(2,1)S(1)}, bf16[192,1536]{1,0:T(8,128)(2,1)S(1)}, u32[]{:S(2)}, u32[]{:S(2)}) collective-permute-start(bf16[192,1536]{1,0:T(8,128)(2,1)S(1)} %collective-permute-done.5), channel_id=1, source_target_pairs={{0,8},{8,0},{1,9},{9,1},{2,10},{10,2},{3,11},{11,3},{4,12},{12,4},... | collective-permute-start | bytes 1769480 | tf_op jit(solution)/shard_map/ppermute | solution.py:262
  100.1 18.5 %collective-permute-start.8 = (bf16[1024,384]{1,0:T(8,128)(2,1)}, bf16[1024,384]{1,0:T(8,128)(2,1)}, u32[]{:S(2)}, u32[]{:S(2)}) collective-permute-start(bf16[1024,384]{1,0:T(8,128)(2,1)} %slice.822), channel_id=1, source_target_pairs={{0,4},{4,0},{1,5},{5,1},{2,6},{6,2},{3,7},{7,3},{8,12},{12,8},{9,1... | collective-permute-start | bytes 2359304 | tf_op jit(solution)/shard_map/ppermute | solution.py:481
  128.7 19.6 %collective-permute-start.10 = (bf16[1024,192]{1,0:T(8,128)(2,1)S(1)}, bf16[1024,192]{1,0:T(8,128)(2,1)S(1)}, u32[]{:S(2)}, u32[]{:S(2)}) collective-permute-start(bf16[1024,192]{1,0:T(8,128)(2,1)S(1)} %get-tuple-element.231), channel_id=1, source_target_pairs={{0,4},{4,0},{1,5},{5,1},{2,6},{6,2},{3,7},{7,3},{8,12},{12,8},{9,1... | collective-permute-start | bytes 1179656 | tf_op jit(solution)/shard_map/ppermute | solution.py:481
  130.0 23.2 %collective-permute-start.11 = (bf16[192,1536]{1,0:T(8,128)(2,1)S(1)}, bf16[192,1536]{1,0:T(8,128)(2,1)}, u32[]{:S(2)}, u32[]{:S(2)}) collective-permute-start(bf16[192,1536]{1,0:T(8,128)(2,1)S(1)} %bitcast.393), channel_id=1, source_target_pairs={{0,4},{4,0},{1,5},{5,1},{2,6},{6,2},{3,7},{7,3},{8,12},{12,8},{9,1... | collective-permute-start | bytes 1769480 | tf_op jit(solution)/shard_map/ppermute | solution.py:262
  130.7 22.5 %collective-permute-start.12 = (bf16[192,1536]{1,0:T(8,128)(2,1)S(1)}, bf16[192,1536]{1,0:T(8,128)(2,1)S(1)}, u32[]{:S(2)}, u32[]{:S(2)}) collective-permute-start(bf16[192,1536]{1,0:T(8,128)(2,1)S(1)} %bitcast.394), channel_id=1, source_target_pairs={{0,8},{8,0},{1,9},{9,1},{2,10},{10,2},{3,11},{11,3},{4,12},{12,4},... | collective-permute-start | bytes 1769480 | tf_op jit(solution)/shard_map/ppermute | solution.py:262
  154.0 17.0 %collective-permute-start.14 = (bf16[192,1536]{1,0:T(8,128)(2,1)}, bf16[192,1536]{1,0:T(8,128)(2,1)}, u32[]{:S(2)}, u32[]{:S(2)}) collective-permute-start(bf16[192,1536]{1,0:T(8,128)(2,1)} %collective-permute-done.11), channel_id=1, source_target_pairs={{0,8},{8,0},{1,9},{9,1},{2,10},{10,2},{3,11},{11,3},{4,12},{12,4},... | collective-permute-start | bytes 1769480 | tf_op jit(solution)/shard_map/ppermute | solution.py:262
  192.5 15.4 %collective-permute-start.19 = (bf16[192,1536]{1,0:T(8,128)(2,1)S(1)}, bf16[192,1536]{1,0:T(8,128)(2,1)S(1)}, u32[]{:S(2)}, u32[]{:S(2)}) collective-permute-start(bf16[192,1536]{1,0:T(8,128)(2,1)S(1)} %copy-done.38), channel_id=1, source_target_pairs={{0,8},{8,0},{1,9},{9,1},{2,10},{10,2},{3,11},{11,3},{4,12},{12,4},... | collective-permute-start | bytes 1769480 | tf_op jit(solution)/shard_map/ppermute | solution.py:262
  193.1 15.1 %collective-permute-start.18 = (bf16[192,1536]{1,0:T(8,128)(2,1)S(1)}, bf16[192,1536]{1,0:T(8,128)(2,1)S(1)}, u32[]{:S(2)}, u32[]{:S(2)}) collective-permute-start(bf16[192,1536]{1,0:T(8,128)(2,1)S(1)} %bitcast.392), channel_id=1, source_target_pairs={{0,4},{4,0},{1,5},{5,1},{2,6},{6,2},{3,7},{7,3},{8,12},{12,8},{9,1... | collective-permute-start | bytes 1769480 | tf_op jit(solution)/shard_map/ppermute | solution.py:262
  210.2 14.4 %collective-permute-start.21 = (bf16[192,1536]{1,0:T(8,128)(2,1)S(1)}, bf16[192,1536]{1,0:T(8,128)(2,1)S(1)}, u32[]{:S(2)}, u32[]{:S(2)}) collective-permute-start(bf16[192,1536]{1,0:T(8,128)(2,1)S(1)} %concatenate.382), channel_id=1, source_target_pairs={{0,4},{4,0},{1,5},{5,1},{2,6},{6,2},{3,7},{7,3},{8,12},{12,8},{9,1... | collective-permute-start | bytes 1769480 | tf_op jit(solution)/shard_map/ppermute | solution.py:262
  210.7 14.2 %collective-permute-start.20 = (bf16[192,1536]{1,0:T(8,128)(2,1)}, bf16[192,1536]{1,0:T(8,128)(2,1)S(1)}, u32[]{:S(2)}, u32[]{:S(2)}) collective-permute-start(bf16[192,1536]{1,0:T(8,128)(2,1)} %copy-done.84), channel_id=1, source_target_pairs={{0,8},{8,0},{1,9},{9,1},{2,10},{10,2},{3,11},{11,3},{4,12},{12,4},... | collective-permute-start | bytes 1769480 | tf_op jit(solution)/shard_map/ppermute | solution.py:262
  227.8 15.8 %collective-permute-start.23 = (bf16[192,1536]{1,0:T(8,128)(2,1)S(1)}, bf16[192,1536]{1,0:T(8,128)(2,1)S(1)}, u32[]{:S(2)}, u32[]{:S(2)}) collective-permute-start(bf16[192,1536]{1,0:T(8,128)(2,1)S(1)} %collective-permute-done.21), channel_id=1, source_target_pairs={{0,8},{8,0},{1,9},{9,1},{2,10},{10,2},{3,11},{11,3},{4,12},{12,4},... | collective-permute-start | bytes 1769480 | tf_op jit(solution)/shard_map/ppermute | solution.py:262
  246.0 19.2 %collective-permute-start.24 = (bf16[1024,384]{1,0:T(8,128)(2,1)S(1)}, bf16[1024,384]{1,0:T(8,128)(2,1)S(1)}, u32[]{:S(2)}, u32[]{:S(2)}) collective-permute-start(bf16[1024,384]{1,0:T(8,128)(2,1)S(1)} %slice.841), channel_id=1, source_target_pairs={{0,4},{4,0},{1,5},{5,1},{2,6},{6,2},{3,7},{7,3},{8,12},{12,8},{9,1... | collective-permute-start | bytes 2359304 | tf_op jit(solution)/shard_map/ppermute | solution.py:481
  247.7 17.9 %collective-permute-start.25 = (bf16[192,1536]{1,0:T(8,128)(2,1)S(1)}, bf16[192,1536]{1,0:T(8,128)(2,1)S(1)}, u32[]{:S(2)}, u32[]{:S(2)}) collective-permute-start(bf16[192,1536]{1,0:T(8,128)(2,1)S(1)} %bitcast.388), channel_id=1, source_target_pairs={{0,8},{8,0},{1,9},{9,1},{2,10},{10,2},{3,11},{11,3},{4,12},{12,4},... | collective-permute-start | bytes 1769480 | tf_op jit(solution)/shard_map/ppermute | solution.py:262
  267.9 29.9 %all-to-all-start.1 = ((bf16[4,128,768]{2,1,0:T(8,128)(2,1)}), bf16[4,128,768]{2,1,0:T(8,128)(2,1)}, u32[]{:S(2)}, u32[]{:S(2)}) async-start(bf16[4,128,768]{2,1,0:T(8,128)(2,1)} %maximum_select_fusion.3), calls=%async_computation.1 | async-start | bytes 1572864 | tf_op jit(solution)/shard_map/all_to_all | solution.py:290
  272.1 19.8 %collective-permute-start.26 = (bf16[1024,192]{1,0:T(8,128)(2,1)}, bf16[1024,192]{1,0:T(8,128)(2,1)S(1)}, u32[]{:S(2)}, u32[]{:S(2)}) collective-permute-start(bf16[1024,192]{1,0:T(8,128)(2,1)} %get-tuple-element.282), channel_id=1, source_target_pairs={{0,4},{4,0},{1,5},{5,1},{2,6},{6,2},{3,7},{7,3},{8,12},{12,8},{9,1... | collective-permute-start | bytes 1179656 | tf_op jit(solution)/shard_map/ppermute | solution.py:481
  273.8 19.3 %collective-permute-start.28 = (bf16[192,1536]{1,0:T(8,128)(2,1)}, bf16[192,1536]{1,0:T(8,128)(2,1)}, u32[]{:S(2)}, u32[]{:S(2)}) collective-permute-start(bf16[192,1536]{1,0:T(8,128)(2,1)} %bitcast.384), channel_id=1, source_target_pairs={{0,8},{8,0},{1,9},{9,1},{2,10},{10,2},{3,11},{11,3},{4,12},{12,4},... | collective-permute-start | bytes 1769480 | tf_op jit(solution)/shard_map/ppermute | solution.py:262
  275.1 22.6 %collective-permute-start.27 = (bf16[192,1536]{1,0:T(8,128)(2,1)}, bf16[192,1536]{1,0:T(8,128)(2,1)}, u32[]{:S(2)}, u32[]{:S(2)}) collective-permute-start(bf16[192,1536]{1,0:T(8,128)(2,1)} %bitcast.387), channel_id=1, source_target_pairs={{0,4},{4,0},{1,5},{5,1},{2,6},{6,2},{3,7},{7,3},{8,12},{12,8},{9,1... | collective-permute-start | bytes 1769480 | tf_op jit(solution)/shard_map/ppermute | solution.py:262
  314.4 22.4 %all-to-all-start.2 = ((bf16[4,128,768]{2,1,0:T(8,128)(2,1)}), bf16[4,128,768]{2,1,0:T(8,128)(2,1)}, u32[]{:S(2)}, u32[]{:S(2)}) async-start(bf16[4,128,768]{2,1,0:T(8,128)(2,1)} %maximum_select_fusion.5), calls=%async_computation.2 | async-start | bytes 1572864 | tf_op jit(solution)/shard_map/all_to_all | solution.py:290
  346.5 15.4 %collective-permute-start.33 = (bf16[192,1536]{1,0:T(8,128)(2,1)S(1)}, bf16[192,1536]{1,0:T(8,128)(2,1)S(1)}, u32[]{:S(2)}, u32[]{:S(2)}) collective-permute-start(bf16[192,1536]{1,0:T(8,128)(2,1)S(1)} %bitcast.386), channel_id=1, source_target_pairs={{0,4},{4,0},{1,5},{5,1},{2,6},{6,2},{3,7},{7,3},{8,12},{12,8},{9,1... | collective-permute-start | bytes 1769480 | tf_op jit(solution)/shard_map/ppermute | solution.py:262
  362.7 14.5 %collective-permute-start.35 = (bf16[192,1536]{1,0:T(8,128)(2,1)S(1)}, bf16[192,1536]{1,0:T(8,128)(2,1)S(1)}, u32[]{:S(2)}, u32[]{:S(2)}) collective-permute-start(bf16[192,1536]{1,0:T(8,128)(2,1)S(1)} %collective-permute-done.33), channel_id=1, source_target_pairs={{0,8},{8,0},{1,9},{9,1},{2,10},{10,2},{3,11},{11,3},{4,12},{12,4},... | collective-permute-start | bytes 1769480 | tf_op jit(solution)/shard_map/ppermute | solution.py:262
  382.5 20.8 %collective-permute-start.45 = (bf16[1024,768]{1,0:T(8,128)(2,1)S(1)}, bf16[1024,768]{1,0:T(8,128)(2,1)S(1)}, u32[]{:S(2)}, u32[]{:S(2)}) collective-permute-start(bf16[1024,768]{1,0:T(8,128)(2,1)S(1)} %get-tuple-element.671), channel_id=1, source_target_pairs={{0,16},{16,0},{1,17},{17,1},{2,18},{18,2},{3,19},{19,3},{4,20},{20... | collective-permute-start | bytes 4718600 | tf_op jit(solution)/shard_map/ppermute | solution.py:262
  410.1 15.3 %collective-permute-start.37 = (bf16[192,1536]{1,0:T(8,128)(2,1)S(1)}, bf16[192,1536]{1,0:T(8,128)(2,1)S(1)}, u32[]{:S(2)}, u32[]{:S(2)}) collective-permute-start(bf16[192,1536]{1,0:T(8,128)(2,1)S(1)} %slice.705), channel_id=1, source_target_pairs={{0,8},{8,0},{1,9},{9,1},{2,10},{10,2},{3,11},{11,3},{4,12},{12,4},... | collective-permute-start | bytes 1769480 | tf_op jit(solution)/shard_map/ppermute | solution.py:262
  427.2 14.7 %collective-permute-start.39 = (bf16[192,1536]{1,0:T(8,128)(2,1)}, bf16[192,1536]{1,0:T(8,128)(2,1)}, u32[]{:S(2)}, u32[]{:S(2)}) collective-permute-start(bf16[192,1536]{1,0:T(8,128)(2,1)} %slice.707), channel_id=1, source_target_pairs={{0,8},{8,0},{1,9},{9,1},{2,10},{10,2},{3,11},{11,3},{4,12},{12,4},... | collective-permute-start | bytes 1769480 | tf_op jit(solution)/shard_map/ppermute | solution.py:262
  430.6 60.2 %all-to-all-start.3 = ((bf16[4,128,768]{2,1,0:T(8,128)(2,1)}), bf16[4,128,768]{2,1,0:T(8,128)(2,1)}, u32[]{:S(2)}, u32[]{:S(2)}) async-start(bf16[4,128,768]{2,1,0:T(8,128)(2,1)} %maximum_select_fusion.7), calls=%async_computation.3 | async-start | bytes 1572864 | tf_op jit(solution)/shard_map/all_to_all | solution.py:290
  435.0 15.1 %collective-permute-start.41 = (bf16[192,1536]{1,0:T(8,128)(2,1)}, bf16[192,1536]{1,0:T(8,128)(2,1)}, u32[]{:S(2)}, u32[]{:S(2)}) collective-permute-start(bf16[192,1536]{1,0:T(8,128)(2,1)} %add_convert_fusion.19), channel_id=1, source_target_pairs={{0,4},{4,0},{1,5},{5,1},{2,6},{6,2},{3,7},{7,3},{8,12},{12,8},{9,1... | collective-permute-start | bytes 1769480 | tf_op jit(solution)/shard_map/ppermute | solution.py:262
  445.5 16.3 %collective-permute-start.43 = (bf16[192,1536]{1,0:T(8,128)(2,1)S(1)}, bf16[192,1536]{1,0:T(8,128)(2,1)S(1)}, u32[]{:S(2)}, u32[]{:S(2)}) collective-permute-start(bf16[192,1536]{1,0:T(8,128)(2,1)S(1)} %get-tuple-element.471), channel_id=1, source_target_pairs={{0,8},{8,0},{1,9},{9,1},{2,10},{10,2},{3,11},{11,3},{4,12},{12,4},... | collective-permute-start | bytes 1769480 | tf_op jit(solution)/shard_map/ppermute | solution.py:262
  448.0 40.3 %collective-permute-start.42 = (bf16[192,1536]{1,0:T(8,128)(2,1)}, bf16[192,1536]{1,0:T(8,128)(2,1)}, u32[]{:S(2)}, u32[]{:S(2)}) collective-permute-start(bf16[192,1536]{1,0:T(8,128)(2,1)} %get-tuple-element.470), channel_id=1, source_target_pairs={{0,8},{8,0},{1,9},{9,1},{2,10},{10,2},{3,11},{11,3},{4,12},{12,4},... | collective-permute-start | bytes 1769480 | tf_op jit(solution)/shard_map/ppermute | solution.py:262
  449.3 37.9 %collective-permute-start.40 = (bf16[1024,64]{0,1:T(8,128)(2,1)S(1)}, bf16[1024,64]{0,1:T(8,128)(2,1)S(1)}, u32[]{:S(2)}, u32[]{:S(2)}) collective-permute-start(bf16[1024,64]{0,1:T(8,128)(2,1)S(1)} %copy-done.99), channel_id=1, source_target_pairs={{0,4},{4,0},{1,5},{5,1},{2,6},{6,2},{3,7},{7,3},{8,12},{12,8},{9,1... | collective-permute-start | bytes 393224 | tf_op jit(solution)/shard_map/ppermute | solution.py:481
  463.8 24.6 %collective-permute-start.44 = (bf16[192,1536]{1,0:T(8,128)(2,1)}, bf16[192,1536]{1,0:T(8,128)(2,1)}, u32[]{:S(2)}, u32[]{:S(2)}) collective-permute-start(bf16[192,1536]{1,0:T(8,128)(2,1)} %add_convert_fusion.15), channel_id=1, source_target_pairs={{0,4},{4,0},{1,5},{5,1},{2,6},{6,2},{3,7},{7,3},{8,12},{12,8},{9,1... | collective-permute-start | bytes 1769480 | tf_op jit(solution)/shard_map/ppermute | solution.py:262
  491.0 25.0 %collective-permute-start.47 = (bf16[1024,384]{1,0:T(8,128)(2,1)S(1)}, bf16[1024,384]{1,0:T(8,128)(2,1)S(1)}, u32[]{:S(2)}, u32[]{:S(2)}) collective-permute-start(bf16[1024,384]{1,0:T(8,128)(2,1)S(1)} %get-tuple-element.484), channel_id=1, source_target_pairs={{0,4},{4,0},{1,5},{5,1},{2,6},{6,2},{3,7},{7,3},{8,12},{12,8},{9,1... | collective-permute-start | bytes 2359304 | tf_op jit(solution)/shard_map/ppermute | solution.py:481
  528.5 16.2 %collective-permute-start.50 = (bf16[192,1536]{1,0:T(8,128)(2,1)S(1)}, bf16[192,1536]{1,0:T(8,128)(2,1)S(1)}, u32[]{:S(2)}, u32[]{:S(2)}) collective-permute-start(bf16[192,1536]{1,0:T(8,128)(2,1)S(1)} %slice.723), channel_id=1, source_target_pairs={{0,8},{8,0},{1,9},{9,1},{2,10},{10,2},{3,11},{11,3},{4,12},{12,4},... | collective-permute-start | bytes 1769480 | tf_op jit(solution)/shard_map/ppermute | solution.py:262
  533.5 24.8 %collective-permute-start.51 = (bf16[192,1536]{1,0:T(8,128)(2,1)}, bf16[192,1536]{1,0:T(8,128)(2,1)}, u32[]{:S(2)}, u32[]{:S(2)}) collective-permute-start(bf16[192,1536]{1,0:T(8,128)(2,1)} %slice.725), channel_id=1, source_target_pairs={{0,8},{8,0},{1,9},{9,1},{2,10},{10,2},{3,11},{11,3},{4,12},{12,4},... | collective-permute-start | bytes 1769480 | tf_op jit(solution)/shard_map/ppermute | solution.py:262
  564.9 19.4 %collective-permute-start.52 = (bf16[1024,768]{1,0:T(8,128)(2,1)}, bf16[1024,768]{1,0:T(8,128)(2,1)S(1)}, u32[]{:S(2)}, u32[]{:S(2)}) collective-permute-start(bf16[1024,768]{1,0:T(8,128)(2,1)} %get-tuple-element.675), channel_id=1, source_target_pairs={{0,16},{16,0},{1,17},{17,1},{2,18},{18,2},{3,19},{19,3},{4,20},{20... | collective-permute-start | bytes 4718600 | tf_op jit(solution)/shard_map/ppermute | solution.py:262
  567.4 15.9 %collective-permute-start.54 = (bf16[192,1536]{1,0:T(8,128)(2,1)}, bf16[192,1536]{1,0:T(8,128)(2,1)S(1)}, u32[]{:S(2)}, u32[]{:S(2)}) collective-permute-start(bf16[192,1536]{1,0:T(8,128)(2,1)} %concatenate.406), channel_id=1, source_target_pairs={{0,4},{4,0},{1,5},{5,1},{2,6},{6,2},{3,7},{7,3},{8,12},{12,8},{9,1... | collective-permute-start | bytes 1769480 | tf_op jit(solution)/shard_map/ppermute | solution.py:262
  590.6 15.0 %collective-permute-start.53 = (bf16[192,1536]{1,0:T(8,128)(2,1)S(1)}, bf16[192,1536]{1,0:T(8,128)(2,1)S(1)}, u32[]{:S(2)}, u32[]{:S(2)}) collective-permute-start(bf16[192,1536]{1,0:T(8,128)(2,1)S(1)} %slice.731), channel_id=1, source_target_pairs={{0,8},{8,0},{1,9},{9,1},{2,10},{10,2},{3,11},{11,3},{4,12},{12,4},... | collective-permute-start | bytes 1769480 | tf_op jit(solution)/shard_map/ppermute | solution.py:262
  607.4 14.4 %collective-permute-start.56 = (bf16[192,1536]{1,0:T(8,128)(2,1)}, bf16[192,1536]{1,0:T(8,128)(2,1)}, u32[]{:S(2)}, u32[]{:S(2)}) collective-permute-start(bf16[192,1536]{1,0:T(8,128)(2,1)} %slice.741), channel_id=1, source_target_pairs={{0,8},{8,0},{1,9},{9,1},{2,10},{10,2},{3,11},{11,3},{4,12},{12,4},... | collective-permute-start | bytes 1769480 | tf_op jit(solution)/shard_map/ppermute | solution.py:262
  610.6 59.1 %all-to-all-start.4 = ((bf16[4,128,768]{2,1,0:T(8,128)(2,1)}), bf16[4,128,768]{2,1,0:T(8,128)(2,1)S(1)}, u32[]{:S(2)}, u32[]{:S(2)}) async-start(bf16[4,128,768]{2,1,0:T(8,128)(2,1)} %maximum_select_fusion.9), calls=%async_computation.4 | async-start | bytes 1572864 | tf_op jit(solution)/shard_map/all_to_all | solution.py:290
  614.1 128.5 %reduce-scatter.3.cloned.1.call-start = ((), (), s32[]{:S(2)}) async-start(), calls=%async_computation.8 | async-start | bytes 1474560 | tf_op jit(solution)/shard_map/reduce_scatter | solution.py:671
  614.2 16.2 %collective-permute-start.58 = (bf16[192,1536]{1,0:T(8,128)(2,1)}, bf16[192,1536]{1,0:T(8,128)(2,1)}, u32[]{:S(2)}, u32[]{:S(2)}) collective-permute-start(bf16[192,1536]{1,0:T(8,128)(2,1)} %add_convert_fusion.11), channel_id=1, source_target_pairs={{0,4},{4,0},{1,5},{5,1},{2,6},{6,2},{3,7},{7,3},{8,12},{12,8},{9,1... | collective-permute-start | bytes 1769480 | tf_op jit(solution)/shard_map/ppermute | solution.py:262
  625.3 16.3 %collective-permute-start.60 = (bf16[192,1536]{1,0:T(8,128)(2,1)S(1)}, bf16[192,1536]{1,0:T(8,128)(2,1)S(1)}, u32[]{:S(2)}, u32[]{:S(2)}) collective-permute-start(bf16[192,1536]{1,0:T(8,128)(2,1)S(1)} %get-tuple-element.467), channel_id=1, source_target_pairs={{0,8},{8,0},{1,9},{9,1},{2,10},{10,2},{3,11},{11,3},{4,12},{12,4},... | collective-permute-start | bytes 1769480 | tf_op jit(solution)/shard_map/ppermute | solution.py:262
  628.5 38.8 %collective-permute-start.59 = (bf16[192,1536]{1,0:T(8,128)(2,1)}, bf16[192,1536]{1,0:T(8,128)(2,1)}, u32[]{:S(2)}, u32[]{:S(2)}) collective-permute-start(bf16[192,1536]{1,0:T(8,128)(2,1)} %get-tuple-element.466), channel_id=1, source_target_pairs={{0,8},{8,0},{1,9},{9,1},{2,10},{10,2},{3,11},{11,3},{4,12},{12,4},... | collective-permute-start | bytes 1769480 | tf_op jit(solution)/shard_map/ppermute | solution.py:262
  629.2 37.7 %collective-permute-start.57 = (bf16[1024,64]{0,1:T(8,128)(2,1)S(1)}, bf16[1024,64]{0,1:T(8,128)(2,1)S(1)}, u32[]{:S(2)}, u32[]{:S(2)}) collective-permute-start(bf16[1024,64]{0,1:T(8,128)(2,1)S(1)} %get-tuple-element.386), channel_id=1, source_target_pairs={{0,4},{4,0},{1,5},{5,1},{2,6},{6,2},{3,7},{7,3},{8,12},{12,8},{9,1... | collective-permute-start | bytes 393224 | tf_op jit(solution)/shard_map/ppermute | solution.py:481
  643.6 23.7 %collective-permute-start.61 = (bf16[192,1536]{1,0:T(8,128)(2,1)}, bf16[192,1536]{1,0:T(8,128)(2,1)}, u32[]{:S(2)}, u32[]{:S(2)}) collective-permute-start(bf16[192,1536]{1,0:T(8,128)(2,1)} %add_convert_fusion.6), channel_id=1, source_target_pairs={{0,4},{4,0},{1,5},{5,1},{2,6},{6,2},{3,7},{7,3},{8,12},{12,8},{9,1... | collective-permute-start | bytes 1769480 | tf_op jit(solution)/shard_map/ppermute | solution.py:262
  671.4 16.5 %collective-permute-start.64 = (bf16[2,192,768]{2,1,0:T(8,128)(2,1)S(1)}, bf16[2,192,768]{2,1,0:T(8,128)(2,1)S(1)}, u32[]{:S(2)}, u32[]{:S(2)}) collective-permute-start(bf16[2,192,768]{2,1,0:T(8,128)(2,1)S(1)} %bitcast.413), channel_id=1, source_target_pairs={{0,16},{16,0},{1,17},{17,1},{2,18},{18,2},{3,19},{19,3},{4,20},{20... | collective-permute-start | bytes 1769480 | tf_op jit(solution)/shard_map/ppermute | solution.py:262
  671.8 16.2 %collective-permute-start.65 = (bf16[2,192,768]{2,1,0:T(8,128)(2,1)S(1)}, bf16[2,192,768]{2,1,0:T(8,128)(2,1)S(1)}, u32[]{:S(2)}, u32[]{:S(2)}) collective-permute-start(bf16[2,192,768]{2,1,0:T(8,128)(2,1)S(1)} %bitcast.414), channel_id=1, source_target_pairs={{0,16},{16,0},{1,17},{17,1},{2,18},{18,2},{3,19},{19,3},{4,20},{20... | collective-permute-start | bytes 1769480 | tf_op jit(solution)/shard_map/ppermute | solution.py:262
  674.5 30.8 %collective-permute-start.62 = (bf16[1024,384]{1,0:T(8,128)(2,1)}, bf16[1024,384]{1,0:T(8,128)(2,1)}, u32[]{:S(2)}, u32[]{:S(2)}) collective-permute-start(bf16[1024,384]{1,0:T(8,128)(2,1)} %get-tuple-element.482), channel_id=1, source_target_pairs={{0,4},{4,0},{1,5},{5,1},{2,6},{6,2},{3,7},{7,3},{8,12},{12,8},{9,1... | collective-permute-start | bytes 2359304 | tf_op jit(solution)/shard_map/ppermute | solution.py:481
  686.7 18.6 %collective-permute-start.63 = (bf16[1024,192]{1,0:T(8,128)(2,1)}, bf16[1024,192]{1,0:T(8,128)(2,1)}, u32[]{:S(2)}, u32[]{:S(2)}) collective-permute-start(bf16[1024,192]{1,0:T(8,128)(2,1)} %get-tuple-element.509), channel_id=1, source_target_pairs={{0,4},{4,0},{1,5},{5,1},{2,6},{6,2},{3,7},{7,3},{8,12},{12,8},{9,1... | collective-permute-start | bytes 1179656 | tf_op jit(solution)/shard_map/ppermute | solution.py:481
  709.6 75.1 %reduce-scatter.5.cloned.1.call-start = ((), (), s32[]{:S(2)}) async-start(), calls=%async_computation.9 | async-start | bytes 1474560 | tf_op jit(solution)/shard_map/reduce_scatter | solution.py:671
  724.8 16.4 %collective-permute-start.68 = (bf16[192,1536]{1,0:T(8,128)(2,1)}, bf16[192,1536]{1,0:T(8,128)(2,1)}, u32[]{:S(2)}, u32[]{:S(2)}) collective-permute-start(bf16[192,1536]{1,0:T(8,128)(2,1)} %slice.759), channel_id=1, source_target_pairs={{0,8},{8,0},{1,9},{9,1},{2,10},{10,2},{3,11},{11,3},{4,12},{12,4},... | collective-permute-start | bytes 1769480 | tf_op jit(solution)/shard_map/ppermute | solution.py:262
  728.1 55.0 %collective-permute-start.67 = (bf16[192,1536]{1,0:T(8,128)(2,1)}, bf16[192,1536]{1,0:T(8,128)(2,1)}, u32[]{:S(2)}, u32[]{:S(2)}) collective-permute-start(bf16[192,1536]{1,0:T(8,128)(2,1)} %slice.753), channel_id=1, source_target_pairs={{0,8},{8,0},{1,9},{9,1},{2,10},{10,2},{3,11},{11,3},{4,12},{12,4},... | collective-permute-start | bytes 1769480 | tf_op jit(solution)/shard_map/ppermute | solution.py:262
  754.4 30.2 %all-to-all-start.5 = ((bf16[4,128,768]{2,1,0:T(8,128)(2,1)}), bf16[4,128,768]{2,1,0:T(8,128)(2,1)S(1)}, u32[]{:S(2)}, u32[]{:S(2)}) async-start(bf16[4,128,768]{2,1,0:T(8,128)(2,1)} %maximum_select_fusion.11), calls=%async_computation.6 | async-start | bytes 1572864 | tf_op jit(solution)/shard_map/all_to_all | solution.py:290
  758.3 24.8 %collective-permute-start.69 = (bf16[192,1536]{1,0:T(8,128)(2,1)S(1)}, bf16[192,1536]{1,0:T(8,128)(2,1)S(1)}, u32[]{:S(2)}, u32[]{:S(2)}) collective-permute-start(bf16[192,1536]{1,0:T(8,128)(2,1)S(1)} %concatenate.417), channel_id=1, source_target_pairs={{0,4},{4,0},{1,5},{5,1},{2,6},{6,2},{3,7},{7,3},{8,12},{12,8},{9,1... | collective-permute-start | bytes 1769480 | tf_op jit(solution)/shard_map/ppermute | solution.py:262
  759.6 20.1 %collective-permute-start.77 = (f32[4,192]{1,0:T(4,128)S(1)}, f32[4,192]{1,0:T(4,128)S(1)}, u32[]{:S(2)}, u32[]{:S(2)}) collective-permute-start(f32[4,192]{1,0:T(4,128)S(1)} %slice_add_fusion.1), channel_id=1, source_target_pairs={{0,1},{1,2},{2,3},{3,0},{4,5},{5,6},{6,7},{7,4},{8,9},{9,10},{10,1... | collective-permute-start | bytes 9224 | tf_op jit(solution)/shard_map/ppermute | solution.py:318
  761.6 21.5 %collective-permute-start.78 = (f32[4,192]{1,0:T(4,128)S(1)}, f32[4,192]{1,0:T(4,128)S(1)}, u32[]{:S(2)}, u32[]{:S(2)}) collective-permute-start(f32[4,192]{1,0:T(4,128)S(1)} %slice_add_fusion.1), channel_id=1, source_target_pairs={{0,2},{1,3},{2,0},{3,1},{4,6},{5,7},{6,4},{7,5},{8,10},{9,11},{10,... | collective-permute-start | bytes 9224 | tf_op jit(solution)/shard_map/ppermute | solution.py:318
  764.0 19.1 %collective-permute-start.79 = (f32[4,192]{1,0:T(4,128)S(1)}, f32[4,192]{1,0:T(4,128)S(1)}, u32[]{:S(2)}, u32[]{:S(2)}) collective-permute-start(f32[4,192]{1,0:T(4,128)S(1)} %slice_add_fusion.1), channel_id=1, source_target_pairs={{0,3},{1,0},{2,1},{3,2},{4,7},{5,4},{6,5},{7,6},{8,11},{9,8},{10,9... | collective-permute-start | bytes 9224 | tf_op jit(solution)/shard_map/ppermute | solution.py:318
  789.0 23.2 %collective-permute-start.73 = (bf16[192,768]{1,0:T(8,128)(2,1)S(1)}, bf16[192,768]{1,0:T(8,128)(2,1)S(1)}, u32[]{:S(2)}, u32[]{:S(2)}) collective-permute-start(bf16[192,768]{1,0:T(8,128)(2,1)S(1)} %get-tuple-element.491), channel_id=1, source_target_pairs={{0,2},{1,3},{2,0},{3,1},{4,6},{5,7},{6,4},{7,5},{8,10},{9,11},{10,... | collective-permute-start | bytes 884744 | tf_op jit(solution)/shard_map/ppermute | solution.py:679
  790.5 21.8 %collective-permute-start.74 = (bf16[192,768]{1,0:T(8,128)(2,1)S(1)}, bf16[192,768]{1,0:T(8,128)(2,1)S(1)}, u32[]{:S(2)}, u32[]{:S(2)}) collective-permute-start(bf16[192,768]{1,0:T(8,128)(2,1)S(1)} %get-tuple-element.492), channel_id=1, source_target_pairs={{0,3},{1,0},{2,1},{3,2},{4,7},{5,4},{6,5},{7,6},{8,11},{9,8},{10,9... | collective-permute-start | bytes 884744 | tf_op jit(solution)/shard_map/ppermute | solution.py:679
  (133 other events, 1017.4 us)
Sparse Core Ops, SparseCore 0:
  10.5 47.6 all-gather.4
  60.7 49.6 all-gather.6
  709.7 27.4 reduce-scatter.2
  739.3 31.7 reduce-scatter.4

commit v4 on v3

--- a/solution.py
+++ b/solution.py
@@ -11,7 +11,7 @@
 HEAD_DIM = 64
 EPS = 1e-05
 NEG = -1e30
-BLOCK = 512
+BLOCK = 1024
 SCALE = HEAD_DIM ** (-0.5)
 F32 = jnp.float32
 BF16 = jnp.bfloat16
@@ -347,7 +347,7 @@
     def stage(compute, *jobs):
         made = {}
         for key, job in jobs:
-            value = job()
+            value = held[key] if job is None else job()
             made.update(value if isinstance(value, dict) else {key: value})
         leaves, shape = jax.tree.flatten((compute(), [*made.values()]))
         if not leaves:
@@ -593,6 +593,7 @@
         for number in range(last + 1):
             if number:
                 returned.append(to_own_rows(grad_packed[number - 1]))
+            sent_back = returned[number - 1:] if number and layer == 0 else []
 
             def work():
                 done = attend_back(packed[number], grad_mixed[number], attended[number][0],
@@ -601,14 +602,15 @@
                 extra = grad_out
                 if number == 0:
                     extra = dot(grad_attn, mixture, ((0,), (0,))).astype(BF16)
-                return done, more, extra
+                return done, more, extra, sent_back
             beside = jobs[5] if number == 1 else []
             if number == 0:
                 beside = [
                     ((DOWN, layer, SUM), lambda: reduce_ctx(
                         held[DOWN, layer, SUM_0], held[DOWN, layer, SUM_1])),
                     ((UP, layer, SUM), reduce_up)] + list(jobs[4])
-            done, more, grad_out = stage(work, *beside)
+            done, more, grad_out, sent_back = stage(work, *beside)
+            returned[len(returned) - len(sent_back):] = sent_back
             grad_packed.append(done)
             grad_mixed += more
         if last == 0:
@@ -636,13 +638,12 @@
     def sum_norms(lower, upper):
         chosen = jnp.where(section == 0, lower, upper)
         if not square():
-            total = lax.psum(chosen, (DP, CTX, TEN))
+            total = lax.psum(chosen, (DP, CTX))
             place = lax.axis_index(DP) * contexts + ctx
             return lax.dynamic_slice_in_dim(total, place * own_rows, own_rows, 1)
         half = width // 2
         total = chosen[:, :half] + swap(chosen[:, half:], DP)
-        total = total[:, :own_rows] + swap(total[:, own_rows:], CTX)
-        return functools.reduce(jnp.add, tensor_pieces(total))
+        return total[:, :own_rows] + swap(total[:, own_rows:], CTX)
 
     def entry_half(value):
         half = take(value.reshape(micro, 2, half_span, width), section, 1)
@@ -652,9 +653,9 @@
         other = swap(mine, SEC)
         return paired(mine[:, None], other[:, None], section, 1).reshape(count, width)
 
-    def exit_rows(value):
-        half = take(value.reshape(tensors, 2, half_span, width), section, 1)
-        return spread_tensor(reorder(half))
+    def exit_rows(*values):
+        halves = [take(value.reshape(tensors, 2, half_span, width), section, 1) for value in values]
+        return spread_tensor(reorder(jnp.concatenate(halves, 1)))
 
     def place_layers(lower, upper):
         keep = jnp.where(section == 0, lower, upper)
@@ -724,8 +725,11 @@
     def late(value):
         return hold(value, held[LAST])
 
-    def near_job(what, layer):
-        return (what, layer, NEAR), lambda: near_rows(late(held[what, layer, OWN]), what == ATTN)
+    def near_job(what, layer, start=late):
+        return (what, layer, NEAR), lambda: near_rows(start(held[what, layer, OWN]), what == ATTN)
+
+    def same(value):
+        return value
 
     def far_job(what, layer, state, start=late):
         return ((what, layer, OWN_FAR if state == OWN else NEAR_FAR),
@@ -741,33 +745,30 @@
             [(FFN, ffn_begin)],
             [near_job(UP, 0), far_job(UP, 0, OWN)],
             [far_job(UP, 0, NEAR), ((ATTN, 1, OWN), lambda: attn_layer(1))],
-            [far_job(DOWN, 0, OWN)],
+            [far_job(DOWN, 0, OWN), ((DOWN, 0, OWN), None), ((ATTN, 1, OWN), None)],
             [],
-            [near_job(DOWN, 0), far_job(ATTN, 1, OWN)],
+            [near_job(DOWN, 0, same), far_job(ATTN, 1, OWN, same)],
             [far_job(DOWN, 0, NEAR), near_job(ATTN, 1)],
             [],
         ])
-    held[EXIT, 0, OWN] = out_zero
     out_one, saved_one, weights_one = forward(
         out_zero, norms_one, lambda: cut(finish(ATTN, 1)()), finish(UP, 1), finish(DOWN, 1), [
-            [far_job(ATTN, 1, NEAR, lambda value: value)],
+            [far_job(ATTN, 1, NEAR, same)],
             [far_job(UP, 1, OWN)],
-            [near_job(UP, 1), far_job(DOWN, 1, OWN),
-             ((EXIT, 0), lambda: exit_rows(late(held.pop((EXIT, 0, OWN)))))],
+            [near_job(UP, 1), far_job(DOWN, 1, OWN), ((ENTRY, 1), lambda: entry_half(cotangent))],
             [far_job(UP, 1, NEAR)],
-            [((ENTRY, 1), lambda: entry_half(hold(cotangent, held[UP, 1, NEAR_FAR])))],
+            [((DOWN, 1, OWN), None)],
             [],
-            [near_job(DOWN, 1)],
+            [near_job(DOWN, 1, same)],
             [far_job(DOWN, 1, NEAR)],
             [],
         ])
     top_grad = entry_rows(held.pop((ENTRY, 1)))
-    held[EXIT, 1, OWN] = out_one
     grad_one, norm_sum_one, grad_heads_one = backward(
         1, top_grad, saved_one, norms_one, weights_one, [
-            [], [], [], [], [((EXIT, 1), lambda: exit_rows(held.pop((EXIT, 1, OWN))))],
+            [], [], [], [],
+            [((EXIT, 0), lambda: exit_rows(out_zero, out_one))],
             [], [], [], []])
-    held[EXIT, 0, OWN] = grad_one
 
     def all_shares(what):
         return (what, ALL), lambda: own_layer(hidden_shares(held.pop((what, 0, SUM))),
@@ -783,8 +784,8 @@
             [((ATTN, 1, SUM), lambda: reduce_ctx(
                 held[ATTN, 1, SUM_0], held[ATTN, 1, SUM_1], True))],
             [],
-            [((EXIT, 2), lambda: exit_rows(held.pop((EXIT, 0, OWN))))],
-            [],
+            [((EXIT, 2), lambda: exit_rows(grad_one))],
+            [((DOWN, 0, SUM), None), ((UP, 0, SUM), None)],
             [all_shares(DOWN), all_shares(UP)],
             [],
             [sum_shares(DOWN)],
@@ -792,15 +793,19 @@
 
     def last_rows():
         sent = held[ATTN, 0, SUM_1]
-        return reduce_ctx(reduce_dp(grad_heads_zero, 0), sent, True), exit_rows(grad_zero)
-
-    attn_zero_sum, back_zero = stage(last_rows, sum_shares(UP))
-    attn_all = own_layer(attn_shares(attn_zero_sum), attn_shares(held[ATTN, 1, SUM]))
+        return (reduce_ctx(reduce_dp(grad_heads_zero, 0), sent, True),
+                sum_norms(norm_sum_zero, norm_sum_one))
+
+    def last_shares():
+        return (own_layer(attn_shares(attn_zero_sum), attn_shares(held[ATTN, 1, SUM])),
+                exit_rows(grad_zero), functools.reduce(jnp.add, tensor_pieces(norm_part)))
+
+    attn_zero_sum, norm_part = stage(last_rows)
+    attn_all, back_zero, norm_sums = stage(last_shares, sum_shares(UP))
     attn_total = reduce_direct(attn_all)
-    layer_outputs = place_layers(held[EXIT, 0], held[EXIT, 1])
+    layer_outputs = place_layers(held[EXIT, 0][:, :half_span], held[EXIT, 0][:, half_span:])
     boundary_grads = place_layers(back_zero, held[EXIT, 2])
     grad_down, grad_up = held[DOWN, DONE].astype(F32).T, held[UP, DONE].astype(F32)
-    norm_sums = sum_norms(hold(norm_sum_zero, attn_all), norm_sum_one)
     grad_qkv, grad_out = attn_total[:, :qkv_cols], attn_total[:, qkv_cols:]
     cut_list, place = [], 0
     for size in (parts if fast else [1] * share_heads):

time: 830 us -> 808 us (0.973)
  waiting for transfers between devices: 304 us -> 284 us
  Pallas kernels: 147 us -> 133 us
  local copies, waits for them, and re-layouts: 86.7 us -> 98.5 us
  starting transfers between devices: 102 us -> 90.7 us
    pallas_call x4, Pallas kernels: 47.2 us -> 34.9 us  [attend(): pl.pallas_call(functools.partial(attend_kernel, block, heads), grid=(leng...]
    all_to_all x6 -> x5, waiting for transfers between devices: 9.84 us -> 0.01 us  [spread_tensor(): return lax.all_to_all(blocks, TEN, 0, 0, tiled=True)]
    ppermute x16, waiting for transfers between devices: 55.6 us -> 47.1 us  [exchanged(): moved.append(lax.ppermute(blocks[step], CTX, pairs))]
    all_to_all x6 -> x5, starting transfers between devices: 26.9 us -> 22.9 us  [spread_tensor(): return lax.all_to_all(blocks, TEN, 0, 0, tiled=True)]
  transfers between devices with their start and end apart: 90 -> 89, of which waited for: 43 -> 44; matrix products, arithmetic and copies ran while one was open for 22% -> 25% of each run, Pallas kernels for 16% -> 16%
where the time goes in v4:
time: 808 us; the launch traced here: 794 us
  waiting for transfers between devices  284 us (35%)
  Pallas kernels  133 us (16%)
  local copies, waits for them, and re-layouts  98.5 us (12%)
  starting transfers between devices  90.7 us (11%)
  matrix products  88.6 us (11%)
  other arithmetic  82.1 us (10%)
  between operations  16.5 us (2%)
    ppermute x58, waiting for transfers between devices, swap(): return lax.ppermute(value, axis, [(0, 1), (1, 0)])  167 us
    dot_general x24, matrix products, dot(): lax.dot_general(left, right, ((contract[0], contract[1]), ((), ())), pref...  88.6 us
    pallas_call x4, Pallas kernels, attend_back(): pl.pallas_call(functools.partial(attend_back_kernel, block, heads), grid=...  64 us
    ppermute x16, waiting for transfers between devices, exchanged(): moved.append(lax.ppermute(blocks[step], CTX, pairs))  47.1 us
    all_gather x2, waiting for transfers between devices, over_tensor(): gathered = lax.all_gather(share, TEN)  41.2 us
    ppermute x58, starting transfers between devices, swap(): return lax.ppermute(value, axis, [(0, 1), (1, 0)])  40.9 us
    pallas_call x4, Pallas kernels, attend(): pl.pallas_call(functools.partial(attend_kernel, block, heads), grid=(leng...  34.9 us
    unnamed x240, local copies, waits for them, and re-layouts  34 us
  transfers between devices with their start and end apart: 89, of which 44 were waited for; matrix products, arithmetic and copies ran while one was open for 25% of the time, Pallas kernels for 16%

profile of v4, /device:TPU:0, one launch (start us, length us, event | category | flops | bytes accessed | tf_op | source)
XLA Modules:
  0.0 793.7 jit_solution(11096885275547941223)
XLA Ops:
  12.3 6.4 all-to-all-start
  26.2 32.0 %all-gather.5.cloned.1.call-done = bf16[768,768]{1,0:T(8,128)(2,1)} async-done(((bf16[192,768]{1,0:T(8,128)(2,1)}), bf16[768,768]{1,0:T(8,128)(2,1)}) %all-gather.5.cloned.1.call-update) | async-done | bytes 1179664 | tf_op jit(solution)/shard_map/all_gather | solution.py:411
  67.4 12.1 %collective-permute-done.5 = bf16[192,1536]{1,0:T(8,128)(2,1)S(1)} collective-permute-done((bf16[192,1536]{1,0:T(8,128)(2,1)}, bf16[192,1536]{1,0:T(8,128)(2,1)S(1)}, u32[]{:S(2)}, u32[]{:S(2)}) %collective-permute-start.5) | collective-permute-done | bytes 589856 | tf_op jit(solution)/shard_map/ppermute | solution.py:262
  81.6 12.6 %collective-permute-done.7 = bf16[192,1536]{1,0:T(8,128)(2,1)S(1)} collective-permute-done((bf16[192,1536]{1,0:T(8,128)(2,1)S(1)}, bf16[192,1536]{1,0:T(8,128)(2,1)S(1)}, u32[]{:S(2)}, u32[]{:S(2)}) %collective-permute-start.7) | collective-permute-done | bytes 589856 | tf_op jit(solution)/shard_map/ppermute | solution.py:262
  101.2 9.2 %all-gather.7.cloned.1.call-done = bf16[768,1536]{1,0:T(8,128)(2,1)} async-done(((bf16[192,1536]{1,0:T(8,128)(2,1)}), bf16[768,1536]{1,0:T(8,128)(2,1)}) %all-gather.7.cloned.1.call-update) | async-done | bytes 2359312 | tf_op jit(solution)/shard_map/all_gather | solution.py:411
  119.9 4.0 broadcast_select_fusion
  131.9 11.4 %attend.4 = (bf16[2048,128]{1,0:T(8,128)(2,1)S(1)}, f32[2,1,2048]{2,1,0:T(1,128)S(1)}) custom-call(bf16[2048,384]{1,0:T(8,128)(2,1)S(1)} %bitcast.338, bf16[2048,384]{1,0:T(8,128)(2,1)S(1)} %bitcast.339), custom_call_target="tpu_custom_call" | custom-call | flops 2147483648 | bytes 3145728 | tf_op jit(solution)/shard_map/attend/pallas_call | solution.py:153
  143.7 9.4 %collective-permute-done.11 = bf16[192,1536]{1,0:T(8,128)(2,1)} collective-permute-done((bf16[192,1536]{1,0:T(8,128)(2,1)S(1)}, bf16[192,1536]{1,0:T(8,128)(2,1)}, u32[]{:S(2)}, u32[]{:S(2)}) %collective-permute-start.11) | collective-permute-done | bytes 589856 | tf_op jit(solution)/shard_map/ppermute | solution.py:262
  163.1 6.1 attend.5
  170.6 5.8 collective-permute-done.15
  176.4 5.0 collective-permute-done.16
  183.5 4.0 fusion.92
  194.3 4.6 norm.5
  198.9 7.3 collective-permute-done.18
  211.5 7.2 fusion.21
  218.7 4.6 collective-permute-done.21
  232.9 10.5 %collective-permute-done.23 = bf16[192,1536]{1,0:T(8,128)(2,1)S(1)} collective-permute-done((bf16[192,1536]{1,0:T(8,128)(2,1)S(1)}, bf16[192,1536]{1,0:T(8,128)(2,1)S(1)}, u32[]{:S(2)}, u32[]{:S(2)}) %collective-permute-start.23) | collective-permute-done | bytes 589856 | tf_op jit(solution)/shard_map/ppermute | solution.py:262
  249.2 4.2 all-to-all-start.1
  255.5 9.8 %collective-permute-done.24 = bf16[1024,384]{1,0:T(8,128)(2,1)} collective-permute-done((bf16[1024,384]{1,0:T(8,128)(2,1)}, bf16[1024,384]{1,0:T(8,128)(2,1)}, u32[]{:S(2)}, u32[]{:S(2)}) %collective-permute-start.24) | collective-permute-done | bytes 786464 | tf_op jit(solution)/shard_map/ppermute | solution.py:481
  270.1 11.2 %attend.6 = (bf16[2048,128]{1,0:T(8,128)(2,1)S(1)}, f32[2,1,2048]{2,1,0:T(1,128)S(1)}) custom-call(bf16[2048,384]{1,0:T(8,128)(2,1)S(1)} %bitcast.342, bf16[2048,384]{1,0:T(8,128)(2,1)S(1)} %bitcast.343), custom_call_target="tpu_custom_call" | custom-call | flops 2147483648 | bytes 3145728 | tf_op jit(solution)/shard_map/attend/pallas_call | solution.py:153
  283.6 8.2 %collective-permute-done.27 = bf16[192,1536]{1,0:T(8,128)(2,1)} collective-permute-done((bf16[192,1536]{1,0:T(8,128)(2,1)}, bf16[192,1536]{1,0:T(8,128)(2,1)}, u32[]{:S(2)}, u32[]{:S(2)}) %collective-permute-start.27) | collective-permute-done | bytes 589856 | tf_op jit(solution)/shard_map/ppermute | solution.py:262
  296.0 6.1 attend.7
  305.3 5.2 collective-permute-done.31
  310.9 4.0 fusion.94
  322.5 4.5 norm.7
  327.1 6.3 collective-permute-done.33
  340.3 8.4 %collective-permute-done.35 = bf16[192,1536]{1,0:T(8,128)(2,1)S(1)} collective-permute-done((bf16[192,1536]{1,0:T(8,128)(2,1)S(1)}, bf16[192,1536]{1,0:T(8,128)(2,1)S(1)}, u32[]{:S(2)}, u32[]{:S(2)}) %collective-permute-start.35) | collective-permute-done | bytes 589856 | tf_op jit(solution)/shard_map/ppermute | solution.py:262
  349.5 6.0 fusion.96
  355.6 4.1 convolution_convert_fusion.5
  359.7 4.3 fusion.100
  364.0 4.2 fusion.6
  368.3 4.4 fusion.95
  373.1 4.0 convolution_convert_fusion.4
  378.3 6.2 norm_back.4
  392.3 9.2 %collective-permute-done.37 = bf16[192,1536]{1,0:T(8,128)(2,1)S(1)} collective-permute-done((bf16[192,1536]{1,0:T(8,128)(2,1)S(1)}, bf16[192,1536]{1,0:T(8,128)(2,1)S(1)}, u32[]{:S(2)}, u32[]{:S(2)}) %collective-permute-start.37) | collective-permute-done | bytes 589856 | tf_op jit(solution)/shard_map/ppermute | solution.py:262
  407.1 4.4 all-to-all-start.2
  428.7 9.2 %collective-permute-done.43 = bf16[192,1536]{1,0:T(8,128)(2,1)S(1)} collective-permute-done((bf16[192,1536]{1,0:T(8,128)(2,1)S(1)}, bf16[192,1536]{1,0:T(8,128)(2,1)S(1)}, u32[]{:S(2)}, u32[]{:S(2)}) %collective-permute-start.43) | collective-permute-done | bytes 589856 | tf_op jit(solution)/shard_map/ppermute | solution.py:262
  441.0 21.8 %attend_back.4 = bf16[2048,384]{1,0:T(8,128)(2,1)S(1)} custom-call(bf16[2048,384]{1,0:T(8,128)(2,1)S(1)} %bitcast.344, bf16[2048,384]{1,0:T(8,128)(2,1)S(1)} %bitcast.345, bf16[2048,128]{1,0:T(8,128)(2,1)S(1)} %bitcast.366, bf16[2048,128]{1,0:T(8,128)(2,1)S(1)} %copy-done.23, f32[2,1,2048]{2,1,0:T(1,128)S(1)} %get-tuple-element.335.log_ref), custom_call_target="tpu_custom_call" | custom-call | flops 5368709120 | bytes 6291456 | tf_op jit(solution)/shard_map/attend_back/pallas_call | solution.py:235
  469.1 10.3 %attend_back.5 = bf16[2048,192]{1,0:T(8,128)(2,1)S(1)} custom-call(bf16[2048,192]{1,0:T(8,128)(2,1)S(1)} %bitcast.356, bf16[2048,192]{1,0:T(8,128)(2,1)S(1)} %bitcast.357, bf16[2048,64]{1,0:T(8,128)(2,1)S(1)} %bitcast.365, bf16[2048,64]{1,0:T(8,128)(2,1)S(1)} %copy-done.21, f32[1,1,2048]{2,1,0:T(1,128)S(1)} %get-tuple-element.347.log_ref), custom_call_target="tpu_custom_call" | custom-call | flops 2684354560 | bytes 3145728 | tf_op jit(solution)/shard_map/attend_back/pallas_call | solution.py:235
  480.4 12.5 %collective-permute-done.48 = bf16[1024,192]{1,0:T(8,128)(2,1)S(1)} collective-permute-done((bf16[1024,192]{1,0:T(8,128)(2,1)S(1)}, bf16[1024,192]{1,0:T(8,128)(2,1)S(1)}, u32[]{:S(2)}, u32[]{:S(2)}) %collective-permute-start.48) | collective-permute-done | bytes 393248 | tf_op jit(solution)/shard_map/ppermute | solution.py:481
  495.0 3.9 fusion.97
  507.6 4.8 norm_back.5
  513.1 5.5 collective-permute-done.50
  523.9 4.2 fusion.13
  528.2 4.0 convolution_convert_fusion.3
  534.2 5.9 fusion.98
  545.5 5.8 convolution_convert_fusion.2
  551.4 7.6 collective-permute-done.54
  560.0 6.2 norm_back.6
  569.0 12.4 %collective-permute-done.53 = bf16[192,1536]{1,0:T(8,128)(2,1)S(1)} collective-permute-done((bf16[192,1536]{1,0:T(8,128)(2,1)S(1)}, bf16[192,1536]{1,0:T(8,128)(2,1)S(1)}, u32[]{:S(2)}, u32[]{:S(2)}) %collective-permute-start.53) | collective-permute-done | bytes 589856 | tf_op jit(solution)/shard_map/ppermute | solution.py:262
  586.0 4.0 all-to-all-start.3
  593.8 3.7 collective-permute-done.56
  607.8 9.5 %collective-permute-done.60 = bf16[192,1536]{1,0:T(8,128)(2,1)S(1)} collective-permute-done((bf16[192,1536]{1,0:T(8,128)(2,1)S(1)}, bf16[192,1536]{1,0:T(8,128)(2,1)S(1)}, u32[]{:S(2)}, u32[]{:S(2)}) %collective-permute-start.60) | collective-permute-done | bytes 589856 | tf_op jit(solution)/shard_map/ppermute | solution.py:262
  620.2 21.6 %attend_back.6 = bf16[2048,384]{1,0:T(8,128)(2,1)S(1)} custom-call(bf16[2048,384]{1,0:T(8,128)(2,1)S(1)} %bitcast.340, bf16[2048,384]{1,0:T(8,128)(2,1)S(1)} %bitcast.341, bf16[2048,128]{1,0:T(8,128)(2,1)S(1)} %bitcast.367, bf16[2048,128]{1,0:T(8,128)(2,1)S(1)} %copy-done.19, f32[2,1,2048]{2,1,0:T(1,128)S(1)} %get-tuple-element.384.log_ref), custom_call_target="tpu_custom_call" | custom-call | flops 5368709120 | bytes 6291456 | tf_op jit(solution)/shard_map/attend_back/pallas_call | solution.py:235
  650.1 10.3 %attend_back.7 = bf16[2048,192]{1,0:T(8,128)(2,1)S(1)} custom-call(bf16[2048,192]{1,0:T(8,128)(2,1)S(1)} %bitcast.352, bf16[2048,192]{1,0:T(8,128)(2,1)S(1)} %bitcast.353, bf16[2048,64]{1,0:T(8,128)(2,1)S(1)} %bitcast.364, bf16[2048,64]{1,0:T(8,128)(2,1)S(1)} %copy-done.17, f32[1,1,2048]{2,1,0:T(1,128)S(1)} %get-tuple-element.392.log_ref), custom_call_target="tpu_custom_call" | custom-call | flops 2684354560 | bytes 3145728 | tf_op jit(solution)/shard_map/attend_back/pallas_call | solution.py:235
  667.7 11.3 %collective-permute-done.63 = bf16[1024,192]{1,0:T(8,128)(2,1)} collective-permute-done((bf16[1024,192]{1,0:T(8,128)(2,1)}, bf16[1024,192]{1,0:T(8,128)(2,1)}, u32[]{:S(2)}, u32[]{:S(2)}) %collective-permute-start.63) | collective-permute-done | bytes 393248 | tf_op jit(solution)/shard_map/ppermute | solution.py:481
  684.5 5.8 fusion.99
  704.6 4.8 norm_back.7
  709.4 5.5 collective-permute-done.68
  721.8 5.4 collective-permute-done.70
  730.2 3.9 all-to-all-start.4
  745.5 8.5 %collective-permute-done.73 = f32[4,192]{1,0:T(4,128)S(1)} collective-permute-done((f32[4,192]{1,0:T(4,128)S(1)}, f32[4,192]{1,0:T(4,128)S(1)}, u32[]{:S(2)}, u32[]{:S(2)}) %collective-permute-start.73) | collective-permute-done | bytes 3104 | tf_op jit(solution)/shard_map/ppermute | solution.py:318
  764.4 5.5 collective-permute-done.77
  770.0 11.6 %collective-permute-done.78 = bf16[192,768]{1,0:T(8,128)(2,1)S(1)} collective-permute-done((bf16[192,768]{1,0:T(8,128)(2,1)S(1)}, bf16[192,768]{1,0:T(8,128)(2,1)S(1)}, u32[]{:S(2)}, u32[]{:S(2)}) %collective-permute-start.78) | collective-permute-done | bytes 294944 | tf_op jit(solution)/shard_map/ppermute | solution.py:680
  (631 shorter events, 284.1 us)
Async XLA Ops:
  7.2 51.0 %all-gather.5.cloned.1.call-start = ((), (), s32[]{:S(2)}) async-start(), calls=%async_computation.9 | async-start | bytes 1474560 | tf_op jit(solution)/shard_map/all_gather | solution.py:411
  12.3 47.2 %all-to-all-start = ((bf16[4,128,768]{2,1,0:T(8,128)(2,1)}), bf16[4,128,768]{2,1,0:T(8,128)(2,1)S(1)}, u32[]{:S(2)}, u32[]{:S(2)}) async-start(bf16[4,128,768]{2,1,0:T(8,128)(2,1)} %maximum_select_fusion.2), calls=%async_computation | async-start | bytes 1572864 | tf_op jit(solution)/shard_map/all_to_all | solution.py:290
  18.8 91.6 %all-gather.7.cloned.1.call-start = ((), (), s32[]{:S(2)}) async-start(), calls=%async_computation.10 | async-start | bytes 2949120 | tf_op jit(solution)/shard_map/all_gather | solution.py:411
  26.2 33.3 %collective-permute-start.2 = (bf16[4,768]{1,0:T(4,128)(2,1)S(1)}, bf16[4,768]{1,0:T(4,128)(2,1)S(1)}, u32[]{:S(2)}, u32[]{:S(2)}) collective-permute-start(bf16[4,768]{1,0:T(4,128)(2,1)S(1)} %pad_maximum_fusion.40), channel_id=1, source_target_pairs={{0,16},{16,0},{1,17},{17,1},{2,18},{18,2},{3,19},{19,3},{4,20},{20... | collective-permute-start | bytes 18440 | tf_op jit(solution)/shard_map/ppermute | solution.py:262
  64.0 15.6 %collective-permute-start.5 = (bf16[192,1536]{1,0:T(8,128)(2,1)}, bf16[192,1536]{1,0:T(8,128)(2,1)S(1)}, u32[]{:S(2)}, u32[]{:S(2)}) collective-permute-start(bf16[192,1536]{1,0:T(8,128)(2,1)} %concatenate.369), channel_id=1, source_target_pairs={{0,4},{4,0},{1,5},{5,1},{2,6},{6,2},{3,7},{7,3},{8,12},{12,8},{9,1... | collective-permute-start | bytes 1769480 | tf_op jit(solution)/shard_map/ppermute | solution.py:262
  65.4 15.6 %collective-permute-start.3 = (bf16[4,128,768]{2,1,0:T(8,128)(2,1)S(1)}, bf16[4,128,768]{2,1,0:T(8,128)(2,1)S(1)}, u32[]{:S(2)}, u32[]{:S(2)}) collective-permute-start(bf16[4,128,768]{2,1,0:T(8,128)(2,1)S(1)} %all-to-all-done), channel_id=1, source_target_pairs={{0,16},{16,0},{1,17},{17,1},{2,18},{18,2},{3,19},{19,3},{4,20},{20... | collective-permute-start | bytes 2359304 | tf_op jit(solution)/shard_map/ppermute | solution.py:262
  65.8 15.8 %collective-permute-start.6 = (bf16[192,1536]{1,0:T(8,128)(2,1)S(1)}, bf16[192,1536]{1,0:T(8,128)(2,1)S(1)}, u32[]{:S(2)}, u32[]{:S(2)}) collective-permute-start(bf16[192,1536]{1,0:T(8,128)(2,1)S(1)} %concatenate.368), channel_id=1, source_target_pairs={{0,8},{8,0},{1,9},{9,1},{2,10},{10,2},{3,11},{11,3},{4,12},{12,4},... | collective-permute-start | bytes 1769480 | tf_op jit(solution)/shard_map/ppermute | solution.py:262
  79.5 14.7 %collective-permute-start.7 = (bf16[192,1536]{1,0:T(8,128)(2,1)S(1)}, bf16[192,1536]{1,0:T(8,128)(2,1)S(1)}, u32[]{:S(2)}, u32[]{:S(2)}) collective-permute-start(bf16[192,1536]{1,0:T(8,128)(2,1)S(1)} %collective-permute-done.5), channel_id=1, source_target_pairs={{0,8},{8,0},{1,9},{9,1},{2,10},{10,2},{3,11},{11,3},{4,12},{12,4},... | collective-permute-start | bytes 1769480 | tf_op jit(solution)/shard_map/ppermute | solution.py:262
  99.8 18.4 %collective-permute-start.8 = (bf16[1024,384]{1,0:T(8,128)(2,1)}, bf16[1024,384]{1,0:T(8,128)(2,1)}, u32[]{:S(2)}, u32[]{:S(2)}) collective-permute-start(bf16[1024,384]{1,0:T(8,128)(2,1)} %slice.806), channel_id=1, source_target_pairs={{0,4},{4,0},{1,5},{5,1},{2,6},{6,2},{3,7},{7,3},{8,12},{12,8},{9,1... | collective-permute-start | bytes 2359304 | tf_op jit(solution)/shard_map/ppermute | solution.py:481
  128.4 15.0 %collective-permute-start.10 = (bf16[1024,192]{1,0:T(8,128)(2,1)S(1)}, bf16[1024,192]{1,0:T(8,128)(2,1)S(1)}, u32[]{:S(2)}, u32[]{:S(2)}) collective-permute-start(bf16[1024,192]{1,0:T(8,128)(2,1)S(1)} %get-tuple-element.234), channel_id=1, source_target_pairs={{0,4},{4,0},{1,5},{5,1},{2,6},{6,2},{3,7},{7,3},{8,12},{12,8},{9,1... | collective-permute-start | bytes 1179656 | tf_op jit(solution)/shard_map/ppermute | solution.py:481
  129.7 23.5 %collective-permute-start.11 = (bf16[192,1536]{1,0:T(8,128)(2,1)S(1)}, bf16[192,1536]{1,0:T(8,128)(2,1)}, u32[]{:S(2)}, u32[]{:S(2)}) collective-permute-start(bf16[192,1536]{1,0:T(8,128)(2,1)S(1)} %bitcast.379), channel_id=1, source_target_pairs={{0,4},{4,0},{1,5},{5,1},{2,6},{6,2},{3,7},{7,3},{8,12},{12,8},{9,1... | collective-permute-start | bytes 1769480 | tf_op jit(solution)/shard_map/ppermute | solution.py:262
  130.4 22.7 %collective-permute-start.12 = (bf16[192,1536]{1,0:T(8,128)(2,1)S(1)}, bf16[192,1536]{1,0:T(8,128)(2,1)S(1)}, u32[]{:S(2)}, u32[]{:S(2)}) collective-permute-start(bf16[192,1536]{1,0:T(8,128)(2,1)S(1)} %bitcast.380), channel_id=1, source_target_pairs={{0,8},{8,0},{1,9},{9,1},{2,10},{10,2},{3,11},{11,3},{4,12},{12,4},... | collective-permute-start | bytes 1769480 | tf_op jit(solution)/shard_map/ppermute | solution.py:262
  154.0 15.3 %collective-permute-start.14 = (bf16[192,1536]{1,0:T(8,128)(2,1)}, bf16[192,1536]{1,0:T(8,128)(2,1)}, u32[]{:S(2)}, u32[]{:S(2)}) collective-permute-start(bf16[192,1536]{1,0:T(8,128)(2,1)} %collective-permute-done.11), channel_id=1, source_target_pairs={{0,8},{8,0},{1,9},{9,1},{2,10},{10,2},{3,11},{11,3},{4,12},{12,4},... | collective-permute-start | bytes 1769480 | tf_op jit(solution)/shard_map/ppermute | solution.py:262
  190.4 15.7 %collective-permute-start.18 = (bf16[192,1536]{1,0:T(8,128)(2,1)S(1)}, bf16[192,1536]{1,0:T(8,128)(2,1)S(1)}, u32[]{:S(2)}, u32[]{:S(2)}) collective-permute-start(bf16[192,1536]{1,0:T(8,128)(2,1)S(1)} %bitcast.377), channel_id=1, source_target_pairs={{0,4},{4,0},{1,5},{5,1},{2,6},{6,2},{3,7},{7,3},{8,12},{12,8},{9,1... | collective-permute-start | bytes 1769480 | tf_op jit(solution)/shard_map/ppermute | solution.py:262
  190.9 15.4 %collective-permute-start.19 = (bf16[192,1536]{1,0:T(8,128)(2,1)S(1)}, bf16[192,1536]{1,0:T(8,128)(2,1)S(1)}, u32[]{:S(2)}, u32[]{:S(2)}) collective-permute-start(bf16[192,1536]{1,0:T(8,128)(2,1)S(1)} %copy-done.38), channel_id=1, source_target_pairs={{0,8},{8,0},{1,9},{9,1},{2,10},{10,2},{3,11},{11,3},{4,12},{12,4},... | collective-permute-start | bytes 1769480 | tf_op jit(solution)/shard_map/ppermute | solution.py:262
  208.3 15.0 %collective-permute-start.21 = (bf16[192,1536]{1,0:T(8,128)(2,1)S(1)}, bf16[192,1536]{1,0:T(8,128)(2,1)S(1)}, u32[]{:S(2)}, u32[]{:S(2)}) collective-permute-start(bf16[192,1536]{1,0:T(8,128)(2,1)S(1)} %concatenate.379), channel_id=1, source_target_pairs={{0,4},{4,0},{1,5},{5,1},{2,6},{6,2},{3,7},{7,3},{8,12},{12,8},{9,1... | collective-permute-start | bytes 1769480 | tf_op jit(solution)/shard_map/ppermute | solution.py:262
  210.0 14.6 %collective-permute-start.20 = (bf16[192,1536]{1,0:T(8,128)(2,1)}, bf16[192,1536]{1,0:T(8,128)(2,1)S(1)}, u32[]{:S(2)}, u32[]{:S(2)}) collective-permute-start(bf16[192,1536]{1,0:T(8,128)(2,1)} %copy-done.85), channel_id=1, source_target_pairs={{0,8},{8,0},{1,9},{9,1},{2,10},{10,2},{3,11},{11,3},{4,12},{12,4},... | collective-permute-start | bytes 1769480 | tf_op jit(solution)/shard_map/ppermute | solution.py:262
  228.4 15.0 %collective-permute-start.23 = (bf16[192,1536]{1,0:T(8,128)(2,1)S(1)}, bf16[192,1536]{1,0:T(8,128)(2,1)S(1)}, u32[]{:S(2)}, u32[]{:S(2)}) collective-permute-start(bf16[192,1536]{1,0:T(8,128)(2,1)S(1)} %collective-permute-done.21), channel_id=1, source_target_pairs={{0,8},{8,0},{1,9},{9,1},{2,10},{10,2},{3,11},{11,3},{4,12},{12,4},... | collective-permute-start | bytes 1769480 | tf_op jit(solution)/shard_map/ppermute | solution.py:262
  246.8 18.6 %collective-permute-start.24 = (bf16[1024,384]{1,0:T(8,128)(2,1)}, bf16[1024,384]{1,0:T(8,128)(2,1)}, u32[]{:S(2)}, u32[]{:S(2)}) collective-permute-start(bf16[1024,384]{1,0:T(8,128)(2,1)} %slice.825), channel_id=1, source_target_pairs={{0,4},{4,0},{1,5},{5,1},{2,6},{6,2},{3,7},{7,3},{8,12},{12,8},{9,1... | collective-permute-start | bytes 2359304 | tf_op jit(solution)/shard_map/ppermute | solution.py:481
  249.2 34.4 %all-to-all-start.1 = ((bf16[4,128,768]{2,1,0:T(8,128)(2,1)}), bf16[4,128,768]{2,1,0:T(8,128)(2,1)}, u32[]{:S(2)}, u32[]{:S(2)}) async-start(bf16[4,128,768]{2,1,0:T(8,128)(2,1)} %maximum_select_fusion.4), calls=%async_computation.1 | async-start | bytes 1572864 | tf_op jit(solution)/shard_map/all_to_all | solution.py:290
  253.4 14.1 %collective-permute-start.25 = (bf16[192,1536]{1,0:T(8,128)(2,1)}, bf16[192,1536]{1,0:T(8,128)(2,1)S(1)}, u32[]{:S(2)}, u32[]{:S(2)}) collective-permute-start(bf16[192,1536]{1,0:T(8,128)(2,1)} %bitcast.165), channel_id=1, source_target_pairs={{0,8},{8,0},{1,9},{9,1},{2,10},{10,2},{3,11},{11,3},{4,12},{12,4},... | collective-permute-start | bytes 1769480 | tf_op jit(solution)/shard_map/ppermute | solution.py:262
  267.5 14.9 %collective-permute-start.26 = (bf16[1024,192]{1,0:T(8,128)(2,1)S(1)}, bf16[1024,192]{1,0:T(8,128)(2,1)S(1)}, u32[]{:S(2)}, u32[]{:S(2)}) collective-permute-start(bf16[1024,192]{1,0:T(8,128)(2,1)S(1)} %get-tuple-element.285), channel_id=1, source_target_pairs={{0,4},{4,0},{1,5},{5,1},{2,6},{6,2},{3,7},{7,3},{8,12},{12,8},{9,1... | collective-permute-start | bytes 1179656 | tf_op jit(solution)/shard_map/ppermute | solution.py:481
  268.8 14.8 %collective-permute-start.28 = (bf16[192,1536]{1,0:T(8,128)(2,1)}, bf16[192,1536]{1,0:T(8,128)(2,1)}, u32[]{:S(2)}, u32[]{:S(2)}) collective-permute-start(bf16[192,1536]{1,0:T(8,128)(2,1)} %bitcast.167), channel_id=1, source_target_pairs={{0,8},{8,0},{1,9},{9,1},{2,10},{10,2},{3,11},{11,3},{4,12},{12,4},... | collective-permute-start | bytes 1769480 | tf_op jit(solution)/shard_map/ppermute | solution.py:262
  269.4 22.4 %collective-permute-start.27 = (bf16[192,1536]{1,0:T(8,128)(2,1)}, bf16[192,1536]{1,0:T(8,128)(2,1)}, u32[]{:S(2)}, u32[]{:S(2)}) collective-permute-start(bf16[192,1536]{1,0:T(8,128)(2,1)} %bitcast.165), channel_id=1, source_target_pairs={{0,4},{4,0},{1,5},{5,1},{2,6},{6,2},{3,7},{7,3},{8,12},{12,8},{9,1... | collective-permute-start | bytes 1769480 | tf_op jit(solution)/shard_map/ppermute | solution.py:262
  317.8 15.6 %collective-permute-start.33 = (bf16[192,1536]{1,0:T(8,128)(2,1)}, bf16[192,1536]{1,0:T(8,128)(2,1)S(1)}, u32[]{:S(2)}, u32[]{:S(2)}) collective-permute-start(bf16[192,1536]{1,0:T(8,128)(2,1)} %bitcast.167), channel_id=1, source_target_pairs={{0,4},{4,0},{1,5},{5,1},{2,6},{6,2},{3,7},{7,3},{8,12},{12,8},{9,1... | collective-permute-start | bytes 1769480 | tf_op jit(solution)/shard_map/ppermute | solution.py:262
  334.2 14.5 %collective-permute-start.35 = (bf16[192,1536]{1,0:T(8,128)(2,1)S(1)}, bf16[192,1536]{1,0:T(8,128)(2,1)S(1)}, u32[]{:S(2)}, u32[]{:S(2)}) collective-permute-start(bf16[192,1536]{1,0:T(8,128)(2,1)S(1)} %collective-permute-done.33), channel_id=1, source_target_pairs={{0,8},{8,0},{1,9},{9,1},{2,10},{10,2},{3,11},{11,3},{4,12},{12,4},... | collective-permute-start | bytes 1769480 | tf_op jit(solution)/shard_map/ppermute | solution.py:262
  386.2 15.4 %collective-permute-start.37 = (bf16[192,1536]{1,0:T(8,128)(2,1)S(1)}, bf16[192,1536]{1,0:T(8,128)(2,1)S(1)}, u32[]{:S(2)}, u32[]{:S(2)}) collective-permute-start(bf16[192,1536]{1,0:T(8,128)(2,1)S(1)} %slice.687), channel_id=1, source_target_pairs={{0,8},{8,0},{1,9},{9,1},{2,10},{10,2},{3,11},{11,3},{4,12},{12,4},... | collective-permute-start | bytes 1769480 | tf_op jit(solution)/shard_map/ppermute | solution.py:262
  403.3 14.8 %collective-permute-start.39 = (bf16[192,1536]{1,0:T(8,128)(2,1)}, bf16[192,1536]{1,0:T(8,128)(2,1)}, u32[]{:S(2)}, u32[]{:S(2)}) collective-permute-start(bf16[192,1536]{1,0:T(8,128)(2,1)} %slice.689), channel_id=1, source_target_pairs={{0,8},{8,0},{1,9},{9,1},{2,10},{10,2},{3,11},{11,3},{4,12},{12,4},... | collective-permute-start | bytes 1769480 | tf_op jit(solution)/shard_map/ppermute | solution.py:262
  407.1 60.5 %all-to-all-start.2 = ((bf16[4,256,768]{2,1,0:T(8,128)(2,1)}), bf16[4,256,768]{2,1,0:T(8,128)(2,1)}, u32[]{:S(2)}, u32[]{:S(2)}) async-start(bf16[4,256,768]{2,1,0:T(8,128)(2,1)} %maximum_select_fusion), calls=%async_computation.2 | async-start | bytes 3145728 | tf_op jit(solution)/shard_map/all_to_all | solution.py:290
  411.4 15.2 %collective-permute-start.41 = (bf16[192,1536]{1,0:T(8,128)(2,1)}, bf16[192,1536]{1,0:T(8,128)(2,1)}, u32[]{:S(2)}, u32[]{:S(2)}) collective-permute-start(bf16[192,1536]{1,0:T(8,128)(2,1)} %add_convert_fusion.19), channel_id=1, source_target_pairs={{0,4},{4,0},{1,5},{5,1},{2,6},{6,2},{3,7},{7,3},{8,12},{12,8},{9,1... | collective-permute-start | bytes 1769480 | tf_op jit(solution)/shard_map/ppermute | solution.py:262
  421.6 16.3 %collective-permute-start.43 = (bf16[192,1536]{1,0:T(8,128)(2,1)S(1)}, bf16[192,1536]{1,0:T(8,128)(2,1)S(1)}, u32[]{:S(2)}, u32[]{:S(2)}) collective-permute-start(bf16[192,1536]{1,0:T(8,128)(2,1)S(1)} %get-tuple-element.477), channel_id=1, source_target_pairs={{0,8},{8,0},{1,9},{9,1},{2,10},{10,2},{3,11},{11,3},{4,12},{12,4},... | collective-permute-start | bytes 1769480 | tf_op jit(solution)/shard_map/ppermute | solution.py:262
  424.1 41.0 %collective-permute-start.42 = (bf16[192,1536]{1,0:T(8,128)(2,1)}, bf16[192,1536]{1,0:T(8,128)(2,1)}, u32[]{:S(2)}, u32[]{:S(2)}) collective-permute-start(bf16[192,1536]{1,0:T(8,128)(2,1)} %get-tuple-element.476), channel_id=1, source_target_pairs={{0,8},{8,0},{1,9},{9,1},{2,10},{10,2},{3,11},{11,3},{4,12},{12,4},... | collective-permute-start | bytes 1769480 | tf_op jit(solution)/shard_map/ppermute | solution.py:262
  425.5 38.5 %collective-permute-start.40 = (bf16[1024,64]{0,1:T(8,128)(2,1)S(1)}, bf16[1024,64]{0,1:T(8,128)(2,1)S(1)}, u32[]{:S(2)}, u32[]{:S(2)}) collective-permute-start(bf16[1024,64]{0,1:T(8,128)(2,1)S(1)} %copy-done.97), channel_id=1, source_target_pairs={{0,4},{4,0},{1,5},{5,1},{2,6},{6,2},{3,7},{7,3},{8,12},{12,8},{9,1... | collective-permute-start | bytes 393224 | tf_op jit(solution)/shard_map/ppermute | solution.py:481
  439.9 25.2 %collective-permute-start.44 = (bf16[192,1536]{1,0:T(8,128)(2,1)}, bf16[192,1536]{1,0:T(8,128)(2,1)}, u32[]{:S(2)}, u32[]{:S(2)}) collective-permute-start(bf16[192,1536]{1,0:T(8,128)(2,1)} %add_convert_fusion.15), channel_id=1, source_target_pairs={{0,4},{4,0},{1,5},{5,1},{2,6},{6,2},{3,7},{7,3},{8,12},{12,8},{9,1... | collective-permute-start | bytes 1769480 | tf_op jit(solution)/shard_map/ppermute | solution.py:262
  467.8 25.1 %collective-permute-start.47 = (bf16[1024,384]{1,0:T(8,128)(2,1)S(1)}, bf16[1024,384]{1,0:T(8,128)(2,1)S(1)}, u32[]{:S(2)}, u32[]{:S(2)}) collective-permute-start(bf16[1024,384]{1,0:T(8,128)(2,1)S(1)} %get-tuple-element.490), channel_id=1, source_target_pairs={{0,4},{4,0},{1,5},{5,1},{2,6},{6,2},{3,7},{7,3},{8,12},{12,8},{9,1... | collective-permute-start | bytes 2359304 | tf_op jit(solution)/shard_map/ppermute | solution.py:481
  479.5 13.4 %collective-permute-start.48 = (bf16[1024,192]{1,0:T(8,128)(2,1)S(1)}, bf16[1024,192]{1,0:T(8,128)(2,1)S(1)}, u32[]{:S(2)}, u32[]{:S(2)}) collective-permute-start(bf16[1024,192]{1,0:T(8,128)(2,1)S(1)} %get-tuple-element.523), channel_id=1, source_target_pairs={{0,4},{4,0},{1,5},{5,1},{2,6},{6,2},{3,7},{7,3},{8,12},{12,8},{9,1... | collective-permute-start | bytes 1179656 | tf_op jit(solution)/shard_map/ppermute | solution.py:481
  502.4 16.2 %collective-permute-start.50 = (bf16[192,1536]{1,0:T(8,128)(2,1)S(1)}, bf16[192,1536]{1,0:T(8,128)(2,1)S(1)}, u32[]{:S(2)}, u32[]{:S(2)}) collective-permute-start(bf16[192,1536]{1,0:T(8,128)(2,1)S(1)} %slice.707), channel_id=1, source_target_pairs={{0,8},{8,0},{1,9},{9,1},{2,10},{10,2},{3,11},{11,3},{4,12},{12,4},... | collective-permute-start | bytes 1769480 | tf_op jit(solution)/shard_map/ppermute | solution.py:262
  505.4 141.8 %collective-permute-start.46 = (bf16[4,128,768]{2,1,0:T(8,128)(2,1)}, bf16[4,128,768]{2,1,0:T(8,128)(2,1)}, u32[]{:S(2)}, u32[]{:S(2)}) collective-permute-start(bf16[4,128,768]{2,1,0:T(8,128)(2,1)} %broadcast_select_fusion.4), channel_id=1, source_target_pairs={{0,16},{16,0},{1,17},{17,1},{2,18},{18,2},{3,19},{19,3},{4,20},{20... | collective-permute-start | bytes 2359304 | tf_op jit(solution)/shard_map/ppermute | solution.py:262
  506.3 25.9 %collective-permute-start.51 = (bf16[192,1536]{1,0:T(8,128)(2,1)}, bf16[192,1536]{1,0:T(8,128)(2,1)}, u32[]{:S(2)}, u32[]{:S(2)}) collective-permute-start(bf16[192,1536]{1,0:T(8,128)(2,1)} %slice.709), channel_id=1, source_target_pairs={{0,8},{8,0},{1,9},{9,1},{2,10},{10,2},{3,11},{11,3},{4,12},{12,4},... | collective-permute-start | bytes 1769480 | tf_op jit(solution)/shard_map/ppermute | solution.py:262
  540.1 19.8 %collective-permute-start.52 = (bf16[1024,768]{1,0:T(8,128)(2,1)}, bf16[1024,768]{1,0:T(8,128)(2,1)S(1)}, u32[]{:S(2)}, u32[]{:S(2)}) collective-permute-start(bf16[1024,768]{1,0:T(8,128)(2,1)} %get-tuple-element.675), channel_id=1, source_target_pairs={{0,16},{16,0},{1,17},{17,1},{2,18},{18,2},{3,19},{19,3},{4,20},{20... | collective-permute-start | bytes 4718600 | tf_op jit(solution)/shard_map/ppermute | solution.py:262
  543.0 16.0 %collective-permute-start.54 = (bf16[192,1536]{1,0:T(8,128)(2,1)}, bf16[192,1536]{1,0:T(8,128)(2,1)S(1)}, u32[]{:S(2)}, u32[]{:S(2)}) collective-permute-start(bf16[192,1536]{1,0:T(8,128)(2,1)} %concatenate.402), channel_id=1, source_target_pairs={{0,4},{4,0},{1,5},{5,1},{2,6},{6,2},{3,7},{7,3},{8,12},{12,8},{9,1... | collective-permute-start | bytes 1769480 | tf_op jit(solution)/shard_map/ppermute | solution.py:262
  566.3 15.0 %collective-permute-start.53 = (bf16[192,1536]{1,0:T(8,128)(2,1)S(1)}, bf16[192,1536]{1,0:T(8,128)(2,1)S(1)}, u32[]{:S(2)}, u32[]{:S(2)}) collective-permute-start(bf16[192,1536]{1,0:T(8,128)(2,1)S(1)} %slice.715), channel_id=1, source_target_pairs={{0,8},{8,0},{1,9},{9,1},{2,10},{10,2},{3,11},{11,3},{4,12},{12,4},... | collective-permute-start | bytes 1769480 | tf_op jit(solution)/shard_map/ppermute | solution.py:262
  583.1 14.4 %collective-permute-start.56 = (bf16[192,1536]{1,0:T(8,128)(2,1)}, bf16[192,1536]{1,0:T(8,128)(2,1)}, u32[]{:S(2)}, u32[]{:S(2)}) collective-permute-start(bf16[192,1536]{1,0:T(8,128)(2,1)} %slice.725), channel_id=1, source_target_pairs={{0,8},{8,0},{1,9},{9,1},{2,10},{10,2},{3,11},{11,3},{4,12},{12,4},... | collective-permute-start | bytes 1769480 | tf_op jit(solution)/shard_map/ppermute | solution.py:262
  586.0 58.7 %all-to-all-start.3 = ((bf16[4,128,768]{2,1,0:T(8,128)(2,1)}), bf16[4,128,768]{2,1,0:T(8,128)(2,1)S(1)}, u32[]{:S(2)}, u32[]{:S(2)}) async-start(bf16[4,128,768]{2,1,0:T(8,128)(2,1)} %maximum_select_fusion.6), calls=%async_computation.3 | async-start | bytes 1572864 | tf_op jit(solution)/shard_map/all_to_all | solution.py:290
  590.0 126.3 %reduce-scatter.3.cloned.1.call-start = ((), (), s32[]{:S(2)}) async-start(), calls=%async_computation.7 | async-start | bytes 1474560 | tf_op jit(solution)/shard_map/reduce_scatter | solution.py:672
  590.0 15.8 %collective-permute-start.58 = (bf16[192,1536]{1,0:T(8,128)(2,1)}, bf16[192,1536]{1,0:T(8,128)(2,1)}, u32[]{:S(2)}, u32[]{:S(2)}) collective-permute-start(bf16[192,1536]{1,0:T(8,128)(2,1)} %add_convert_fusion.11), channel_id=1, source_target_pairs={{0,4},{4,0},{1,5},{5,1},{2,6},{6,2},{3,7},{7,3},{8,12},{12,8},{9,1... | collective-permute-start | bytes 1769480 | tf_op jit(solution)/shard_map/ppermute | solution.py:262
  601.0 16.3 %collective-permute-start.60 = (bf16[192,1536]{1,0:T(8,128)(2,1)S(1)}, bf16[192,1536]{1,0:T(8,128)(2,1)S(1)}, u32[]{:S(2)}, u32[]{:S(2)}) collective-permute-start(bf16[192,1536]{1,0:T(8,128)(2,1)S(1)} %get-tuple-element.473), channel_id=1, source_target_pairs={{0,8},{8,0},{1,9},{9,1},{2,10},{10,2},{3,11},{11,3},{4,12},{12,4},... | collective-permute-start | bytes 1769480 | tf_op jit(solution)/shard_map/ppermute | solution.py:262
  603.5 38.7 %collective-permute-start.59 = (bf16[192,1536]{1,0:T(8,128)(2,1)}, bf16[192,1536]{1,0:T(8,128)(2,1)}, u32[]{:S(2)}, u32[]{:S(2)}) collective-permute-start(bf16[192,1536]{1,0:T(8,128)(2,1)} %get-tuple-element.472), channel_id=1, source_target_pairs={{0,8},{8,0},{1,9},{9,1},{2,10},{10,2},{3,11},{11,3},{4,12},{12,4},... | collective-permute-start | bytes 1769480 | tf_op jit(solution)/shard_map/ppermute | solution.py:262
  604.9 36.9 %collective-permute-start.57 = (bf16[1024,64]{0,1:T(8,128)(2,1)S(1)}, bf16[1024,64]{0,1:T(8,128)(2,1)S(1)}, u32[]{:S(2)}, u32[]{:S(2)}) collective-permute-start(bf16[1024,64]{0,1:T(8,128)(2,1)S(1)} %get-tuple-element.386), channel_id=1, source_target_pairs={{0,4},{4,0},{1,5},{5,1},{2,6},{6,2},{3,7},{7,3},{8,12},{12,8},{9,1... | collective-permute-start | bytes 393224 | tf_op jit(solution)/shard_map/ppermute | solution.py:481
  619.3 22.9 %collective-permute-start.61 = (bf16[192,1536]{1,0:T(8,128)(2,1)}, bf16[192,1536]{1,0:T(8,128)(2,1)}, u32[]{:S(2)}, u32[]{:S(2)}) collective-permute-start(bf16[192,1536]{1,0:T(8,128)(2,1)} %add_convert_fusion.6), channel_id=1, source_target_pairs={{0,4},{4,0},{1,5},{5,1},{2,6},{6,2},{3,7},{7,3},{8,12},{12,8},{9,1... | collective-permute-start | bytes 1769480 | tf_op jit(solution)/shard_map/ppermute | solution.py:262
  646.0 14.4 %collective-permute-start.62 = (bf16[1024,384]{1,0:T(8,128)(2,1)}, bf16[1024,384]{1,0:T(8,128)(2,1)}, u32[]{:S(2)}, u32[]{:S(2)}) collective-permute-start(bf16[1024,384]{1,0:T(8,128)(2,1)} %get-tuple-element.488), channel_id=1, source_target_pairs={{0,4},{4,0},{1,5},{5,1},{2,6},{6,2},{3,7},{7,3},{8,12},{12,8},{9,1... | collective-permute-start | bytes 2359304 | tf_op jit(solution)/shard_map/ppermute | solution.py:481
  664.4 14.7 %collective-permute-start.63 = (bf16[1024,192]{1,0:T(8,128)(2,1)}, bf16[1024,192]{1,0:T(8,128)(2,1)}, u32[]{:S(2)}, u32[]{:S(2)}) collective-permute-start(bf16[1024,192]{1,0:T(8,128)(2,1)} %get-tuple-element.521), channel_id=1, source_target_pairs={{0,4},{4,0},{1,5},{5,1},{2,6},{6,2},{3,7},{7,3},{8,12},{12,8},{9,1... | collective-permute-start | bytes 1179656 | tf_op jit(solution)/shard_map/ppermute | solution.py:481
  683.2 74.8 %reduce-scatter.5.cloned.1.call-start = ((), (), s32[]{:S(2)}) async-start(), calls=%async_computation.8 | async-start | bytes 1474560 | tf_op jit(solution)/shard_map/reduce_scatter | solution.py:672
  698.5 16.4 %collective-permute-start.68 = (bf16[192,1536]{1,0:T(8,128)(2,1)}, bf16[192,1536]{1,0:T(8,128)(2,1)}, u32[]{:S(2)}, u32[]{:S(2)}) collective-permute-start(bf16[192,1536]{1,0:T(8,128)(2,1)} %slice.743), channel_id=1, source_target_pairs={{0,8},{8,0},{1,9},{9,1},{2,10},{10,2},{3,11},{11,3},{4,12},{12,4},... | collective-permute-start | bytes 1769480 | tf_op jit(solution)/shard_map/ppermute | solution.py:262
  701.7 33.2 %collective-permute-start.67 = (bf16[192,1536]{1,0:T(8,128)(2,1)}, bf16[192,1536]{1,0:T(8,128)(2,1)}, u32[]{:S(2)}, u32[]{:S(2)}) collective-permute-start(bf16[192,1536]{1,0:T(8,128)(2,1)} %slice.737), channel_id=1, source_target_pairs={{0,8},{8,0},{1,9},{9,1},{2,10},{10,2},{3,11},{11,3},{4,12},{12,4},... | collective-permute-start | bytes 1769480 | tf_op jit(solution)/shard_map/ppermute | solution.py:262
  720.3 14.7 %collective-permute-start.69 = (bf16[192,1536]{1,0:T(8,128)(2,1)S(1)}, bf16[192,1536]{1,0:T(8,128)(2,1)}, u32[]{:S(2)}, u32[]{:S(2)}) collective-permute-start(bf16[192,1536]{1,0:T(8,128)(2,1)S(1)} %concatenate.413), channel_id=1, source_target_pairs={{0,4},{4,0},{1,5},{5,1},{2,6},{6,2},{3,7},{7,3},{8,12},{12,8},{9,1... | collective-permute-start | bytes 1769480 | tf_op jit(solution)/shard_map/ppermute | solution.py:262
  730.2 27.8 %all-to-all-start.4 = ((bf16[4,128,768]{2,1,0:T(8,128)(2,1)}), bf16[4,128,768]{2,1,0:T(8,128)(2,1)S(1)}, u32[]{:S(2)}, u32[]{:S(2)}) async-start(bf16[4,128,768]{2,1,0:T(8,128)(2,1)} %maximum_select_fusion.8), calls=%async_computation.5 | async-start | bytes 1572864 | tf_op jit(solution)/shard_map/all_to_all | solution.py:290
  737.4 20.1 %collective-permute-start.72 = (bf16[2,192,768]{2,1,0:T(8,128)(2,1)S(1)}, bf16[2,192,768]{2,1,0:T(8,128)(2,1)S(1)}, u32[]{:S(2)}, u32[]{:S(2)}) collective-permute-start(bf16[2,192,768]{2,1,0:T(8,128)(2,1)S(1)} %broadcast_select_fusion.13), channel_id=1, source_target_pairs={{0,16},{16,0},{1,17},{17,1},{2,18},{18,2},{3,19},{19,3},{4,20},{20... | collective-permute-start | bytes 1769480 | tf_op jit(solution)/shard_map/ppermute | solution.py:262
  739.4 14.6 %collective-permute-start.73 = (f32[4,192]{1,0:T(4,128)S(1)}, f32[4,192]{1,0:T(4,128)S(1)}, u32[]{:S(2)}, u32[]{:S(2)}) collective-permute-start(f32[4,192]{1,0:T(4,128)S(1)} %slice_add_fusion.1), channel_id=1, source_target_pairs={{0,1},{1,2},{2,3},{3,0},{4,5},{5,6},{6,7},{7,4},{8,9},{9,10},{10,1... | collective-permute-start | bytes 9224 | tf_op jit(solution)/shard_map/ppermute | solution.py:318
  740.9 16.6 %collective-permute-start.74 = (f32[4,192]{1,0:T(4,128)S(1)}, f32[4,192]{1,0:T(4,128)S(1)}, u32[]{:S(2)}, u32[]{:S(2)}) collective-permute-start(f32[4,192]{1,0:T(4,128)S(1)} %slice_add_fusion.1), channel_id=1, source_target_pairs={{0,2},{1,3},{2,0},{3,1},{4,6},{5,7},{6,4},{7,5},{8,10},{9,11},{10,... | collective-permute-start | bytes 9224 | tf_op jit(solution)/shard_map/ppermute | solution.py:318
  743.1 14.3 %collective-permute-start.75 = (f32[4,192]{1,0:T(4,128)S(1)}, f32[4,192]{1,0:T(4,128)S(1)}, u32[]{:S(2)}, u32[]{:S(2)}) collective-permute-start(f32[4,192]{1,0:T(4,128)S(1)} %slice_add_fusion.1), channel_id=1, source_target_pairs={{0,3},{1,0},{2,1},{3,2},{4,7},{5,4},{6,5},{7,6},{8,11},{9,8},{10,9... | collective-permute-start | bytes 9224 | tf_op jit(solution)/shard_map/ppermute | solution.py:318
  758.8 22.8 %collective-permute-start.78 = (bf16[192,768]{1,0:T(8,128)(2,1)S(1)}, bf16[192,768]{1,0:T(8,128)(2,1)S(1)}, u32[]{:S(2)}, u32[]{:S(2)}) collective-permute-start(bf16[192,768]{1,0:T(8,128)(2,1)S(1)} %get-tuple-element.504), channel_id=1, source_target_pairs={{0,2},{1,3},{2,0},{3,1},{4,6},{5,7},{6,4},{7,5},{8,10},{9,11},{10,... | collective-permute-start | bytes 884744 | tf_op jit(solution)/shard_map/ppermute | solution.py:680
  760.2 21.4 %collective-permute-start.79 = (bf16[192,768]{1,0:T(8,128)(2,1)S(1)}, bf16[192,768]{1,0:T(8,128)(2,1)S(1)}, u32[]{:S(2)}, u32[]{:S(2)}) collective-permute-start(bf16[192,768]{1,0:T(8,128)(2,1)S(1)} %get-tuple-element.503), channel_id=1, source_target_pairs={{0,3},{1,0},{2,1},{3,2},{4,7},{5,4},{6,5},{7,6},{8,11},{9,8},{10,9... | collective-permute-start | bytes 884744 | tf_op jit(solution)/shard_map/ppermute | solution.py:680
  763.0 21.1 %collective-permute-start.76 = (bf16[4,128,768]{2,1,0:T(8,128)(2,1)}, bf16[4,128,768]{2,1,0:T(8,128)(2,1)}, u32[]{:S(2)}, u32[]{:S(2)}) collective-permute-start(bf16[4,128,768]{2,1,0:T(8,128)(2,1)} %broadcast_select_fusion.2), channel_id=1, source_target_pairs={{0,16},{16,0},{1,17},{17,1},{2,18},{18,2},{3,19},{19,3},{4,20},{20... | collective-permute-start | bytes 2359304 | tf_op jit(solution)/shard_map/ppermute | solution.py:262
  (132 other events, 1003.4 us)
Sparse Core Ops, SparseCore 0:
  10.5 47.6 all-gather.4
  60.7 49.6 all-gather.6
  683.3 28.1 reduce-scatter.2
  713.7 29.7 reduce-scatter.4
